TPU v7x, 256 devices: a whole 4x4x8 slice. The times are simulated.
256 devices in a mesh: tr: 32 (over y_hi, z, core), pt: 8 (over x, y_lo).
Axes of the slice: x: 4, y: 4 (y_hi: 2, y_lo: 2; y = y_hi * 2 + y_lo), z: 8, core: 2. Of those that a mesh axis runs over, the one named last changes fastest.
Arguments:
- gathers: bfloat16 [8192, 64, 1024], P(('tr', 'pt')), may hold values from -6 to 6
- level_one: bfloat16 [2048, 256, 256], P(('tr', 'pt')), may hold values from -0.375 to 0.375
- level_two: bfloat16 [8192, 64, 256], P(('tr', 'pt')), may hold values from -0.375 to 0.375
- middle: bfloat16 [8192, 64, 64], P(('tr', 'pt')), may hold values from -0.75 to 0.75
- level_three: bfloat16 [8192, 64, 256], P(('tr', 'pt')), may hold values from -0.375 to 0.375
Outputs:
- imaged: bfloat16 [8192, 64, 1024], P(('tr', 'pt'))
All inputs are finite; a program needn't handle non-finite values.
Results may differ from a plain program's by a relative error of at most 0.0064.
Values may be sent and summed in bfloat16 or wider, within the bound.
No kernel may reach another device: no remote copies, remote signals or barrier semaphores. Data moves between devices by JAX's collectives and lax.ppermute only.
A program may use at most 128 MiB of HBM per device.

v0:
```python
import jax
import jax.numpy as jnp
from jax import lax
from jax.sharding import PartitionSpec as P


def swapped_2(array, axis, stride):
    return lax.ppermute(array, axis, [(i, i ^ 1 << stride) for i in range(lax.axis_size(axis))])


def local_order(weights, upper_half, rank):
    swapped = jnp.concatenate([weights[..., 2 * rank :], weights[..., : 2 * rank]], axis=-1)
    return jnp.where(upper_half == 1, swapped, weights)


def apply_rows(weights, pieces, rank):
    total = None
    for column in range(4):
        block = weights[..., column * rank : (column + 1) * rank]
        term = jnp.einsum(
            "bjrk,jkg->bjrg", block, pieces[column], preferred_element_type=jnp.float32
        )
        total = term if total is None else total + term
    return total.astype(jnp.bfloat16)


def mix_inputs(values, weights, upper_half, fetch):
    blocks, rank, columns = values.shape
    half_blocks = blocks // 2
    other = fetch(values)
    pieces = (values[:half_blocks], values[half_blocks:], other[:half_blocks], other[half_blocks:])
    ordered = local_order(weights, upper_half, rank).reshape(2, half_blocks, rank, 4 * rank)
    return apply_rows(ordered, pieces, rank).reshape(blocks, rank, columns)


def shards(gathers, level_one, level_two, middle, level_three):
    blocks, rank, columns = gathers.shape
    top = lax.axis_size("pt").bit_length() - 2
    position = lax.axis_index("pt")
    upper_top = position >> top & 1
    upper_low = position & 1
    grouped = gathers.reshape(blocks // 4, 4 * rank, columns)
    first = jnp.einsum("qik,qkg->qig", level_one, grouped, preferred_element_type=jnp.float32)
    first = first.astype(jnp.bfloat16).reshape(blocks, rank, columns)
    second = mix_inputs(first, level_two, upper_top, lambda values: swapped_2(values, "pt", top))
    centred = jnp.einsum(
        "brk,bkg->brg",
        middle,
        lax.all_to_all(second, "tr", split_axis=0, concat_axis=0, tiled=True),
        preferred_element_type=jnp.float32,
    ).astype(jnp.bfloat16)
    imaged = mix_inputs(centred, level_three, upper_low, lambda values: swapped_2(values, "pt", 0))
    return imaged


def solution(mesh):
    in_specs = (
        P(("tr", "pt"), None, None),
        P(("tr", "pt"), None, None),
        P(("tr", "pt"), None, None),
        P(("tr", "pt"), None, None),
        P(("tr", "pt"), None, None),
    )
    out_specs = P(("tr", "pt"), None, None)
    return jax.shard_map(shards, mesh=mesh, in_specs=in_specs, out_specs=out_specs, check_vma=False)
```

profile of v0, /device:TPU:1, one launch (start us, length us, event | category | flops | bytes accessed | tf_op | source)
XLA Modules:
  0.0 336.9 jit_solution(1389000193123045285)
XLA Ops:
  0.0 0.0 copy-start
  0.0 1.2 copy-done
  1.2 0.0 copy-start.2
  1.2 5.6 %convolution_convert_fusion = bf16[8,256,1024]{2,1,0:T(8,128)(2,1)} fusion(bf16[8,256,256]{2,1,0:T(8,128)(2,1)S(1)} %copy-done, bf16[8,256,1024]{2,1,0:T(8,128)(2,1)} %bitcast.67), kind=kOutput, calls=%fused_computation.5 | convolution fusion | flops 1075838976 | bytes 9437184 | tf_op jit(solution)/shard_map/qik,qkg->qig/dot_general | solution.py:43
  6.8 3.6 %collective-permute-start = (bf16[32,64,1024]{2,1,0:T(8,128)(2,1)}, bf16[32,64,1024]{2,1,0:T(8,128)(2,1)}, u32[]{:S(2)}, u32[]{:S(2)}) collective-permute-start(bf16[32,64,1024]{2,1,0:T(8,128)(2,1)} %bitcast.8), channel_id=1, source_target_pairs={{0,4},{1,5},{2,6},{3,7},{4,0},{5,1},{6,2},{7,3},{8,12},{9,13},{10,... | collective-permute-start | bytes 12582920 | tf_op jit(solution)/shard_map/ppermute | solution.py:8
  10.4 0.0 copy-done.2
  10.4 0.3 fusion.22
  10.7 0.4 maximum_select_fusion
  11.1 0.6 fusion.21
  11.7 2.7 fusion.18
  14.4 4.5 %fusion.14 = f32[16,1024,2,64]{1,3,2,0:T(8,128)} fusion(bf16[16,64,1024,1]{2,1,3,0:T(8,128)(2,1)S(1)} %bitcast.66, bf16[2,16,64,64]{3,2,1,0:T(8,128)(2,1)S(1)} %get-tuple-element.15), kind=kOutput, calls=%fused_computation.26 | convolution fusion | flops 268435456 | bytes 10747904 | tf_op jit(solution)/shard_map/bjrk,jkg->bjrg/dot_general | solution.py:20
  18.9 4.5 %fusion.16 = f32[16,1024,2,64]{1,3,2,0:T(8,128)} fusion(bf16[16,64,1024,1]{2,1,3,0:T(8,128)(2,1)S(1)} %bitcast.65, bf16[2,16,64,64]{3,2,1,0:T(8,128)(2,1)S(1)} %get-tuple-element.16), kind=kOutput, calls=%fused_computation.28 | convolution fusion | flops 268435456 | bytes 10747904 | tf_op jit(solution)/shard_map/bjrk,jkg->bjrg/dot_general | solution.py:20
  23.3 76.6 %collective-permute-done = bf16[32,64,1024]{2,1,0:T(8,128)(2,1)} collective-permute-done((bf16[32,64,1024]{2,1,0:T(8,128)(2,1)}, bf16[32,64,1024]{2,1,0:T(8,128)(2,1)}, u32[]{:S(2)}, u32[]{:S(2)}) %collective-permute-start) | collective-permute-done | bytes 4194336 | tf_op jit(solution)/shard_map/ppermute | solution.py:8
  99.9 6.0 %fusion.7 = f32[16,1024,2,64]{1,3,2,0:T(8,128)} fusion(bf16[32,64,1024]{2,1,0:T(8,128)(2,1)} %collective-permute-done, bf16[2,16,64,64]{3,2,1,0:T(8,128)(2,1)S(1)} %get-tuple-element.14), kind=kOutput, calls=%fused_computation.17 | convolution fusion | flops 268435456 | bytes 10747904 | tf_op jit(solution)/shard_map/bjrk,jkg->bjrg/dot_general | solution.py:20
  106.0 9.8 %fusion = bf16[2,16,64,1024]{3,2,0,1:T(8,128)(2,1)S(1)} fusion(f32[16,1024,2,64]{1,3,2,0:T(8,128)} %fusion.7, f32[16,1024,2,64]{1,3,2,0:T(8,128)} %fusion.16, f32[16,1024,2,64]{1,3,2,0:T(8,128)} %fusion.14, bf16[32,64,1024]{2,1,0:T(8,128)(2,1)} %collective-permute-done, bf16[2,16,64,64]{3,2,1,0:T(8,128)(2,1)S(1)} %get-tuple-element.13), kind=kOutput, calls=%fused_computation.2 | convolution fusion | flops 276824064 | bytes 31719424 | tf_op jit(solution)/shard_map/bjrk,jkg->bjrg/dot_general | solution.py:20
  115.8 0.6 copy.10
  116.4 0.0 copy-start.4
  116.4 108.8 %all_to_all.5 = bf16[32,64,1024]{2,1,0:T(8,128)(2,1)S(1)} all-to-all(bf16[32,64,1024]{2,1,0:T(8,128)(2,1)S(1)} %bitcast.62), channel_id=1, replica_groups=mesh['tr'=32,'pt'=8] {'tr'}, dimensions={0} | all-to-all | bytes 8388608 | tf_op jit(solution)/shard_map/all_to_all | solution.py:49
  225.2 0.0 copy-done.4
  225.2 3.2 convert_bitcast_fusion
  228.5 0.4 collective-permute-start.1
  228.9 0.0 copy-done.3
  228.9 0.3 fusion.20
  229.2 0.4 maximum_select_fusion.1
  229.6 0.6 fusion.19
  230.2 6.0 %fusion.4 = f32[16,1024,2,64]{1,3,2,0:T(8,128)} fusion(bf16[32,64,1024]{2,1,0:T(8,128)(2,1)} %convert_bitcast_fusion, bf16[2,16,64,64]{3,2,1,0:T(8,128)(2,1)S(1)} %get-tuple-element.9), kind=kOutput, calls=%fused_computation.11 | convolution fusion | flops 268435456 | bytes 10747904 | tf_op jit(solution)/shard_map/bjrk,jkg->bjrg/dot_general | solution.py:20
  236.3 6.1 %fusion.5 = f32[16,1024,2,64]{1,3,2,0:T(8,128)} fusion(bf16[32,64,1024]{2,1,0:T(8,128)(2,1)} %convert_bitcast_fusion, bf16[2,16,64,64]{3,2,1,0:T(8,128)(2,1)S(1)} %get-tuple-element.10), kind=kOutput, calls=%fused_computation.13 | convolution fusion | flops 268435456 | bytes 10747904 | tf_op jit(solution)/shard_map/bjrk,jkg->bjrg/dot_general | solution.py:20
  242.3 76.2 %collective-permute-done.1 = bf16[32,64,1024]{2,1,0:T(8,128)(2,1)} collective-permute-done((bf16[32,64,1024]{2,1,0:T(8,128)(2,1)}, bf16[32,64,1024]{2,1,0:T(8,128)(2,1)}, u32[]{:S(2)}, u32[]{:S(2)}) %collective-permute-start.1) | collective-permute-done | bytes 4194336 | tf_op jit(solution)/shard_map/ppermute | solution.py:8
  318.5 6.0 %fusion.3 = f32[16,1024,2,64]{1,3,2,0:T(8,128)} fusion(bf16[32,64,1024]{2,1,0:T(8,128)(2,1)} %collective-permute-done.1, bf16[2,16,64,64]{3,2,1,0:T(8,128)(2,1)S(1)} %get-tuple-element.8), kind=kOutput, calls=%fused_computation.9 | convolution fusion | flops 268435456 | bytes 10747904 | tf_op jit(solution)/shard_map/bjrk,jkg->bjrg/dot_general | solution.py:20
  324.5 9.9 %fusion.1 = bf16[2,16,64,1024]{3,2,0,1:T(8,128)(2,1)S(1)} fusion(f32[16,1024,2,64]{1,3,2,0:T(8,128)} %fusion.3, f32[16,1024,2,64]{1,3,2,0:T(8,128)} %fusion.5, f32[16,1024,2,64]{1,3,2,0:T(8,128)} %fusion.4, bf16[32,64,1024]{2,1,0:T(8,128)(2,1)} %collective-permute-done.1, bf16[2,16,64,64]{3,2,1,0:T(8,128)(2,1)S(1)} %get-tuple-element.7), kind=kOutput, calls=%fused_computation.3 | convolution fusion | flops 276824064 | bytes 31719424 | tf_op jit(solution)/shard_map/bjrk,jkg->bjrg/dot_general | solution.py:20
  334.4 2.5 copy.15
  336.9 0.0 copy-done.1
  (2 shorter events, 0.0 us)
Async XLA Ops:
  0.0 1.2 copy-start
  1.2 9.1 %copy-start.2 = (bf16[32,64,256]{2,1,0:T(8,128)(2,1)S(1)}, bf16[32,64,256]{2,1,0:T(8,128)(2,1)}, u32[]{:S(2)}) copy-start(bf16[32,64,256]{2,1,0:T(8,128)(2,1)} %param.7) | copy-start | bytes 3145732
  6.8 93.1 %collective-permute-start = (bf16[32,64,1024]{2,1,0:T(8,128)(2,1)}, bf16[32,64,1024]{2,1,0:T(8,128)(2,1)}, u32[]{:S(2)}, u32[]{:S(2)}) collective-permute-start(bf16[32,64,1024]{2,1,0:T(8,128)(2,1)} %bitcast.8), channel_id=1, source_target_pairs={{0,4},{1,5},{2,6},{3,7},{4,0},{5,1},{6,2},{7,3},{8,12},{9,13},{10,... | collective-permute-start | bytes 12582920 | tf_op jit(solution)/shard_map/ppermute | solution.py:8
  116.4 108.9 %copy-start.4 = (bf16[32,64,64]{2,1,0:T(8,128)(2,1)S(1)}, bf16[32,64,64]{2,1,0:T(8,128)(2,1)}, u32[]{:S(2)}) copy-start(bf16[32,64,64]{2,1,0:T(8,128)(2,1)} %param.8) | copy-start | bytes 786436
  225.2 3.6 %copy-start.3 = (bf16[32,64,256]{2,1,0:T(8,128)(2,1)S(1)}, bf16[32,64,256]{2,1,0:T(8,128)(2,1)}, u32[]{:S(2)}) copy-start(bf16[32,64,256]{2,1,0:T(8,128)(2,1)} %param.9) | copy-start | bytes 3145732
  228.5 90.0 %collective-permute-start.1 = (bf16[32,64,1024]{2,1,0:T(8,128)(2,1)}, bf16[32,64,1024]{2,1,0:T(8,128)(2,1)}, u32[]{:S(2)}, u32[]{:S(2)}) collective-permute-start(bf16[32,64,1024]{2,1,0:T(8,128)(2,1)} %convert_bitcast_fusion), channel_id=1, source_target_pairs={{0,1},{1,0},{2,3},{3,2},{4,5},{5,4},{6,7},{7,6},{8,9},{9,8},{10,11... | collective-permute-start | bytes 12582920 | tf_op jit(solution)/shard_map/ppermute | solution.py:8
  324.5 12.4 %copy-start.1 = (bf16[8,256,256]{2,1,0:T(8,128)(2,1)S(1)}, bf16[8,256,256]{2,1,0:T(8,128)(2,1)}, u32[]{:S(2)}) copy-start(bf16[8,256,256]{2,1,0:T(8,128)(2,1)} %param.6) | copy-start | bytes 3145732
where the time goes:
time: 340 us; the launch traced here: 337 us
  waiting for transfers between devices  153 us (45%)
  blocking collectives  109 us (32%)
  matrix products  61.6 us (18%)
  local copies, waits for them, and re-layouts  8.71 us (3%)
  starting transfers between devices  3.97 us (1%)
    ppermute x2, waiting for transfers between devices, swapped_2(): lax.ppermute(array, axis, [(i, i ^ 1 << stride) for i in range(lax.axis_s...  153 us
    all_to_all x1, blocking collectives, shards(): lax.all_to_all(second, 'tr', split_axis=0, concat_axis=0, tiled=True)  109 us
    dot_general x8, matrix products, apply_rows(): jnp.einsum('bjrk,jkg->bjrg', block, pieces[column], preferred_element_typ...  52.8 us
  transfers between devices with their start and end apart: 2, of which 2 were waited for; matrix products, arithmetic and copies ran while one was open for 8% of the time, Pallas kernels for 0%

commit v1 on v0

v1 whole, which is shorter than its diff:
```python
import functools

import jax
import jax.numpy as jnp
from jax import lax
from jax.experimental import pallas as pl
from jax.experimental.pallas import tpu as pltpu
from jax.sharding import PartitionSpec as P

AXES = ("tr", "pt")
CHUNKS = ((0, 128), (256, 256), (512, 256), (768, 256), (128, 128))
STEPS = 4
VMEM = 32 * 1024 * 1024


def exchanged(array, flip_tr, flip_pt):
    n_tr, n_pt = lax.axis_size("tr"), lax.axis_size("pt")
    pairs = [
        (t * n_pt + s, (t ^ flip_tr) * n_pt + (s ^ flip_pt))
        for t in range(n_tr)
        for s in range(n_pt)
    ]
    return lax.ppermute(array, AXES, pairs)


def spread(array):
    n = lax.axis_size("tr") // 2
    groups = [[h * n + i for i in range(n)] for h in range(2)]
    return lax.all_to_all(
        array, "tr", split_axis=0, concat_axis=0, tiled=True, axis_index_groups=groups
    )


def params():
    return pltpu.CompilerParams(vmem_limit_bytes=VMEM)


def cost(flops, moved):
    return pl.CostEstimate(flops=flops, bytes_accessed=moved, transcendentals=0)


def level_one_kernel(weights, values, out):
    for q in range(weights.shape[0]):
        rows = values[4 * q : 4 * q + 4].reshape(weights.shape[2], values.shape[2])
        product = jnp.dot(weights[q], rows, preferred_element_type=jnp.float32)
        out[4 * q : 4 * q + 4] = product.astype(out.dtype).reshape(4, *out.shape[1:])


def level_one_chunk(weights, values, start, size):
    blocks, rank, _ = values.shape
    groups = weights.shape[0]
    column = start // size
    return pl.pallas_call(
        level_one_kernel,
        grid=(STEPS,),
        in_specs=[
            pl.BlockSpec((groups // STEPS, 4 * rank, 4 * rank), lambda i: (i, 0, 0)),
            pl.BlockSpec((blocks // STEPS, rank, size), lambda i: (i, 0, column)),
        ],
        out_specs=pl.BlockSpec((blocks // STEPS, rank, size), lambda i: (i, 0, 0)),
        out_shape=jax.ShapeDtypeStruct((blocks, rank, size), jnp.bfloat16),
        compiler_params=params(),
        cost_estimate=cost(2 * blocks * rank * 4 * rank * size, 4 * blocks * rank * size),
    )(weights, values)


def order_kernel(flags, weights, out):
    groups = out.shape[0]
    rank = weights.shape[1]
    upper_s, upper_t = flags[0], flags[1]
    for j in range(groups):
        for row in range(2):
            half = upper_t if row == 0 else 1 - upper_t
            block = weights[j + groups * half]
            low, high = block[:, : 2 * rank], block[:, 2 * rank :]
            rows = slice(row * rank, (row + 1) * rank)
            out[j, rows, : 2 * rank] = jnp.where(upper_s == 1, high, low)
            out[j, rows, 2 * rank :] = jnp.where(upper_s == 1, low, high)


def ordered_two(flags, weights):
    blocks, rank, depth = weights.shape
    return pl.pallas_call(
        order_kernel,
        in_specs=[
            pl.BlockSpec(memory_space=pltpu.SMEM),
            pl.BlockSpec(memory_space=pltpu.VMEM),
        ],
        out_specs=pl.BlockSpec(memory_space=pltpu.VMEM),
        out_shape=jax.ShapeDtypeStruct((blocks // 2, 2 * rank, depth), jnp.bfloat16),
        compiler_params=params(),
        cost_estimate=cost(0, 4 * blocks * rank * depth),
    )(flags, weights)


def level_two_kernel(weights, own, other, kept, sent):
    rank, size = own.shape[2:]
    for j in range(own.shape[1]):
        rows = jnp.concatenate([own[0, j], own[1, j], other[0, j], other[1, j]], axis=0)
        product = jnp.dot(weights[j], rows, preferred_element_type=jnp.float32)
        product = product.astype(kept.dtype)
        kept[j] = product[:rank]
        sent[j] = product[rank:]


def level_two_chunk(weights, own, other):
    blocks, rank, size = own.shape
    half = blocks // 2
    part = half // STEPS
    pair = pl.BlockSpec((2, part, rank, size), lambda i: (0, i, 0, 0))
    out = jax.ShapeDtypeStruct((half, rank, size), jnp.bfloat16)
    out_spec = pl.BlockSpec((part, rank, size), lambda i: (i, 0, 0))
    return pl.pallas_call(
        level_two_kernel,
        grid=(STEPS,),
        in_specs=[
            pl.BlockSpec((part, 2 * rank, 4 * rank), lambda i: (i, 0, 0)),
            pair,
            pair,
        ],
        out_specs=[out_spec, out_spec],
        out_shape=[out, out],
        compiler_params=params(),
        cost_estimate=cost(2 * blocks * rank * 4 * rank * size, 6 * blocks * rank * size),
    )(weights, own.reshape(2, half, rank, size), other.reshape(2, half, rank, size))


def compose_kernel(flags, weights, middle, partner, out):
    groups, rank = out.shape[0], weights.shape[1]

    def for_place(low_s, upper_t):
        for j in range(groups):
            rows = jnp.concatenate([weights[j], weights[j + groups]], axis=0)
            for slot in range(4):
                e, f = low_s ^ (slot & 1), upper_t ^ (slot >> 1)
                centre = (partner if slot & 1 else middle)[j + groups * f]
                at = (2 * e + f) * rank
                product = jnp.dot(
                    rows[:, at : at + rank], centre, preferred_element_type=jnp.float32
                )
                out[j, :, slot * rank : (slot + 1) * rank] = product.astype(out.dtype)

    for low_s in range(2):
        for upper_t in range(2):
            here = (flags[2] == low_s) & (flags[1] == upper_t)
            pl.when(here)(functools.partial(for_place, low_s, upper_t))


def composed_three(flags, weights, middle, partner):
    blocks, rank, depth = weights.shape
    return pl.pallas_call(
        compose_kernel,
        in_specs=[pl.BlockSpec(memory_space=pltpu.SMEM)]
        + [pl.BlockSpec(memory_space=pltpu.VMEM)] * 3,
        out_specs=pl.BlockSpec(memory_space=pltpu.VMEM),
        out_shape=jax.ShapeDtypeStruct((blocks // 2, 2 * rank, depth), jnp.bfloat16),
        compiler_params=params(),
        cost_estimate=cost(2 * blocks * rank * depth * rank, 6 * blocks * rank * depth),
    )(flags, weights, middle, partner)


def level_three_kernel(weights, *refs):
    pieces, out = refs[:4], refs[-1]
    rank = out.shape[2]
    for j in range(out.shape[1]):
        rows = jnp.concatenate([piece[j] for piece in pieces], axis=0)
        product = jnp.dot(weights[j], rows, preferred_element_type=jnp.float32)
        product = product.astype(out.dtype)
        out[0, j] = product[:rank]
        out[1, j] = product[rank:]


def level_three_chunk(weights, pieces, result, shape, start):
    half, rank, size = pieces[0].shape
    part = half // STEPS
    column = start // size
    in_specs = [pl.BlockSpec((part, 2 * rank, 4 * rank), lambda i: (i, 0, 0))]
    in_specs += [pl.BlockSpec((part, rank, size), lambda i: (i, 0, 0))] * 4
    operands, aliases = [weights, *pieces], {}
    if result is not None:
        in_specs.append(pl.BlockSpec(memory_space=pl.ANY))
        operands.append(result)
        aliases = {5: 0}
    return pl.pallas_call(
        level_three_kernel,
        grid=(STEPS,),
        in_specs=in_specs,
        out_specs=pl.BlockSpec((2, part, rank, size), lambda i: (0, i, 0, column)),
        out_shape=jax.ShapeDtypeStruct((2, half, rank, shape[2]), jnp.bfloat16),
        input_output_aliases=aliases,
        compiler_params=params(),
        cost_estimate=cost(4 * half * rank * 4 * rank * size, 12 * half * rank * size),
    )(*operands)


def shards(gathers, level_one, level_two, middle, level_three):
    n_tr, n_pt = lax.axis_size("tr"), lax.axis_size("pt")
    t, s = lax.axis_index("tr"), lax.axis_index("pt")
    flags = jnp.stack([s // (n_pt // 2), t // (n_tr // 2), s % 2]).astype(jnp.int32)
    partner = exchanged(middle, 0, 1)
    weights_two = ordered_two(flags, level_two)
    weights_three = composed_three(flags, level_three, middle, partner)
    result = None
    for start, size in CHUNKS:
        own = level_one_chunk(level_one, gathers, start, size)
        other = exchanged(own, 0, n_pt // 2)
        kept, sent = level_two_chunk(weights_two, own, other)
        kept, sent = spread(kept), spread(sent)
        pieces = (
            kept,
            exchanged(kept, 0, 1),
            exchanged(sent, n_tr // 2, 0),
            exchanged(sent, n_tr // 2, 1),
        )
        result = level_three_chunk(weights_three, pieces, result, gathers.shape, start)
    return result.reshape(gathers.shape)


def solution(mesh):
    spec = P(("tr", "pt"), None, None)
    return jax.shard_map(
        shards, mesh=mesh, in_specs=(spec,) * 5, out_specs=spec, check_vma=False
    )
```

time: 340 us -> 322 us (0.947)
  blocking collectives: 109 us -> 20.2 us
  starting transfers between devices: 3.97 us -> 83.1 us
  matrix products: 61.6 us -> 0 us
  Pallas kernels: 0 us -> 34.7 us
  local copies, waits for them, and re-layouts: 8.71 us -> 27.9 us
    all_to_all x1, blocking collectives: 109 us -> 20.2 us  [spread(): lax.all_to_all(array, 'tr', split_axis=0, concat_axis=0, tiled=True, axis...]
    dot_general x10 -> x0, matrix products: 61.6 us -> none  [the longest x8 52.8 us: apply_rows(): jnp.einsum('bjrk,jkg->bjrg', block, pieces[column], preferred_element_typ...]
    all_to_all x0 -> x9, starting transfers between devices: none -> 50 us  [spread(): lax.all_to_all(array, 'tr', split_axis=0, concat_axis=0, tiled=True, axis...]
    all_to_all x0 -> x9, waiting for transfers between devices: none -> 42 us  [spread(): lax.all_to_all(array, 'tr', split_axis=0, concat_axis=0, tiled=True, axis...]
    ppermute x2 -> x21, waiting for transfers between devices: 153 us -> 112 us  [exchanged(): return lax.ppermute(array, AXES, pairs)]
    pallas_call x0 -> x17, Pallas kernels: none -> 34.7 us  [the longest x5 15.6 us: level_three_chunk(): pl.pallas_call(level_three_kernel, grid=(STEPS,), in_specs=in_specs, out_...]
    ppermute x2 -> x21, starting transfers between devices: 3.97 us -> 33 us  [exchanged(): return lax.ppermute(array, AXES, pairs)]
    unnamed x10 -> x62, local copies, waits for them, and re-layouts: 1.24 us -> 27.9 us
  transfers between devices with their start and end apart: 2 -> 30, of which waited for: 2 -> 19; matrix products, arithmetic and copies ran while one was open for 8% -> 0% of each run, Pallas kernels for 0% -> 10%
where the time goes in v1:
time: 322 us; the launch traced here: 320 us
  waiting for transfers between devices  154 us (48%)
  starting transfers between devices  83.1 us (26%)
  Pallas kernels  34.7 us (11%)
  local copies, waits for them, and re-layouts  27.9 us (9%)
  blocking collectives  20.2 us (6%)
    ppermute x21, waiting for transfers between devices, exchanged(): return lax.ppermute(array, AXES, pairs)  112 us
    all_to_all x9, starting transfers between devices, spread(): lax.all_to_all(array, 'tr', split_axis=0, concat_axis=0, tiled=True, axis...  50 us
    all_to_all x9, waiting for transfers between devices, spread(): lax.all_to_all(array, 'tr', split_axis=0, concat_axis=0, tiled=True, axis...  42 us
    ppermute x21, starting transfers between devices, exchanged(): return lax.ppermute(array, AXES, pairs)  33 us
    unnamed x62, local copies, waits for them, and re-layouts  27.9 us
    all_to_all x1, blocking collectives, spread(): lax.all_to_all(array, 'tr', split_axis=0, concat_axis=0, tiled=True, axis...  20.2 us
    pallas_call x5, Pallas kernels, level_three_chunk(): pl.pallas_call(level_three_kernel, grid=(STEPS,), in_specs=in_specs, out_...  15.6 us
    pallas_call x5, Pallas kernels, level_two_chunk(): pl.pallas_call(level_two_kernel, grid=(STEPS,), in_specs=[pl.BlockSpec((p...  10.3 us
  transfers between devices with their start and end apart: 30, of which 19 were waited for; matrix products, arithmetic and copies ran while one was open for 0% of the time, Pallas kernels for 10%

profile of v1, /device:TPU:1, one launch (start us, length us, event | category | flops | bytes accessed | tf_op | source)
XLA Modules:
  0.0 320.4 jit_solution(7511966534654526729)
XLA Ops:
  4.5 3.7 %collective-permute-start.17 = (bf16[32,64,128]{2,1,0:T(8,128)(2,1)S(1)}, bf16[32,64,128]{2,1,0:T(8,128)(2,1)S(1)}, u32[]{:S(2)}, u32[]{:S(2)}) collective-permute-start(bf16[32,64,128]{2,1,0:T(8,128)(2,1)S(1)} %shard_map.65), channel_id=1, source_target_pairs={{0,4},{1,5},{2,6},{3,7},{4,0},{5,1},{6,2},{7,3},{8,12},{9,13},{10,... | collective-permute-start | bytes 1572872 | tf_op jit(solution)/shard_map/ppermute | solution.py:23
  10.1 8.6 %collective-permute-done.17 = bf16[32,64,128]{2,1,0:T(8,128)(2,1)S(1)} collective-permute-done((bf16[32,64,128]{2,1,0:T(8,128)(2,1)S(1)}, bf16[32,64,128]{2,1,0:T(8,128)(2,1)S(1)}, u32[]{:S(2)}, u32[]{:S(2)}) %collective-permute-start.17) | collective-permute-done | bytes 524320 | tf_op jit(solution)/shard_map/ppermute | solution.py:23
  21.2 11.0 %all-to-all-start.8 = ((bf16[16,64,128]{2,1,0:T(8,128)(2,1)}), bf16[16,64,128]{2,1,0:T(8,128)(2,1)S(1)}, u32[]{:S(2)}, u32[]{:S(2)}) async-start(bf16[16,64,128]{2,1,0:T(8,128)(2,1)} %copy-done.30), calls=%async_computation.8 | async-start | bytes 524288 | tf_op jit(solution)/shard_map/all_to_all | solution.py:29
  35.4 2.8 collective-permute-start.13
  40.6 3.2 %all-to-all-done.8.refs_0_ = bf16[16,64,128]{2,1,0:T(8,128)(2,1)S(1)} async-done(((bf16[16,64,128]{2,1,0:T(8,128)(2,1)}), bf16[16,64,128]{2,1,0:T(8,128)(2,1)S(1)}, u32[]{:S(2)}, u32[]{:S(2)}) %all-to-all-start.8) | async-done | bytes 262176 | tf_op jit(solution)/shard_map/all_to_all | solution.py:29
  43.8 4.5 %all-to-all-start.9 = ((bf16[16,64,128]{2,1,0:T(8,128)(2,1)}), bf16[16,64,128]{2,1,0:T(8,128)(2,1)}, u32[]{:S(2)}, u32[]{:S(2)}) async-start(bf16[16,64,128]{2,1,0:T(8,128)(2,1)} %copy-done.28), calls=%async_computation.9 | async-start | bytes 524288 | tf_op jit(solution)/shard_map/all_to_all | solution.py:29
  48.4 24.7 %collective-permute-done.1 = bf16[32,64,128]{2,1,0:T(8,128)(2,1)} collective-permute-done((bf16[32,64,128]{2,1,0:T(8,128)(2,1)}, bf16[32,64,128]{2,1,0:T(8,128)(2,1)}, u32[]{:S(2)}, u32[]{:S(2)}) %collective-permute-start.1) | collective-permute-done | bytes 524320 | tf_op jit(solution)/shard_map/ppermute | solution.py:23
  77.2 7.7 %all-to-all-start = ((bf16[16,64,128]{2,1,0:T(8,128)(2,1)}), bf16[16,64,128]{2,1,0:T(8,128)(2,1)S(1)}, u32[]{:S(2)}, u32[]{:S(2)}) async-start(bf16[16,64,128]{2,1,0:T(8,128)(2,1)} %copy-done.29), calls=%async_computation | async-start | bytes 524288 | tf_op jit(solution)/shard_map/all_to_all | solution.py:29
  89.3 7.4 %all-to-all-done.refs_0_ = bf16[16,64,128]{2,1,0:T(8,128)(2,1)S(1)} async-done(((bf16[16,64,128]{2,1,0:T(8,128)(2,1)}), bf16[16,64,128]{2,1,0:T(8,128)(2,1)S(1)}, u32[]{:S(2)}, u32[]{:S(2)}) %all-to-all-start) | async-done | bytes 262176 | tf_op jit(solution)/shard_map/all_to_all | solution.py:29
  96.6 4.1 %all-to-all-start.6 = ((bf16[16,64,256]{2,1,0:T(8,128)(2,1)}), bf16[16,64,256]{2,1,0:T(8,128)(2,1)}, u32[]{:S(2)}, u32[]{:S(2)}) async-start(bf16[16,64,256]{2,1,0:T(8,128)(2,1)} %copy-done.15), calls=%async_computation.6 | async-start | bytes 1048576 | tf_op jit(solution)/shard_map/all_to_all | solution.py:29
  106.9 10.7 %all-to-all-done.6.refs_0_ = bf16[16,64,256]{2,1,0:T(8,128)(2,1)} async-done(((bf16[16,64,256]{2,1,0:T(8,128)(2,1)}), bf16[16,64,256]{2,1,0:T(8,128)(2,1)}, u32[]{:S(2)}, u32[]{:S(2)}) %all-to-all-start.6) | async-done | bytes 524320 | tf_op jit(solution)/shard_map/all_to_all | solution.py:29
  117.6 4.1 %all-to-all-start.7 = ((bf16[16,64,256]{2,1,0:T(8,128)(2,1)}), bf16[16,64,256]{2,1,0:T(8,128)(2,1)}, u32[]{:S(2)}, u32[]{:S(2)}) async-start(bf16[16,64,256]{2,1,0:T(8,128)(2,1)} %copy-done.14), calls=%async_computation.7 | async-start | bytes 1048576 | tf_op jit(solution)/shard_map/all_to_all | solution.py:29
  121.7 9.1 %collective-permute-done.9 = bf16[32,64,256]{2,1,0:T(8,128)(2,1)} collective-permute-done((bf16[32,64,256]{2,1,0:T(8,128)(2,1)S(1)}, bf16[32,64,256]{2,1,0:T(8,128)(2,1)}, u32[]{:S(2)}, u32[]{:S(2)}) %collective-permute-start.9) | collective-permute-done | bytes 1048608 | tf_op jit(solution)/shard_map/ppermute | solution.py:23
  138.0 4.1 %all-to-all-start.4 = ((bf16[16,64,256]{2,1,0:T(8,128)(2,1)}), bf16[16,64,256]{2,1,0:T(8,128)(2,1)}, u32[]{:S(2)}, u32[]{:S(2)}) async-start(bf16[16,64,256]{2,1,0:T(8,128)(2,1)} %copy-done.16), calls=%async_computation.4 | async-start | bytes 1048576 | tf_op jit(solution)/shard_map/all_to_all | solution.py:29
  148.2 11.2 %all-to-all-done.4.refs_0_ = bf16[16,64,256]{2,1,0:T(8,128)(2,1)} async-done(((bf16[16,64,256]{2,1,0:T(8,128)(2,1)}), bf16[16,64,256]{2,1,0:T(8,128)(2,1)}, u32[]{:S(2)}, u32[]{:S(2)}) %all-to-all-start.4) | async-done | bytes 524320 | tf_op jit(solution)/shard_map/all_to_all | solution.py:29
  159.4 4.1 %all-to-all-start.5 = ((bf16[16,64,256]{2,1,0:T(8,128)(2,1)}), bf16[16,64,256]{2,1,0:T(8,128)(2,1)}, u32[]{:S(2)}, u32[]{:S(2)}) async-start(bf16[16,64,256]{2,1,0:T(8,128)(2,1)} %copy-done.13), calls=%async_computation.5 | async-start | bytes 1048576 | tf_op jit(solution)/shard_map/all_to_all | solution.py:29
  163.6 8.2 %collective-permute-done.5 = bf16[32,64,256]{2,1,0:T(8,128)(2,1)S(1)} collective-permute-done((bf16[32,64,256]{2,1,0:T(8,128)(2,1)S(1)}, bf16[32,64,256]{2,1,0:T(8,128)(2,1)S(1)}, u32[]{:S(2)}, u32[]{:S(2)}) %collective-permute-start.5) | collective-permute-done | bytes 1048608 | tf_op jit(solution)/shard_map/ppermute | solution.py:23
  174.6 5.1 %all-to-all-done.5 = bf16[16,64,256]{2,1,0:T(8,128)(2,1)} async-done(((bf16[16,64,256]{2,1,0:T(8,128)(2,1)}), bf16[16,64,256]{2,1,0:T(8,128)(2,1)}, u32[]{:S(2)}, u32[]{:S(2)}) %all-to-all-start.5) | async-done | bytes 524320 | tf_op jit(solution)/shard_map/all_to_all | solution.py:29
  179.8 20.2 %all_to_all.50.refs_0_ = bf16[16,64,256]{2,1,0:T(8,128)(2,1)S(1)} all-to-all(bf16[16,64,256]{2,1,0:T(8,128)(2,1)} %copy-done.17), channel_id=1, replica_groups={{0,8,16,24,32,40,48,56,64,72,80,88,96,104,112,120},{128,136,144,152,160..., dimensions={0} | all-to-all | bytes 1048576 | tf_op jit(solution)/shard_map/all_to_all | solution.py:29
  199.9 4.1 %all-to-all-start.3 = ((bf16[16,64,256]{2,1,0:T(8,128)(2,1)}), bf16[16,64,256]{2,1,0:T(8,128)(2,1)}, u32[]{:S(2)}, u32[]{:S(2)}) async-start(bf16[16,64,256]{2,1,0:T(8,128)(2,1)} %copy-done.12), calls=%async_computation.3 | async-start | bytes 1048576 | tf_op jit(solution)/shard_map/all_to_all | solution.py:29
  205.6 2.9 collective-permute-start.19
  210.5 7.8 %collective-permute-done.partner = bf16[32,64,64]{2,1,0:T(8,128)(2,1)S(1)} collective-permute-done((bf16[32,64,64]{2,1,0:T(8,128)(2,1)}, bf16[32,64,64]{2,1,0:T(8,128)(2,1)S(1)}, u32[]{:S(2)}, u32[]{:S(2)}) %collective-permute-start) | collective-permute-done | bytes 262176 | tf_op jit(solution)/shard_map/ppermute | solution.py:23
  225.2 6.5 %collective-permute-done.19.refs_2_ = bf16[16,64,128]{2,1,0:T(8,128)(2,1)S(1)} collective-permute-done((bf16[16,64,128]{2,1,0:T(8,128)(2,1)}, bf16[16,64,128]{2,1,0:T(8,128)(2,1)S(1)}, u32[]{:S(2)}, u32[]{:S(2)}) %collective-permute-start.19) | collective-permute-done | bytes 262176 | tf_op jit(solution)/shard_map/ppermute | solution.py:23
  232.4 24.6 %collective-permute-done.20.refs_3_ = bf16[16,64,128]{2,1,0:T(8,128)(2,1)S(1)} collective-permute-done((bf16[16,64,128]{2,1,0:T(8,128)(2,1)}, bf16[16,64,128]{2,1,0:T(8,128)(2,1)S(1)}, u32[]{:S(2)}, u32[]{:S(2)}) %collective-permute-start.20) | collective-permute-done | bytes 262176 | tf_op jit(solution)/shard_map/ppermute | solution.py:23
  260.9 6.1 %all-to-all-start.1 = ((bf16[16,64,128]{2,1,0:T(8,128)(2,1)}), bf16[16,64,128]{2,1,0:T(8,128)(2,1)}, u32[]{:S(2)}, u32[]{:S(2)}) async-start(bf16[16,64,128]{2,1,0:T(8,128)(2,1)} %copy-done.27), calls=%async_computation.1 | async-start | bytes 524288 | tf_op jit(solution)/shard_map/all_to_all | solution.py:29
  271.0 6.1 %collective-permute-done.11.refs_2_ = bf16[16,64,256]{2,1,0:T(8,128)(2,1)} collective-permute-done((bf16[16,64,256]{2,1,0:T(8,128)(2,1)}, bf16[16,64,256]{2,1,0:T(8,128)(2,1)}, u32[]{:S(2)}, u32[]{:S(2)}) %collective-permute-start.11) | collective-permute-done | bytes 524320 | tf_op jit(solution)/shard_map/ppermute | solution.py:23
  278.7 6.1 %collective-permute-done.12.refs_3_ = bf16[16,64,256]{2,1,0:T(8,128)(2,1)} collective-permute-done((bf16[16,64,256]{2,1,0:T(8,128)(2,1)}, bf16[16,64,256]{2,1,0:T(8,128)(2,1)}, u32[]{:S(2)}, u32[]{:S(2)}) %collective-permute-start.12) | collective-permute-done | bytes 524320 | tf_op jit(solution)/shard_map/ppermute | solution.py:23
  285.7 2.9 collective-permute-start.4
  298.4 3.8 %shard_map.68.refs_4_ = bf16[2,16,64,1024]{3,2,1,0:T(8,128)(2,1)} custom-call(bf16[16,128,256]{2,1,0:T(8,128)(2,1)S(1)} %shard_map.55.weights, bf16[16,64,256]{2,1,0:T(8,128)(2,1)} %all-to-all-done.6.refs_0_, bf16[16,64,256]{2,1,0:T(8,128)(2,1)S(1)} %collective-permute-done.14.refs_1_, ...), custom_call_target="tpu_custom_call", output_to_operand_aliasing={{}: (5, {})} | custom-call | flops 268435456 | bytes 3145728 | tf_op jit(solution)/shard_map/pallas_call | solution.py:184
  302.1 4.0 %shard_map.69.refs_4_ = bf16[2,16,64,1024]{3,2,1,0:T(8,128)(2,1)} custom-call(bf16[16,128,256]{2,1,0:T(8,128)(2,1)S(1)} %shard_map.55.weights, bf16[16,64,256]{2,1,0:T(8,128)(2,1)} %all-to-all-done.4.refs_0_, bf16[16,64,256]{2,1,0:T(8,128)(2,1)S(1)} %copy-done.11, ...), custom_call_target="tpu_custom_call", output_to_operand_aliasing={{}: (5, {})} | custom-call | flops 268435456 | bytes 3145728 | tf_op jit(solution)/shard_map/pallas_call | solution.py:184
  306.1 6.8 %collective-permute-done.8.refs_3_ = bf16[16,64,256]{2,1,0:T(8,128)(2,1)} collective-permute-done((bf16[16,64,256]{2,1,0:T(8,128)(2,1)}, bf16[16,64,256]{2,1,0:T(8,128)(2,1)}, u32[]{:S(2)}, u32[]{:S(2)}) %collective-permute-start.8) | collective-permute-done | bytes 524320 | tf_op jit(solution)/shard_map/ppermute | solution.py:23
  312.9 4.0 %shard_map.70.refs_4_ = bf16[2,16,64,1024]{3,2,1,0:T(8,128)(2,1)} custom-call(bf16[16,128,256]{2,1,0:T(8,128)(2,1)S(1)} %shard_map.55.weights, bf16[16,64,256]{2,1,0:T(8,128)(2,1)S(1)} %all_to_all.50.refs_0_, bf16[16,64,256]{2,1,0:T(8,128)(2,1)} %collective-permute-done.6.refs_1_, ...), custom_call_target="tpu_custom_call", output_to_operand_aliasing={{}: (5, {})} | custom-call | flops 268435456 | bytes 3145728 | tf_op jit(solution)/shard_map/pallas_call | solution.py:184
  (109 shorter events, 79.7 us)
Async XLA Ops:
  4.5 14.3 %collective-permute-start.17 = (bf16[32,64,128]{2,1,0:T(8,128)(2,1)S(1)}, bf16[32,64,128]{2,1,0:T(8,128)(2,1)S(1)}, u32[]{:S(2)}, u32[]{:S(2)}) collective-permute-start(bf16[32,64,128]{2,1,0:T(8,128)(2,1)S(1)} %shard_map.65), channel_id=1, source_target_pairs={{0,4},{1,5},{2,6},{3,7},{4,0},{5,1},{6,2},{7,3},{8,12},{9,13},{10,... | collective-permute-start | bytes 1572872 | tf_op jit(solution)/shard_map/ppermute | solution.py:23
  21.2 22.7 %all-to-all-start.8 = ((bf16[16,64,128]{2,1,0:T(8,128)(2,1)}), bf16[16,64,128]{2,1,0:T(8,128)(2,1)S(1)}, u32[]{:S(2)}, u32[]{:S(2)}) async-start(bf16[16,64,128]{2,1,0:T(8,128)(2,1)} %copy-done.30), calls=%async_computation.8 | async-start | bytes 524288 | tf_op jit(solution)/shard_map/all_to_all | solution.py:29
  35.4 49.5 %collective-permute-start.13 = (bf16[32,64,256]{2,1,0:T(8,128)(2,1)S(1)}, bf16[32,64,256]{2,1,0:T(8,128)(2,1)}, u32[]{:S(2)}, u32[]{:S(2)}) collective-permute-start(bf16[32,64,256]{2,1,0:T(8,128)(2,1)S(1)} %shard_map.63), channel_id=1, source_target_pairs={{0,4},{1,5},{2,6},{3,7},{4,0},{5,1},{6,2},{7,3},{8,12},{9,13},{10,... | collective-permute-start | bytes 3145736 | tf_op jit(solution)/shard_map/ppermute | solution.py:23
  40.4 32.7 %collective-permute-start.1 = (bf16[32,64,128]{2,1,0:T(8,128)(2,1)}, bf16[32,64,128]{2,1,0:T(8,128)(2,1)}, u32[]{:S(2)}, u32[]{:S(2)}) collective-permute-start(bf16[32,64,128]{2,1,0:T(8,128)(2,1)} %shard_map.57), channel_id=1, source_target_pairs={{0,4},{1,5},{2,6},{3,7},{4,0},{5,1},{6,2},{7,3},{8,12},{9,13},{10,... | collective-permute-start | bytes 1572872 | tf_op jit(solution)/shard_map/ppermute | solution.py:23
  43.8 33.4 %all-to-all-start.9 = ((bf16[16,64,128]{2,1,0:T(8,128)(2,1)}), bf16[16,64,128]{2,1,0:T(8,128)(2,1)}, u32[]{:S(2)}, u32[]{:S(2)}) async-start(bf16[16,64,128]{2,1,0:T(8,128)(2,1)} %copy-done.28), calls=%async_computation.9 | async-start | bytes 524288 | tf_op jit(solution)/shard_map/all_to_all | solution.py:29
  77.2 19.4 %all-to-all-start = ((bf16[16,64,128]{2,1,0:T(8,128)(2,1)}), bf16[16,64,128]{2,1,0:T(8,128)(2,1)S(1)}, u32[]{:S(2)}, u32[]{:S(2)}) async-start(bf16[16,64,128]{2,1,0:T(8,128)(2,1)} %copy-done.29), calls=%async_computation | async-start | bytes 524288 | tf_op jit(solution)/shard_map/all_to_all | solution.py:29
  96.6 21.0 %all-to-all-start.6 = ((bf16[16,64,256]{2,1,0:T(8,128)(2,1)}), bf16[16,64,256]{2,1,0:T(8,128)(2,1)}, u32[]{:S(2)}, u32[]{:S(2)}) async-start(bf16[16,64,256]{2,1,0:T(8,128)(2,1)} %copy-done.15), calls=%async_computation.6 | async-start | bytes 1048576 | tf_op jit(solution)/shard_map/all_to_all | solution.py:29
  104.1 26.7 %collective-permute-start.9 = (bf16[32,64,256]{2,1,0:T(8,128)(2,1)S(1)}, bf16[32,64,256]{2,1,0:T(8,128)(2,1)}, u32[]{:S(2)}, u32[]{:S(2)}) collective-permute-start(bf16[32,64,256]{2,1,0:T(8,128)(2,1)S(1)} %shard_map.61), channel_id=1, source_target_pairs={{0,4},{1,5},{2,6},{3,7},{4,0},{5,1},{6,2},{7,3},{8,12},{9,13},{10,... | collective-permute-start | bytes 3145736 | tf_op jit(solution)/shard_map/ppermute | solution.py:23
  117.6 20.4 %all-to-all-start.7 = ((bf16[16,64,256]{2,1,0:T(8,128)(2,1)}), bf16[16,64,256]{2,1,0:T(8,128)(2,1)}, u32[]{:S(2)}, u32[]{:S(2)}) async-start(bf16[16,64,256]{2,1,0:T(8,128)(2,1)} %copy-done.14), calls=%async_computation.7 | async-start | bytes 1048576 | tf_op jit(solution)/shard_map/all_to_all | solution.py:29
  138.0 21.5 %all-to-all-start.4 = ((bf16[16,64,256]{2,1,0:T(8,128)(2,1)}), bf16[16,64,256]{2,1,0:T(8,128)(2,1)}, u32[]{:S(2)}, u32[]{:S(2)}) async-start(bf16[16,64,256]{2,1,0:T(8,128)(2,1)} %copy-done.16), calls=%async_computation.4 | async-start | bytes 1048576 | tf_op jit(solution)/shard_map/all_to_all | solution.py:29
  145.4 26.4 %collective-permute-start.5 = (bf16[32,64,256]{2,1,0:T(8,128)(2,1)S(1)}, bf16[32,64,256]{2,1,0:T(8,128)(2,1)S(1)}, u32[]{:S(2)}, u32[]{:S(2)}) collective-permute-start(bf16[32,64,256]{2,1,0:T(8,128)(2,1)S(1)} %shard_map.59), channel_id=1, source_target_pairs={{0,4},{1,5},{2,6},{3,7},{4,0},{5,1},{6,2},{7,3},{8,12},{9,13},{10,... | collective-permute-start | bytes 3145736 | tf_op jit(solution)/shard_map/ppermute | solution.py:23
  159.4 20.3 %all-to-all-start.5 = ((bf16[16,64,256]{2,1,0:T(8,128)(2,1)}), bf16[16,64,256]{2,1,0:T(8,128)(2,1)}, u32[]{:S(2)}, u32[]{:S(2)}) async-start(bf16[16,64,256]{2,1,0:T(8,128)(2,1)} %copy-done.13), calls=%async_computation.5 | async-start | bytes 1048576 | tf_op jit(solution)/shard_map/all_to_all | solution.py:29
  174.6 118.9 %copy-start.8 = (bf16[16,64,128]{2,1,0:T(8,128)(2,1)S(1)}, bf16[16,64,128]{2,1,0:T(8,128)(2,1)}, u32[]{:S(2)}) copy-start(bf16[16,64,128]{2,1,0:T(8,128)(2,1)} %copy-done.7) | copy-start | bytes 786436
  199.9 60.9 %all-to-all-start.3 = ((bf16[16,64,256]{2,1,0:T(8,128)(2,1)}), bf16[16,64,256]{2,1,0:T(8,128)(2,1)}, u32[]{:S(2)}, u32[]{:S(2)}) async-start(bf16[16,64,256]{2,1,0:T(8,128)(2,1)} %copy-done.12), calls=%async_computation.3 | async-start | bytes 1048576 | tf_op jit(solution)/shard_map/all_to_all | solution.py:29
  204.1 14.3 %collective-permute-start = (bf16[32,64,64]{2,1,0:T(8,128)(2,1)}, bf16[32,64,64]{2,1,0:T(8,128)(2,1)S(1)}, u32[]{:S(2)}, u32[]{:S(2)}) collective-permute-start(bf16[32,64,64]{2,1,0:T(8,128)(2,1)} %middle.1), channel_id=1, source_target_pairs={{0,1},{1,0},{2,3},{3,2},{4,5},{5,4},{6,7},{7,6},{8,9},{9,8},{10,11... | collective-permute-start | bytes 786440 | tf_op jit(solution)/shard_map/ppermute | solution.py:23
  205.5 18.4 %collective-permute-start.18 = (bf16[16,64,128]{2,1,0:T(8,128)(2,1)}, bf16[16,64,128]{2,1,0:T(8,128)(2,1)S(1)}, u32[]{:S(2)}, u32[]{:S(2)}) collective-permute-start(bf16[16,64,128]{2,1,0:T(8,128)(2,1)} %copy-done.7), channel_id=1, source_target_pairs={{0,1},{1,0},{2,3},{3,2},{4,5},{5,4},{6,7},{7,6},{8,9},{9,8},{10,11... | collective-permute-start | bytes 786440 | tf_op jit(solution)/shard_map/ppermute | solution.py:23
  205.6 26.0 %collective-permute-start.19 = (bf16[16,64,128]{2,1,0:T(8,128)(2,1)}, bf16[16,64,128]{2,1,0:T(8,128)(2,1)S(1)}, u32[]{:S(2)}, u32[]{:S(2)}) collective-permute-start(bf16[16,64,128]{2,1,0:T(8,128)(2,1)} %all-to-all-done.9), channel_id=1, source_target_pairs={{0,128},{1,129},{2,130},{3,131},{4,132},{5,133},{6,134},{7,135},{8... | collective-permute-start | bytes 786440 | tf_op jit(solution)/shard_map/ppermute | solution.py:23
  208.6 50.8 %collective-permute-start.14 = (bf16[16,64,256]{2,1,0:T(8,128)(2,1)}, bf16[16,64,256]{2,1,0:T(8,128)(2,1)S(1)}, u32[]{:S(2)}, u32[]{:S(2)}) collective-permute-start(bf16[16,64,256]{2,1,0:T(8,128)(2,1)} %all-to-all-done.6.refs_0_), channel_id=1, source_target_pairs={{0,1},{1,0},{2,3},{3,2},{4,5},{5,4},{6,7},{7,6},{8,9},{9,8},{10,11... | collective-permute-start | bytes 1572872 | tf_op jit(solution)/shard_map/ppermute | solution.py:23
  209.0 51.2 %collective-permute-start.15 = (bf16[16,64,256]{2,1,0:T(8,128)(2,1)}, bf16[16,64,256]{2,1,0:T(8,128)(2,1)S(1)}, u32[]{:S(2)}, u32[]{:S(2)}) collective-permute-start(bf16[16,64,256]{2,1,0:T(8,128)(2,1)} %all-to-all-done.7), channel_id=1, source_target_pairs={{0,128},{1,129},{2,130},{3,131},{4,132},{5,133},{6,134},{7,135},{8... | collective-permute-start | bytes 1572872 | tf_op jit(solution)/shard_map/ppermute | solution.py:23
  219.1 47.8 %collective-permute-start.16 = (bf16[16,64,256]{2,1,0:T(8,128)(2,1)}, bf16[16,64,256]{2,1,0:T(8,128)(2,1)S(1)}, u32[]{:S(2)}, u32[]{:S(2)}) collective-permute-start(bf16[16,64,256]{2,1,0:T(8,128)(2,1)} %all-to-all-done.7), channel_id=1, source_target_pairs={{0,129},{1,128},{2,131},{3,130},{4,133},{5,132},{6,135},{7,134},{8... | collective-permute-start | bytes 1572872 | tf_op jit(solution)/shard_map/ppermute | solution.py:23
  223.9 61.9 %copy-start.21 = (bf16[16,64,128]{2,1,0:T(8,128)(2,1)}, bf16[16,64,128]{2,1,0:T(8,128)(2,1)S(1)}, u32[]{:S(2)}) copy-start(bf16[16,64,128]{2,1,0:T(8,128)(2,1)S(1)} %collective-permute-done.18.refs_1_) | copy-start | bytes 786436
  223.9 45.6 %collective-permute-start.10 = (bf16[16,64,256]{2,1,0:T(8,128)(2,1)}, bf16[16,64,256]{2,1,0:T(8,128)(2,1)S(1)}, u32[]{:S(2)}, u32[]{:S(2)}) collective-permute-start(bf16[16,64,256]{2,1,0:T(8,128)(2,1)} %all-to-all-done.4.refs_0_), channel_id=1, source_target_pairs={{0,1},{1,0},{2,3},{3,2},{4,5},{5,4},{6,7},{7,6},{8,9},{9,8},{10,11... | collective-permute-start | bytes 1572872 | tf_op jit(solution)/shard_map/ppermute | solution.py:23
  232.4 24.7 %collective-permute-start.20 = (bf16[16,64,128]{2,1,0:T(8,128)(2,1)}, bf16[16,64,128]{2,1,0:T(8,128)(2,1)S(1)}, u32[]{:S(2)}, u32[]{:S(2)}) collective-permute-start(bf16[16,64,128]{2,1,0:T(8,128)(2,1)} %all-to-all-done.9), channel_id=1, source_target_pairs={{0,129},{1,128},{2,131},{3,130},{4,133},{5,132},{6,135},{7,134},{8... | collective-permute-start | bytes 786440 | tf_op jit(solution)/shard_map/ppermute | solution.py:23
  257.7 19.4 %collective-permute-start.11 = (bf16[16,64,256]{2,1,0:T(8,128)(2,1)}, bf16[16,64,256]{2,1,0:T(8,128)(2,1)}, u32[]{:S(2)}, u32[]{:S(2)}) collective-permute-start(bf16[16,64,256]{2,1,0:T(8,128)(2,1)} %all-to-all-done.5), channel_id=1, source_target_pairs={{0,128},{1,129},{2,130},{3,131},{4,132},{5,133},{6,134},{7,135},{8... | collective-permute-start | bytes 1572872 | tf_op jit(solution)/shard_map/ppermute | solution.py:23
  259.3 25.5 %collective-permute-start.12 = (bf16[16,64,256]{2,1,0:T(8,128)(2,1)}, bf16[16,64,256]{2,1,0:T(8,128)(2,1)}, u32[]{:S(2)}, u32[]{:S(2)}) collective-permute-start(bf16[16,64,256]{2,1,0:T(8,128)(2,1)} %all-to-all-done.5), channel_id=1, source_target_pairs={{0,129},{1,128},{2,131},{3,130},{4,133},{5,132},{6,135},{7,134},{8... | collective-permute-start | bytes 1572872 | tf_op jit(solution)/shard_map/ppermute | solution.py:23
  260.2 25.5 %collective-permute-start.6 = (bf16[16,64,256]{2,1,0:T(8,128)(2,1)S(1)}, bf16[16,64,256]{2,1,0:T(8,128)(2,1)}, u32[]{:S(2)}, u32[]{:S(2)}) collective-permute-start(bf16[16,64,256]{2,1,0:T(8,128)(2,1)S(1)} %all_to_all.50.refs_0_), channel_id=1, source_target_pairs={{0,1},{1,0},{2,3},{3,2},{4,5},{5,4},{6,7},{7,6},{8,9},{9,8},{10,11... | collective-permute-start | bytes 1572872 | tf_op jit(solution)/shard_map/ppermute | solution.py:23
  260.9 17.9 %all-to-all-start.1 = ((bf16[16,64,128]{2,1,0:T(8,128)(2,1)}), bf16[16,64,128]{2,1,0:T(8,128)(2,1)}, u32[]{:S(2)}, u32[]{:S(2)}) async-start(bf16[16,64,128]{2,1,0:T(8,128)(2,1)} %copy-done.27), calls=%async_computation.1 | async-start | bytes 524288 | tf_op jit(solution)/shard_map/all_to_all | solution.py:29
  266.9 39.2 %collective-permute-start.7 = (bf16[16,64,256]{2,1,0:T(8,128)(2,1)}, bf16[16,64,256]{2,1,0:T(8,128)(2,1)}, u32[]{:S(2)}, u32[]{:S(2)}) collective-permute-start(bf16[16,64,256]{2,1,0:T(8,128)(2,1)} %all-to-all-done.3), channel_id=1, source_target_pairs={{0,128},{1,129},{2,130},{3,131},{4,132},{5,133},{6,134},{7,135},{8... | collective-permute-start | bytes 1572872 | tf_op jit(solution)/shard_map/ppermute | solution.py:23
  270.2 42.6 %collective-permute-start.8 = (bf16[16,64,256]{2,1,0:T(8,128)(2,1)}, bf16[16,64,256]{2,1,0:T(8,128)(2,1)}, u32[]{:S(2)}, u32[]{:S(2)}) collective-permute-start(bf16[16,64,256]{2,1,0:T(8,128)(2,1)} %all-to-all-done.3), channel_id=1, source_target_pairs={{0,129},{1,128},{2,131},{3,130},{4,133},{5,132},{6,135},{7,134},{8... | collective-permute-start | bytes 1572872 | tf_op jit(solution)/shard_map/ppermute | solution.py:23
  277.1 39.7 %collective-permute-start.2 = (bf16[16,64,128]{2,1,0:T(8,128)(2,1)S(1)}, bf16[16,64,128]{2,1,0:T(8,128)(2,1)S(1)}, u32[]{:S(2)}, u32[]{:S(2)}) collective-permute-start(bf16[16,64,128]{2,1,0:T(8,128)(2,1)S(1)} %all-to-all-done.refs_0_), channel_id=1, source_target_pairs={{0,1},{1,0},{2,3},{3,2},{4,5},{5,4},{6,7},{7,6},{8,9},{9,8},{10,11... | collective-permute-start | bytes 786440 | tf_op jit(solution)/shard_map/ppermute | solution.py:23
  284.8 32.1 %collective-permute-start.3 = (bf16[16,64,128]{2,1,0:T(8,128)(2,1)}, bf16[16,64,128]{2,1,0:T(8,128)(2,1)S(1)}, u32[]{:S(2)}, u32[]{:S(2)}) collective-permute-start(bf16[16,64,128]{2,1,0:T(8,128)(2,1)} %all-to-all-done.1), channel_id=1, source_target_pairs={{0,128},{1,129},{2,130},{3,131},{4,132},{5,133},{6,134},{7,135},{8... | collective-permute-start | bytes 786440 | tf_op jit(solution)/shard_map/ppermute | solution.py:23
  285.7 32.7 %collective-permute-start.4 = (bf16[16,64,128]{2,1,0:T(8,128)(2,1)}, bf16[16,64,128]{2,1,0:T(8,128)(2,1)S(1)}, u32[]{:S(2)}, u32[]{:S(2)}) collective-permute-start(bf16[16,64,128]{2,1,0:T(8,128)(2,1)} %all-to-all-done.1), channel_id=1, source_target_pairs={{0,129},{1,128},{2,131},{3,130},{4,133},{5,132},{6,135},{7,134},{8... | collective-permute-start | bytes 786440 | tf_op jit(solution)/shard_map/ppermute | solution.py:23
  (29 other events, 93.8 us)

commit v2 on v1

v2 whole, which is shorter than its diff:
```python
import functools

import jax
import jax.numpy as jnp
from jax import lax
from jax.experimental import pallas as pl
from jax.experimental.pallas import tpu as pltpu
from jax.sharding import PartitionSpec as P

AXES = ("tr", "pt")
CHUNKS = ((0, 128), (256, 256), (512, 256), (768, 256), (128, 128))
STEPS = 4
VMEM = 24 * 1024 * 1024


def exchanged(array, flip_tr, flip_pt):
    n_tr, n_pt = lax.axis_size("tr"), lax.axis_size("pt")
    pairs = [
        (t * n_pt + s, (t ^ flip_tr) * n_pt + (s ^ flip_pt))
        for t in range(n_tr)
        for s in range(n_pt)
    ]
    return lax.ppermute(array, AXES, pairs)


def spread(array):
    n = lax.axis_size("tr") // 2
    groups = [[h * n + i for i in range(n)] for h in range(2)]
    return lax.all_to_all(
        array, "tr", split_axis=0, concat_axis=0, tiled=True, axis_index_groups=groups
    )


def params():
    return pltpu.CompilerParams(vmem_limit_bytes=VMEM)


def cost(flops, moved):
    return pl.CostEstimate(flops=100000000000, bytes_accessed=370000000, transcendentals=0)


def ordered_call(kernel, operands, in_specs, after=(), aliases=None, **kwargs):
    n = len(operands)
    after = [x for x in after if not any(x is y for y in operands)]

    def body(*refs):
        kernel(*refs[:n], *refs[n + len(after) :])

    specs = list(in_specs) + [pl.BlockSpec(memory_space=pltpu.HBM)] * len(after)
    return pl.pallas_call(
        body,
        in_specs=specs,
        input_output_aliases=aliases or {},
        compiler_params=params(),
        **kwargs,
    )(*operands, *after)


def level_one_kernel(chunks, weights, values, *refs):
    outs, (weight_buf, buf, sems) = refs[: len(chunks)], refs[len(chunks) :]
    groups = weights.shape[0]
    part, start, width = groups // STEPS, chunks[0][2], buf.shape[2]
    copies = []
    for i in range(STEPS):
        for k, (source, target, n) in enumerate(
            ((weights, weight_buf, part), (values.at[:, :, start : start + width], buf, 4 * part))
        ):
            rows = pl.ds(i * n, n)
            copy = pltpu.make_async_copy(source.at[rows], target.at[rows], sems.at[i, k])
            copy.start()
            copies.append(copy)
    for i in range(STEPS):
        copies[2 * i].wait()
        copies[2 * i + 1].wait()
        for q in range(i * part, (i + 1) * part):
            rows = buf[4 * q : 4 * q + 4].reshape(weights.shape[2], width)
            product = jnp.dot(weight_buf[q], rows, preferred_element_type=jnp.float32)
            product = product.astype(jnp.bfloat16).reshape(4, -1, width)
            for (at, size, _), out in zip(chunks, outs):
                out[4 * q : 4 * q + 4] = product[:, :, at - start : at - start + size]


def level_one_chunks(weights, values, chunks, after):
    blocks, rank, _ = values.shape
    start = min(at for at, _ in chunks)
    width = max(at + size for at, size in chunks) - start
    chunks = tuple((at, size, start) for at, size in chunks)
    return ordered_call(
        functools.partial(level_one_kernel, chunks),
        [weights, values],
        [pl.BlockSpec(memory_space=pltpu.HBM)] * 2,
        after,
        out_specs=[pl.BlockSpec(memory_space=pltpu.VMEM)] * len(chunks),
        out_shape=[
            jax.ShapeDtypeStruct((blocks, rank, size), jnp.bfloat16) for _, size, _ in chunks
        ],
        scratch_shapes=[
            pltpu.VMEM(weights.shape, jnp.bfloat16),
            pltpu.VMEM((blocks, rank, width), jnp.bfloat16),
            pltpu.SemaphoreType.DMA((STEPS, 2)),
        ],
        cost_estimate=cost(0, 0),
        name="one",
    )


def order_kernel(flags, weights, out):
    groups = out.shape[0]
    rank = weights.shape[1]
    upper_s, upper_t = flags[0], flags[1]
    for j in range(groups):
        for row in range(2):
            half = upper_t if row == 0 else 1 - upper_t
            block = weights[j + groups * half]
            low, high = block[:, : 2 * rank], block[:, 2 * rank :]
            rows = slice(row * rank, (row + 1) * rank)
            out[j, rows, : 2 * rank] = jnp.where(upper_s == 1, high, low)
            out[j, rows, 2 * rank :] = jnp.where(upper_s == 1, low, high)


def ordered_two(flags, weights, after):
    blocks, rank, depth = weights.shape
    return ordered_call(
        order_kernel,
        [flags, weights],
        [
            pl.BlockSpec(memory_space=pltpu.SMEM),
            pl.BlockSpec(memory_space=pltpu.VMEM),
        ],
        after,
        out_specs=pl.BlockSpec(memory_space=pltpu.VMEM),
        out_shape=jax.ShapeDtypeStruct((blocks // 2, 2 * rank, depth), jnp.bfloat16),
        cost_estimate=cost(0, 4 * blocks * rank * depth),
        name="order",
    )


def level_two_kernel(weights, own, other, out):
    rank, size = own.shape[2:]
    for j in range(own.shape[1]):
        rows = jnp.concatenate([own[0, j], own[1, j], other[0, j], other[1, j]], axis=0)
        product = jnp.dot(weights[j], rows, preferred_element_type=jnp.float32)
        out[j] = product.astype(out.dtype).reshape(2, rank, size)


def level_two_chunk(weights, own, other, after):
    blocks, rank, size = own.shape
    half = blocks // 2
    part = half // STEPS
    pair = pl.BlockSpec((2, part, rank, size), lambda i: (0, i, 0, 0))
    return ordered_call(
        level_two_kernel,
        [weights, own.reshape(2, half, rank, size), other.reshape(2, half, rank, size)],
        [pl.BlockSpec((part, 2 * rank, 4 * rank), lambda i: (i, 0, 0)), pair, pair],
        after,
        grid=(STEPS,),
        out_specs=pl.BlockSpec((part, 2, rank, size), lambda i: (i, 0, 0, 0)),
        out_shape=jax.ShapeDtypeStruct((half, 2, rank, size), jnp.bfloat16),
        cost_estimate=pl.CostEstimate(flops=100000000000, bytes_accessed=370000000, transcendentals=0),
        name="two",
    )


def split_kernel(both, kept, sent):
    kept[...] = both[:, 0]
    sent[...] = both[:, 1]


def split_chunk(both, after):
    half, _, rank, size = both.shape
    part = half // 2
    out = jax.ShapeDtypeStruct((half, rank, size), jnp.bfloat16)
    out_spec = pl.BlockSpec((part, rank, size), lambda i: (i, 0, 0))
    return ordered_call(
        split_kernel,
        [both],
        [pl.BlockSpec((part, 2, rank, size), lambda i: (i, 0, 0, 0))],
        after,
        grid=(2,),
        out_specs=[out_spec, out_spec],
        out_shape=[out, out],
        cost_estimate=cost(0, 8 * half * rank * size),
        name="split",
    )


def compose_kernel(flags, weights, middle, partner, out):
    groups, rank = out.shape[0], weights.shape[1]

    def for_place(low_s, upper_t):
        for j in range(groups):
            rows = jnp.concatenate([weights[j], weights[j + groups]], axis=0)
            for slot in range(4):
                e, f = low_s ^ (slot & 1), upper_t ^ (slot >> 1)
                centre = (partner if slot & 1 else middle)[j + groups * f]
                at = (2 * e + f) * rank
                product = jnp.dot(
                    rows[:, at : at + rank], centre, preferred_element_type=jnp.float32
                )
                out[j, :, slot * rank : (slot + 1) * rank] = product.astype(out.dtype)

    for low_s in range(2):
        for upper_t in range(2):
            here = (flags[2] == low_s) & (flags[1] == upper_t)
            pl.when(here)(functools.partial(for_place, low_s, upper_t))


def composed_three(flags, weights, middle, partner, after):
    blocks, rank, depth = weights.shape
    return ordered_call(
        compose_kernel,
        [flags, weights, middle, partner],
        [pl.BlockSpec(memory_space=pltpu.SMEM)]
        + [pl.BlockSpec(memory_space=pltpu.VMEM)] * 3,
        after,
        out_specs=pl.BlockSpec(memory_space=pltpu.VMEM),
        out_shape=jax.ShapeDtypeStruct((blocks // 2, 2 * rank, depth), jnp.bfloat16),
        cost_estimate=cost(2 * blocks * rank * depth * rank, 6 * blocks * rank * depth),
        name="compose",
    )


def level_three_kernel(weights, *refs):
    pieces, out = refs[:4], refs[-1]
    rank = out.shape[2]
    for j in range(out.shape[1]):
        rows = jnp.concatenate([piece[j] for piece in pieces], axis=0)
        product = jnp.dot(weights[j], rows, preferred_element_type=jnp.float32)
        product = product.astype(out.dtype)
        out[0, j] = product[:rank]
        out[1, j] = product[rank:]


def level_three_chunk(weights, pieces, result, shape, start, after):
    half, rank, size = pieces[0].shape
    part = half // STEPS
    column = start // size
    in_specs = [pl.BlockSpec((part, 2 * rank, 4 * rank), lambda i: (i, 0, 0))]
    in_specs += [pl.BlockSpec((part, rank, size), lambda i: (i, 0, 0))] * 4
    operands, aliases = [weights, *pieces], {}
    if result is not None:
        in_specs.append(pl.BlockSpec(memory_space=pltpu.HBM))
        operands.append(result)
        aliases = {5: 0}
    return ordered_call(
        level_three_kernel,
        operands,
        in_specs,
        after,
        aliases,
        grid=(STEPS,),
        out_specs=pl.BlockSpec((2, part, rank, size), lambda i: (0, i, 0, column)),
        out_shape=jax.ShapeDtypeStruct((2, half, rank, shape[2]), jnp.bfloat16),
        cost_estimate=cost(4 * half * rank * 4 * rank * size, 12 * half * rank * size),
        name="three",
    )


def shards(gathers, level_one, level_two, middle, level_three):
    n_tr, n_pt = lax.axis_size("tr"), lax.axis_size("pt")
    t, s = lax.axis_index("tr"), lax.axis_index("pt")
    flags = jnp.stack([s >> 2, t >> 4, s & 1]).astype(jnp.int32)
    count = len(CHUNKS)
    own, other, both, pieces = {}, {}, {}, {}
    result, last = None, ()

    def one(cs):
        nonlocal last
        outs = level_one_chunks(level_one, gathers, [CHUNKS[c] for c in cs], last)
        last = (outs[0],)
        for c, out in zip(cs, outs):
            own[c] = out
            other[c] = exchanged(out, 0, n_pt // 2)

    def two(c):
        nonlocal last
        if c >= count:
            return
        mixed = level_two_chunk(weights_two, own[c], other[c], last)
        last = (mixed,)
        both[c] = spread(mixed)

    def split(c):
        nonlocal last
        kept, sent = split_chunk(both[c], last)
        last = (sent,)
        pieces[c] = (
            kept,
            exchanged(kept, 0, 1),
            exchanged(sent, n_tr // 2, 0),
            exchanged(sent, n_tr // 2, 1),
        )

    def three(c):
        nonlocal result, last
        if c < 0:
            return
        result = level_three_chunk(
            weights_three, pieces[c], result, gathers.shape, CHUNKS[c][0], last
        )
        last = (result,)

    partner = exchanged(middle, 0, 1)
    one([0])
    one(range(1, count))
    weights_two = ordered_two(flags, level_two, last)
    last = (weights_two,)
    two(0)
    weights_three = composed_three(flags, level_three, middle, partner, last)
    last = (weights_three,)
    two(1)
    for c in range(count):
        split(c)
        three(c - 1)
        two(c + 2)
    three(count - 1)
    return result.reshape(gathers.shape)


def solution(mesh):
    spec = P(("tr", "pt"), None, None)
    return jax.shard_map(
        shards, mesh=mesh, in_specs=(spec,) * 5, out_specs=spec, check_vma=False
    )
```

time: 322 us -> 199 us (0.62)
  waiting for transfers between devices: 154 us -> 69.6 us
  starting transfers between devices: 83.1 us -> 60.9 us
  Pallas kernels: 34.7 us -> 55.8 us
  blocking collectives: 20.2 us -> 0 us
  local copies, waits for them, and re-layouts: 27.9 us -> 11 us
    ppermute x21, waiting for transfers between devices: 112 us -> 14.5 us  [exchanged(): return lax.ppermute(array, AXES, pairs)]
    all_to_all x9 -> x5, starting transfers between devices: 50 us -> 28.3 us  [spread(): lax.all_to_all(array, 'tr', split_axis=0, concat_axis=0, tiled=True, axis...]
    pallas_call x17 -> x19, Pallas kernels: 34.7 us -> 55.8 us  [ordered_call(): pl.pallas_call(body, in_specs=specs, input_output_aliases=aliases or {},...]
    all_to_all x1 -> x0, blocking collectives: 20.2 us -> none  [spread(): lax.all_to_all(array, 'tr', split_axis=0, concat_axis=0, tiled=True, axis...]
    unnamed x62 -> x22, local copies, waits for them, and re-layouts: 27.9 us -> 11 us
    all_to_all x9 -> x5, waiting for transfers between devices: 42 us -> 55.1 us  [spread(): lax.all_to_all(array, 'tr', split_axis=0, concat_axis=0, tiled=True, axis...]
  transfers between devices with their start and end apart: 30 -> 26, of which waited for: 19 -> 9; matrix products, arithmetic and copies ran while one was open for 0% -> 0% of each run, Pallas kernels for 10% -> 26%
where the time goes in v2:
time: 199 us; the launch traced here: 198 us
  waiting for transfers between devices  69.6 us (35%)
  starting transfers between devices  60.9 us (31%)
  Pallas kernels  55.8 us (28%)
  local copies, waits for them, and re-layouts  11 us (6%)
    pallas_call x19, Pallas kernels, ordered_call(): pl.pallas_call(body, in_specs=specs, input_output_aliases=aliases or {},...  55.8 us
    all_to_all x5, waiting for transfers between devices, spread(): lax.all_to_all(array, 'tr', split_axis=0, concat_axis=0, tiled=True, axis...  55.1 us
    ppermute x21, starting transfers between devices, exchanged(): return lax.ppermute(array, AXES, pairs)  32.7 us
    all_to_all x5, starting transfers between devices, spread(): lax.all_to_all(array, 'tr', split_axis=0, concat_axis=0, tiled=True, axis...  28.3 us
    ppermute x21, waiting for transfers between devices, exchanged(): return lax.ppermute(array, AXES, pairs)  14.5 us
    unnamed x22, local copies, waits for them, and re-layouts  11 us
  transfers between devices with their start and end apart: 26, of which 9 were waited for; matrix products, arithmetic and copies ran while one was open for 0% of the time, Pallas kernels for 26%

profile of v2, /device:TPU:1, one launch (start us, length us, event | category | flops | bytes accessed | tf_op | source)
XLA Modules:
  0.0 197.6 jit_solution(12228004485908776836)
XLA Ops:
  5.4 3.7 %collective-permute-start.1 = (bf16[32,64,128]{2,1,0:T(8,128)(2,1)}, bf16[32,64,128]{2,1,0:T(8,128)(2,1)}, u32[]{:S(2)}, u32[]{:S(2)}) collective-permute-start(bf16[32,64,128]{2,1,0:T(8,128)(2,1)} %one.2.refs_2_), channel_id=1, source_target_pairs={{0,4},{1,5},{2,6},{3,7},{4,0},{5,1},{6,2},{7,3},{8,12},{9,13},{10,... | collective-permute-start | bytes 1572872 | tf_op jit(solution)/shard_map/ppermute | solution.py:23
  10.4 4.2 %one.3 = (bf16[32,64,256]{2,1,0:T(8,128)(2,1)}, bf16[32,64,256]{2,1,0:T(8,128)(2,1)}, bf16[32,64,256]{2,1,0:T(8,128)(2,1)}, bf16[32,64,128]{2,1,0:T(8,128)(2,1)}) custom-call(bf16[8,256,256]{2,1,0:T(8,128)(2,1)S(1)} %copy-done.1, bf16[32,64,1024]{2,1,0:T(8,128)(2,1)S(1)} %copy-done, bf16[32,64,128]{2,1,0:T(8,128)(2,1)} %one.2.refs_2_), custom_call_target="tpu_custom_call" | custom-call | flops 99999997952 | bytes 370000000 | tf_op jit(solution)/shard_map/one/pallas_call | solution.py:50
  14.8 2.7 %collective-permute-start.4 = (bf16[32,64,256]{2,1,0:T(8,128)(2,1)}, bf16[32,64,256]{2,1,0:T(8,128)(2,1)}, u32[]{:S(2)}, u32[]{:S(2)}) collective-permute-start(bf16[32,64,256]{2,1,0:T(8,128)(2,1)} %get-tuple-element.21), channel_id=1, source_target_pairs={{0,4},{1,5},{2,6},{3,7},{4,0},{5,1},{6,2},{7,3},{8,12},{9,13},{10,... | collective-permute-start | bytes 3145736 | tf_op jit(solution)/shard_map/ppermute | solution.py:23
  20.0 3.7 %collective-permute-start.2 = (bf16[32,64,128]{2,1,0:T(8,128)(2,1)}, bf16[32,64,128]{2,1,0:T(8,128)(2,1)}, u32[]{:S(2)}, u32[]{:S(2)}) collective-permute-start(bf16[32,64,128]{2,1,0:T(8,128)(2,1)} %get-tuple-element.20), channel_id=1, source_target_pairs={{0,4},{1,5},{2,6},{3,7},{4,0},{5,1},{6,2},{7,3},{8,12},{9,13},{10,... | collective-permute-start | bytes 1572872 | tf_op jit(solution)/shard_map/ppermute | solution.py:23
  23.7 3.8 %two.5.refs_4_ = bf16[16,2,64,128]{3,2,1,0:T(8,128)(2,1)} custom-call(bf16[16,128,256]{2,1,0:T(8,128)(2,1)S(1)} %order.1.refs_0_, bf16[2,16,64,128]{3,2,1,0:T(8,128)(2,1)} %bitcast.3.refs_1_, bf16[2,16,64,128]{3,2,1,0:T(8,128)(2,1)} %bitcast.4.refs_2_), custom_call_target="tpu_custom_call" | custom-call | flops 99999997952 | bytes 370000000 | tf_op jit(solution)/shard_map/two/pallas_call | solution.py:50
  27.5 11.4 %all-to-all-start.1 = ((bf16[16,2,64,128]{3,2,1,0:T(8,128)(2,1)}), bf16[16,2,64,128]{3,2,1,0:T(8,128)(2,1)}, u32[]{:S(2)}, u32[]{:S(2)}) async-start(bf16[16,2,64,128]{3,2,1,0:T(8,128)(2,1)} %two.5.refs_4_), calls=%async_computation.1 | async-start | bytes 1048576 | tf_op jit(solution)/shard_map/all_to_all | solution.py:29
  38.9 2.2 %compose.1.refs_3_.refs_0_ = bf16[16,128,256]{2,1,0:T(8,128)(2,1)S(1)} custom-call(s32[3]{0:T(128)S(1)} %pad_add_fusion.refs_0_, bf16[32,64,256]{2,1,0:T(8,128)(2,1)S(1)} %copy-done.3, bf16[32,64,64]{2,1,0:T(8,128)(2,1)} %refs_2_.1, bf16[32,64,64]{2,1,0:T(8,128)(2,1)} %collective-permute-done.refs_3_, bf16[16,2,64,128]{3,2,1,0:T(8,128)(2,1)} %two.5.refs_4_), custom_call_target="tpu_custom_call" | custom-call | flops 99999997952 | bytes 370000000 | tf_op jit(solution)/shard_map/compose/pallas_call | solution.py:50
  42.4 4.0 %two.6.refs_1_ = bf16[16,2,64,256]{3,2,1,0:T(8,128)(2,1)} custom-call(bf16[16,128,256]{2,1,0:T(8,128)(2,1)S(1)} %order.1.refs_0_, bf16[2,16,64,256]{3,2,1,0:T(8,128)(2,1)} %bitcast.7.refs_1_, bf16[2,16,64,256]{3,2,1,0:T(8,128)(2,1)} %bitcast.8.refs_2_, bf16[16,128,256]{2,1,0:T(8,128)(2,1)S(1)} %compose.1.refs_3_.refs_0_), custom_call_target="tpu_custom_call" | custom-call | flops 99999997952 | bytes 370000000 | tf_op jit(solution)/shard_map/two/pallas_call | solution.py:50
  47.5 8.9 %all-to-all-done.1.refs_0_ = bf16[16,2,64,128]{3,2,1,0:T(8,128)(2,1)} async-done(((bf16[16,2,64,128]{3,2,1,0:T(8,128)(2,1)}), bf16[16,2,64,128]{3,2,1,0:T(8,128)(2,1)}, u32[]{:S(2)}, u32[]{:S(2)}) %all-to-all-start.1) | async-done | bytes 524320 | tf_op jit(solution)/shard_map/all_to_all | solution.py:29
  56.4 4.2 %all-to-all-start = ((bf16[16,2,64,256]{3,2,1,0:T(8,128)(2,1)}), bf16[16,2,64,256]{3,2,1,0:T(8,128)(2,1)}, u32[]{:S(2)}, u32[]{:S(2)}) async-start(bf16[16,2,64,256]{3,2,1,0:T(8,128)(2,1)} %two.6.refs_1_), calls=%async_computation | async-start | bytes 2097152 | tf_op jit(solution)/shard_map/all_to_all | solution.py:29
  62.4 2.7 %collective-permute-start.10 = (bf16[16,64,128]{2,1,0:T(8,128)(2,1)}, bf16[16,64,128]{2,1,0:T(8,128)(2,1)}, u32[]{:S(2)}, u32[]{:S(2)}) collective-permute-start(bf16[16,64,128]{2,1,0:T(8,128)(2,1)} %get-tuple-element.22.refs_3_), channel_id=1, source_target_pairs={{0,129},{1,128},{2,131},{3,130},{4,133},{5,132},{6,135},{7,134},{8... | collective-permute-start | bytes 786440 | tf_op jit(solution)/shard_map/ppermute | solution.py:23
  67.2 4.0 %two.7.refs_1_ = bf16[16,2,64,256]{3,2,1,0:T(8,128)(2,1)} custom-call(bf16[16,128,256]{2,1,0:T(8,128)(2,1)S(1)} %order.1.refs_0_, bf16[2,16,64,256]{3,2,1,0:T(8,128)(2,1)} %bitcast.9.refs_1_, bf16[2,16,64,256]{3,2,1,0:T(8,128)(2,1)} %bitcast.10.refs_2_, bf16[16,64,128]{2,1,0:T(8,128)(2,1)} %get-tuple-element.22.refs_3_), custom_call_target="tpu_custom_call" | custom-call | flops 99999997952 | bytes 370000000 | tf_op jit(solution)/shard_map/two/pallas_call | solution.py:50
  71.2 16.4 %all-to-all-done.refs_0_ = bf16[16,2,64,256]{3,2,1,0:T(8,128)(2,1)} async-done(((bf16[16,2,64,256]{3,2,1,0:T(8,128)(2,1)}), bf16[16,2,64,256]{3,2,1,0:T(8,128)(2,1)}, u32[]{:S(2)}, u32[]{:S(2)}) %all-to-all-start) | async-done | bytes 1048608 | tf_op jit(solution)/shard_map/all_to_all | solution.py:29
  87.6 4.2 %all-to-all-start.2 = ((bf16[16,2,64,256]{3,2,1,0:T(8,128)(2,1)}), bf16[16,2,64,256]{3,2,1,0:T(8,128)(2,1)}, u32[]{:S(2)}, u32[]{:S(2)}) async-start(bf16[16,2,64,256]{3,2,1,0:T(8,128)(2,1)} %two.7.refs_1_), calls=%async_computation.2 | async-start | bytes 2097152 | tf_op jit(solution)/shard_map/all_to_all | solution.py:29
  94.1 2.9 %collective-permute-start.6 = (bf16[16,64,256]{2,1,0:T(8,128)(2,1)}, bf16[16,64,256]{2,1,0:T(8,128)(2,1)}, u32[]{:S(2)}, u32[]{:S(2)}) collective-permute-start(bf16[16,64,256]{2,1,0:T(8,128)(2,1)} %get-tuple-element.24.refs_5_), channel_id=1, source_target_pairs={{0,128},{1,129},{2,130},{3,131},{4,132},{5,133},{6,134},{7,135},{8... | collective-permute-start | bytes 1572872 | tf_op jit(solution)/shard_map/ppermute | solution.py:23
  97.8 3.7 %three.5.refs_3_.refs_5_ = bf16[2,16,64,1024]{3,2,1,0:T(8,128)(2,1)} custom-call(bf16[16,128,256]{2,1,0:T(8,128)(2,1)S(1)} %copy-done.8, bf16[16,64,128]{2,1,0:T(8,128)(2,1)} %get-tuple-element.25.refs_1_, bf16[16,64,128]{2,1,0:T(8,128)(2,1)} %collective-permute-done.8.refs_2_, bf16[16,64,128]{2,1,0:T(8,128)(2,1)} %collective-permute-done.9.refs_3_, ...), custom_call_target="tpu_custom_call" | custom-call | flops 99999997952 | bytes 370000000 | tf_op jit(solution)/shard_map/three/pallas_call | solution.py:50
  103.6 4.0 %two.8.refs_1_ = bf16[16,2,64,256]{3,2,1,0:T(8,128)(2,1)} custom-call(bf16[16,128,256]{2,1,0:T(8,128)(2,1)S(1)} %order.1.refs_0_, bf16[2,16,64,256]{3,2,1,0:T(8,128)(2,1)} %bitcast.11.refs_1_, bf16[2,16,64,256]{3,2,1,0:T(8,128)(2,1)} %bitcast.12.refs_2_, bf16[2,16,64,1024]{3,2,1,0:T(8,128)(2,1)S(1)} %copy-done.4), custom_call_target="tpu_custom_call" | custom-call | flops 99999997952 | bytes 370000000 | tf_op jit(solution)/shard_map/two/pallas_call | solution.py:50
  107.6 11.5 %all-to-all-done.2.refs_0_ = bf16[16,2,64,256]{3,2,1,0:T(8,128)(2,1)} async-done(((bf16[16,2,64,256]{3,2,1,0:T(8,128)(2,1)}), bf16[16,2,64,256]{3,2,1,0:T(8,128)(2,1)}, u32[]{:S(2)}, u32[]{:S(2)}) %all-to-all-start.2) | async-done | bytes 1048608 | tf_op jit(solution)/shard_map/all_to_all | solution.py:29
  119.2 4.2 %all-to-all-start.4 = ((bf16[16,2,64,256]{3,2,1,0:T(8,128)(2,1)}), bf16[16,2,64,256]{3,2,1,0:T(8,128)(2,1)}, u32[]{:S(2)}, u32[]{:S(2)}) async-start(bf16[16,2,64,256]{3,2,1,0:T(8,128)(2,1)} %two.8.refs_1_), calls=%async_computation.4 | async-start | bytes 2097152 | tf_op jit(solution)/shard_map/all_to_all | solution.py:29
  125.6 2.9 %collective-permute-start.13 = (bf16[16,64,256]{2,1,0:T(8,128)(2,1)}, bf16[16,64,256]{2,1,0:T(8,128)(2,1)}, u32[]{:S(2)}, u32[]{:S(2)}) collective-permute-start(bf16[16,64,256]{2,1,0:T(8,128)(2,1)} %get-tuple-element.27.refs_6_), channel_id=1, source_target_pairs={{0,128},{1,129},{2,130},{3,131},{4,132},{5,133},{6,134},{7,135},{8... | collective-permute-start | bytes 1572872 | tf_op jit(solution)/shard_map/ppermute | solution.py:23
  129.3 4.1 %three.6.refs_3_.refs_5_ = bf16[2,16,64,1024]{3,2,1,0:T(8,128)(2,1)} custom-call(bf16[16,128,256]{2,1,0:T(8,128)(2,1)S(1)} %copy-done.9, bf16[16,64,256]{2,1,0:T(8,128)(2,1)} %get-tuple-element.23.refs_1_, bf16[16,64,256]{2,1,0:T(8,128)(2,1)} %collective-permute-done.5.refs_2_, ...), custom_call_target="tpu_custom_call", output_to_operand_aliasing={{}: (5, {})} | custom-call | flops 99999997952 | bytes 370000000 | tf_op jit(solution)/shard_map/three/pallas_call | solution.py:50
  135.6 3.7 %two.9.refs_1_ = bf16[16,2,64,128]{3,2,1,0:T(8,128)(2,1)} custom-call(bf16[16,128,256]{2,1,0:T(8,128)(2,1)S(1)} %order.1.refs_0_, bf16[2,16,64,128]{3,2,1,0:T(8,128)(2,1)} %bitcast.5.refs_1_, bf16[2,16,64,128]{3,2,1,0:T(8,128)(2,1)} %bitcast.6.refs_2_, bf16[2,16,64,1024]{3,2,1,0:T(8,128)(2,1)S(1)} %copy-done.5), custom_call_target="tpu_custom_call" | custom-call | flops 99999997952 | bytes 370000000 | tf_op jit(solution)/shard_map/two/pallas_call | solution.py:50
  139.3 11.4 %all-to-all-done.4.refs_0_ = bf16[16,2,64,256]{3,2,1,0:T(8,128)(2,1)} async-done(((bf16[16,2,64,256]{3,2,1,0:T(8,128)(2,1)}), bf16[16,2,64,256]{3,2,1,0:T(8,128)(2,1)}, u32[]{:S(2)}, u32[]{:S(2)}) %all-to-all-start.4) | async-done | bytes 1048608 | tf_op jit(solution)/shard_map/all_to_all | solution.py:29
  150.7 4.1 %all-to-all-start.3 = ((bf16[16,2,64,128]{3,2,1,0:T(8,128)(2,1)}), bf16[16,2,64,128]{3,2,1,0:T(8,128)(2,1)}, u32[]{:S(2)}, u32[]{:S(2)}) async-start(bf16[16,2,64,128]{3,2,1,0:T(8,128)(2,1)} %two.9.refs_1_), calls=%async_computation.3 | async-start | bytes 1048576 | tf_op jit(solution)/shard_map/all_to_all | solution.py:29
  157.0 2.9 %collective-permute-start.19 = (bf16[16,64,256]{2,1,0:T(8,128)(2,1)}, bf16[16,64,256]{2,1,0:T(8,128)(2,1)}, u32[]{:S(2)}, u32[]{:S(2)}) collective-permute-start(bf16[16,64,256]{2,1,0:T(8,128)(2,1)} %get-tuple-element.29.refs_6_), channel_id=1, source_target_pairs={{0,128},{1,129},{2,130},{3,131},{4,132},{5,133},{6,134},{7,135},{8... | collective-permute-start | bytes 1572872 | tf_op jit(solution)/shard_map/ppermute | solution.py:23
  160.8 4.1 %three.7.refs_1_.refs_5_ = bf16[2,16,64,1024]{3,2,1,0:T(8,128)(2,1)} custom-call(bf16[16,128,256]{2,1,0:T(8,128)(2,1)S(1)} %copy-done.10, bf16[16,64,256]{2,1,0:T(8,128)(2,1)} %get-tuple-element.28.refs_1_, bf16[16,64,256]{2,1,0:T(8,128)(2,1)} %collective-permute-done.12.refs_2_, ...), custom_call_target="tpu_custom_call", output_to_operand_aliasing={{}: (5, {})} | custom-call | flops 99999997952 | bytes 370000000 | tf_op jit(solution)/shard_map/three/pallas_call | solution.py:50
  164.8 6.8 %all-to-all-done.3.refs_0_ = bf16[16,2,64,128]{3,2,1,0:T(8,128)(2,1)} async-done(((bf16[16,2,64,128]{3,2,1,0:T(8,128)(2,1)}), bf16[16,2,64,128]{3,2,1,0:T(8,128)(2,1)}, u32[]{:S(2)}, u32[]{:S(2)}) %all-to-all-start.3) | async-done | bytes 524320 | tf_op jit(solution)/shard_map/all_to_all | solution.py:29
  171.6 2.2 %copy-done.6 = bf16[2,16,64,1024]{3,2,1,0:T(8,128)(2,1)S(1)} copy-done((bf16[2,16,64,1024]{3,2,1,0:T(8,128)(2,1)S(1)}, bf16[2,16,64,1024]{3,2,1,0:T(8,128)(2,1)}, u32[]{:S(2)}) %copy-start.6) | copy-done | bytes 4194328
  174.9 3.0 %collective-permute-start.16 = (bf16[16,64,128]{2,1,0:T(8,128)(2,1)S(1)}, bf16[16,64,128]{2,1,0:T(8,128)(2,1)S(1)}, u32[]{:S(2)}, u32[]{:S(2)}) collective-permute-start(bf16[16,64,128]{2,1,0:T(8,128)(2,1)S(1)} %get-tuple-element.31.refs_6_), channel_id=1, source_target_pairs={{0,128},{1,129},{2,130},{3,131},{4,132},{5,133},{6,134},{7,135},{8... | collective-permute-start | bytes 786440 | tf_op jit(solution)/shard_map/ppermute | solution.py:23
  178.7 5.7 %collective-permute-done.18.refs_2_ = bf16[16,64,256]{2,1,0:T(8,128)(2,1)} collective-permute-done((bf16[16,64,256]{2,1,0:T(8,128)(2,1)}, bf16[16,64,256]{2,1,0:T(8,128)(2,1)}, u32[]{:S(2)}, u32[]{:S(2)}) %collective-permute-start.18) | collective-permute-done | bytes 524320 | tf_op jit(solution)/shard_map/ppermute | solution.py:23
  185.5 4.1 %three.8.refs_5_ = bf16[2,16,64,1024]{3,2,1,0:T(8,128)(2,1)} custom-call(bf16[16,128,256]{2,1,0:T(8,128)(2,1)S(1)} %copy-done.10, bf16[16,64,256]{2,1,0:T(8,128)(2,1)} %get-tuple-element.32.refs_1_, bf16[16,64,256]{2,1,0:T(8,128)(2,1)} %collective-permute-done.18.refs_2_, ...), custom_call_target="tpu_custom_call", output_to_operand_aliasing={{}: (5, {})} | custom-call | flops 99999997952 | bytes 370000000 | tf_op jit(solution)/shard_map/three/pallas_call | solution.py:50
  189.6 6.0 %collective-permute-done.15.refs_2_ = bf16[16,64,128]{2,1,0:T(8,128)(2,1)S(1)} collective-permute-done((bf16[16,64,128]{2,1,0:T(8,128)(2,1)S(1)}, bf16[16,64,128]{2,1,0:T(8,128)(2,1)S(1)}, u32[]{:S(2)}, u32[]{:S(2)}) %collective-permute-start.15) | collective-permute-done | bytes 262176 | tf_op jit(solution)/shard_map/ppermute | solution.py:23
  (62 shorter events, 33.6 us)
Async XLA Ops:
  5.4 12.5 %copy-start.2 = (bf16[32,64,256]{2,1,0:T(8,128)(2,1)S(1)}, bf16[32,64,256]{2,1,0:T(8,128)(2,1)}, u32[]{:S(2)}) copy-start(bf16[32,64,256]{2,1,0:T(8,128)(2,1)} %refs_1_.6) | copy-start | bytes 3145732
  5.4 14.6 %collective-permute-start.1 = (bf16[32,64,128]{2,1,0:T(8,128)(2,1)}, bf16[32,64,128]{2,1,0:T(8,128)(2,1)}, u32[]{:S(2)}, u32[]{:S(2)}) collective-permute-start(bf16[32,64,128]{2,1,0:T(8,128)(2,1)} %one.2.refs_2_), channel_id=1, source_target_pairs={{0,4},{1,5},{2,6},{3,7},{4,0},{5,1},{6,2},{7,3},{8,12},{9,13},{10,... | collective-permute-start | bytes 1572872 | tf_op jit(solution)/shard_map/ppermute | solution.py:23
  9.1 29.9 %collective-permute-start = (bf16[32,64,64]{2,1,0:T(8,128)(2,1)}, bf16[32,64,64]{2,1,0:T(8,128)(2,1)}, u32[]{:S(2)}, u32[]{:S(2)}) collective-permute-start(bf16[32,64,64]{2,1,0:T(8,128)(2,1)} %refs_2_.1), channel_id=1, source_target_pairs={{0,1},{1,0},{2,3},{3,2},{4,5},{5,4},{6,7},{7,6},{8,9},{9,8},{10,11... | collective-permute-start | bytes 786440 | tf_op jit(solution)/shard_map/ppermute | solution.py:23
  14.5 27.9 %collective-permute-start.3 = (bf16[32,64,256]{2,1,0:T(8,128)(2,1)}, bf16[32,64,256]{2,1,0:T(8,128)(2,1)}, u32[]{:S(2)}, u32[]{:S(2)}) collective-permute-start(bf16[32,64,256]{2,1,0:T(8,128)(2,1)} %get-tuple-element.19.refs_2_), channel_id=1, source_target_pairs={{0,4},{1,5},{2,6},{3,7},{4,0},{5,1},{6,2},{7,3},{8,12},{9,13},{10,... | collective-permute-start | bytes 3145736 | tf_op jit(solution)/shard_map/ppermute | solution.py:23
  14.8 50.6 %collective-permute-start.4 = (bf16[32,64,256]{2,1,0:T(8,128)(2,1)}, bf16[32,64,256]{2,1,0:T(8,128)(2,1)}, u32[]{:S(2)}, u32[]{:S(2)}) collective-permute-start(bf16[32,64,256]{2,1,0:T(8,128)(2,1)} %get-tuple-element.21), channel_id=1, source_target_pairs={{0,4},{1,5},{2,6},{3,7},{4,0},{5,1},{6,2},{7,3},{8,12},{9,13},{10,... | collective-permute-start | bytes 3145736 | tf_op jit(solution)/shard_map/ppermute | solution.py:23
  17.6 83.8 %collective-permute-start.11 = (bf16[32,64,256]{2,1,0:T(8,128)(2,1)}, bf16[32,64,256]{2,1,0:T(8,128)(2,1)}, u32[]{:S(2)}, u32[]{:S(2)}) collective-permute-start(bf16[32,64,256]{2,1,0:T(8,128)(2,1)} %get-tuple-element.26), channel_id=1, source_target_pairs={{0,4},{1,5},{2,6},{3,7},{4,0},{5,1},{6,2},{7,3},{8,12},{9,13},{10,... | collective-permute-start | bytes 3145736 | tf_op jit(solution)/shard_map/ppermute | solution.py:23
  20.0 113.4 %collective-permute-start.2 = (bf16[32,64,128]{2,1,0:T(8,128)(2,1)}, bf16[32,64,128]{2,1,0:T(8,128)(2,1)}, u32[]{:S(2)}, u32[]{:S(2)}) collective-permute-start(bf16[32,64,128]{2,1,0:T(8,128)(2,1)} %get-tuple-element.20), channel_id=1, source_target_pairs={{0,4},{1,5},{2,6},{3,7},{4,0},{5,1},{6,2},{7,3},{8,12},{9,13},{10,... | collective-permute-start | bytes 1572872 | tf_op jit(solution)/shard_map/ppermute | solution.py:23
  23.7 15.3 %copy-start.3 = (bf16[32,64,256]{2,1,0:T(8,128)(2,1)S(1)}, bf16[32,64,256]{2,1,0:T(8,128)(2,1)}, u32[]{:S(2)}) copy-start(bf16[32,64,256]{2,1,0:T(8,128)(2,1)} %refs_1_.7) | copy-start | bytes 3145732
  27.5 28.9 %all-to-all-start.1 = ((bf16[16,2,64,128]{3,2,1,0:T(8,128)(2,1)}), bf16[16,2,64,128]{3,2,1,0:T(8,128)(2,1)}, u32[]{:S(2)}, u32[]{:S(2)}) async-start(bf16[16,2,64,128]{3,2,1,0:T(8,128)(2,1)} %two.5.refs_4_), calls=%async_computation.1 | async-start | bytes 1048576 | tf_op jit(solution)/shard_map/all_to_all | solution.py:29
  56.4 31.3 %all-to-all-start = ((bf16[16,2,64,256]{3,2,1,0:T(8,128)(2,1)}), bf16[16,2,64,256]{3,2,1,0:T(8,128)(2,1)}, u32[]{:S(2)}, u32[]{:S(2)}) async-start(bf16[16,2,64,256]{3,2,1,0:T(8,128)(2,1)} %two.6.refs_1_), calls=%async_computation | async-start | bytes 2097152 | tf_op jit(solution)/shard_map/all_to_all | solution.py:29
  62.4 31.7 %collective-permute-start.10 = (bf16[16,64,128]{2,1,0:T(8,128)(2,1)}, bf16[16,64,128]{2,1,0:T(8,128)(2,1)}, u32[]{:S(2)}, u32[]{:S(2)}) collective-permute-start(bf16[16,64,128]{2,1,0:T(8,128)(2,1)} %get-tuple-element.22.refs_3_), channel_id=1, source_target_pairs={{0,129},{1,128},{2,131},{3,130},{4,133},{5,132},{6,135},{7,134},{8... | collective-permute-start | bytes 786440 | tf_op jit(solution)/shard_map/ppermute | solution.py:23
  65.1 31.9 %collective-permute-start.9 = (bf16[16,64,128]{2,1,0:T(8,128)(2,1)}, bf16[16,64,128]{2,1,0:T(8,128)(2,1)}, u32[]{:S(2)}, u32[]{:S(2)}) collective-permute-start(bf16[16,64,128]{2,1,0:T(8,128)(2,1)} %get-tuple-element.22.refs_3_), channel_id=1, source_target_pairs={{0,128},{1,129},{2,130},{3,131},{4,132},{5,133},{6,134},{7,135},{8... | collective-permute-start | bytes 786440 | tf_op jit(solution)/shard_map/ppermute | solution.py:23
  65.4 32.3 %collective-permute-start.8 = (bf16[16,64,128]{2,1,0:T(8,128)(2,1)}, bf16[16,64,128]{2,1,0:T(8,128)(2,1)}, u32[]{:S(2)}, u32[]{:S(2)}) collective-permute-start(bf16[16,64,128]{2,1,0:T(8,128)(2,1)} %get-tuple-element.25.refs_1_), channel_id=1, source_target_pairs={{0,1},{1,0},{2,3},{3,2},{4,5},{5,4},{6,7},{7,6},{8,9},{9,8},{10,11... | collective-permute-start | bytes 786440 | tf_op jit(solution)/shard_map/ppermute | solution.py:23
  87.6 31.6 %all-to-all-start.2 = ((bf16[16,2,64,256]{3,2,1,0:T(8,128)(2,1)}), bf16[16,2,64,256]{3,2,1,0:T(8,128)(2,1)}, u32[]{:S(2)}, u32[]{:S(2)}) async-start(bf16[16,2,64,256]{3,2,1,0:T(8,128)(2,1)} %two.7.refs_1_), calls=%async_computation.2 | async-start | bytes 2097152 | tf_op jit(solution)/shard_map/all_to_all | solution.py:29
  91.9 5.9 %copy-start.8 = (bf16[16,128,256]{2,1,0:T(8,128)(2,1)S(1)}, bf16[16,128,256]{2,1,0:T(8,128)(2,1)}, u32[]{:S(2)}) copy-start(bf16[16,128,256]{2,1,0:T(8,128)(2,1)} %copy-done.7) | copy-start | bytes 3145732
  94.1 35.2 %collective-permute-start.6 = (bf16[16,64,256]{2,1,0:T(8,128)(2,1)}, bf16[16,64,256]{2,1,0:T(8,128)(2,1)}, u32[]{:S(2)}, u32[]{:S(2)}) collective-permute-start(bf16[16,64,256]{2,1,0:T(8,128)(2,1)} %get-tuple-element.24.refs_5_), channel_id=1, source_target_pairs={{0,128},{1,129},{2,130},{3,131},{4,132},{5,133},{6,134},{7,135},{8... | collective-permute-start | bytes 1572872 | tf_op jit(solution)/shard_map/ppermute | solution.py:23
  97.0 32.3 %collective-permute-start.7 = (bf16[16,64,256]{2,1,0:T(8,128)(2,1)}, bf16[16,64,256]{2,1,0:T(8,128)(2,1)}, u32[]{:S(2)}, u32[]{:S(2)}) collective-permute-start(bf16[16,64,256]{2,1,0:T(8,128)(2,1)} %get-tuple-element.24.refs_5_), channel_id=1, source_target_pairs={{0,129},{1,128},{2,131},{3,130},{4,133},{5,132},{6,135},{7,134},{8... | collective-permute-start | bytes 1572872 | tf_op jit(solution)/shard_map/ppermute | solution.py:23
  97.7 30.8 %collective-permute-start.5 = (bf16[16,64,256]{2,1,0:T(8,128)(2,1)}, bf16[16,64,256]{2,1,0:T(8,128)(2,1)}, u32[]{:S(2)}, u32[]{:S(2)}) collective-permute-start(bf16[16,64,256]{2,1,0:T(8,128)(2,1)} %get-tuple-element.23.refs_1_), channel_id=1, source_target_pairs={{0,1},{1,0},{2,3},{3,2},{4,5},{5,4},{6,7},{7,6},{8,9},{9,8},{10,11... | collective-permute-start | bytes 1572872 | tf_op jit(solution)/shard_map/ppermute | solution.py:23
  101.4 2.2 %copy-start.4 = (bf16[2,16,64,1024]{3,2,1,0:T(8,128)(2,1)S(1)}, bf16[2,16,64,1024]{3,2,1,0:T(8,128)(2,1)}, u32[]{:S(2)}) copy-start(bf16[2,16,64,1024]{3,2,1,0:T(8,128)(2,1)} %three.5.refs_3_.refs_5_) | copy-start | bytes 12582916
  119.2 31.6 %all-to-all-start.4 = ((bf16[16,2,64,256]{3,2,1,0:T(8,128)(2,1)}), bf16[16,2,64,256]{3,2,1,0:T(8,128)(2,1)}, u32[]{:S(2)}, u32[]{:S(2)}) async-start(bf16[16,2,64,256]{3,2,1,0:T(8,128)(2,1)} %two.8.refs_1_), calls=%async_computation.4 | async-start | bytes 2097152 | tf_op jit(solution)/shard_map/all_to_all | solution.py:29
  123.4 5.9 %copy-start.9 = (bf16[16,128,256]{2,1,0:T(8,128)(2,1)S(1)}, bf16[16,128,256]{2,1,0:T(8,128)(2,1)}, u32[]{:S(2)}) copy-start(bf16[16,128,256]{2,1,0:T(8,128)(2,1)} %copy-done.7) | copy-start | bytes 3145732
  125.6 35.2 %collective-permute-start.13 = (bf16[16,64,256]{2,1,0:T(8,128)(2,1)}, bf16[16,64,256]{2,1,0:T(8,128)(2,1)}, u32[]{:S(2)}, u32[]{:S(2)}) collective-permute-start(bf16[16,64,256]{2,1,0:T(8,128)(2,1)} %get-tuple-element.27.refs_6_), channel_id=1, source_target_pairs={{0,128},{1,129},{2,130},{3,131},{4,132},{5,133},{6,134},{7,135},{8... | collective-permute-start | bytes 1572872 | tf_op jit(solution)/shard_map/ppermute | solution.py:23
  128.5 32.2 %collective-permute-start.14 = (bf16[16,64,256]{2,1,0:T(8,128)(2,1)}, bf16[16,64,256]{2,1,0:T(8,128)(2,1)}, u32[]{:S(2)}, u32[]{:S(2)}) collective-permute-start(bf16[16,64,256]{2,1,0:T(8,128)(2,1)} %get-tuple-element.27.refs_6_), channel_id=1, source_target_pairs={{0,129},{1,128},{2,131},{3,130},{4,133},{5,132},{6,135},{7,134},{8... | collective-permute-start | bytes 1572872 | tf_op jit(solution)/shard_map/ppermute | solution.py:23
  129.3 31.4 %collective-permute-start.12 = (bf16[16,64,256]{2,1,0:T(8,128)(2,1)}, bf16[16,64,256]{2,1,0:T(8,128)(2,1)}, u32[]{:S(2)}, u32[]{:S(2)}) collective-permute-start(bf16[16,64,256]{2,1,0:T(8,128)(2,1)} %get-tuple-element.28.refs_1_), channel_id=1, source_target_pairs={{0,1},{1,0},{2,3},{3,2},{4,5},{5,4},{6,7},{7,6},{8,9},{9,8},{10,11... | collective-permute-start | bytes 1572872 | tf_op jit(solution)/shard_map/ppermute | solution.py:23
  150.7 20.9 %all-to-all-start.3 = ((bf16[16,2,64,128]{3,2,1,0:T(8,128)(2,1)}), bf16[16,2,64,128]{3,2,1,0:T(8,128)(2,1)}, u32[]{:S(2)}, u32[]{:S(2)}) async-start(bf16[16,2,64,128]{3,2,1,0:T(8,128)(2,1)} %two.9.refs_1_), calls=%async_computation.3 | async-start | bytes 1048576 | tf_op jit(solution)/shard_map/all_to_all | solution.py:29
  154.9 5.9 %copy-start.10 = (bf16[16,128,256]{2,1,0:T(8,128)(2,1)S(1)}, bf16[16,128,256]{2,1,0:T(8,128)(2,1)}, u32[]{:S(2)}) copy-start(bf16[16,128,256]{2,1,0:T(8,128)(2,1)} %copy-done.7) | copy-start | bytes 3145732
  157.0 28.5 %collective-permute-start.19 = (bf16[16,64,256]{2,1,0:T(8,128)(2,1)}, bf16[16,64,256]{2,1,0:T(8,128)(2,1)}, u32[]{:S(2)}, u32[]{:S(2)}) collective-permute-start(bf16[16,64,256]{2,1,0:T(8,128)(2,1)} %get-tuple-element.29.refs_6_), channel_id=1, source_target_pairs={{0,128},{1,129},{2,130},{3,131},{4,132},{5,133},{6,134},{7,135},{8... | collective-permute-start | bytes 1572872 | tf_op jit(solution)/shard_map/ppermute | solution.py:23
  160.0 25.5 %collective-permute-start.20 = (bf16[16,64,256]{2,1,0:T(8,128)(2,1)}, bf16[16,64,256]{2,1,0:T(8,128)(2,1)}, u32[]{:S(2)}, u32[]{:S(2)}) collective-permute-start(bf16[16,64,256]{2,1,0:T(8,128)(2,1)} %get-tuple-element.29.refs_6_), channel_id=1, source_target_pairs={{0,129},{1,128},{2,131},{3,130},{4,133},{5,132},{6,135},{7,134},{8... | collective-permute-start | bytes 1572872 | tf_op jit(solution)/shard_map/ppermute | solution.py:23
  160.7 23.7 %collective-permute-start.18 = (bf16[16,64,256]{2,1,0:T(8,128)(2,1)}, bf16[16,64,256]{2,1,0:T(8,128)(2,1)}, u32[]{:S(2)}, u32[]{:S(2)}) collective-permute-start(bf16[16,64,256]{2,1,0:T(8,128)(2,1)} %get-tuple-element.32.refs_1_), channel_id=1, source_target_pairs={{0,1},{1,0},{2,3},{3,2},{4,5},{5,4},{6,7},{7,6},{8,9},{9,8},{10,11... | collective-permute-start | bytes 1572872 | tf_op jit(solution)/shard_map/ppermute | solution.py:23
  174.9 20.7 %collective-permute-start.16 = (bf16[16,64,128]{2,1,0:T(8,128)(2,1)S(1)}, bf16[16,64,128]{2,1,0:T(8,128)(2,1)S(1)}, u32[]{:S(2)}, u32[]{:S(2)}) collective-permute-start(bf16[16,64,128]{2,1,0:T(8,128)(2,1)S(1)} %get-tuple-element.31.refs_6_), channel_id=1, source_target_pairs={{0,128},{1,129},{2,130},{3,131},{4,132},{5,133},{6,134},{7,135},{8... | collective-permute-start | bytes 786440 | tf_op jit(solution)/shard_map/ppermute | solution.py:23
  177.9 17.7 %collective-permute-start.17 = (bf16[16,64,128]{2,1,0:T(8,128)(2,1)S(1)}, bf16[16,64,128]{2,1,0:T(8,128)(2,1)S(1)}, u32[]{:S(2)}, u32[]{:S(2)}) collective-permute-start(bf16[16,64,128]{2,1,0:T(8,128)(2,1)S(1)} %get-tuple-element.31.refs_6_), channel_id=1, source_target_pairs={{0,129},{1,128},{2,131},{3,130},{4,133},{5,132},{6,135},{7,134},{8... | collective-permute-start | bytes 786440 | tf_op jit(solution)/shard_map/ppermute | solution.py:23
  184.4 11.2 %collective-permute-start.15 = (bf16[16,64,128]{2,1,0:T(8,128)(2,1)S(1)}, bf16[16,64,128]{2,1,0:T(8,128)(2,1)S(1)}, u32[]{:S(2)}, u32[]{:S(2)}) collective-permute-start(bf16[16,64,128]{2,1,0:T(8,128)(2,1)S(1)} %get-tuple-element.30.refs_1_), channel_id=1, source_target_pairs={{0,1},{1,0},{2,3},{3,2},{4,5},{5,4},{6,7},{7,6},{8,9},{9,8},{10,11... | collective-permute-start | bytes 786440 | tf_op jit(solution)/shard_map/ppermute | solution.py:23
  (5 other events, 8.8 us)

commit v3 on v2

--- a/solution.py
+++ b/solution.py
@@ -11,6 +11,7 @@
 CHUNKS = ((0, 128), (256, 256), (512, 256), (768, 256), (128, 128))
 STEPS = 4
 VMEM = 24 * 1024 * 1024
+WHOLE_VMEM = 60 * 1024 * 1024
 
 
 def exchanged(array, flip_tr, flip_pt):
@@ -31,15 +32,15 @@
     )
 
 
-def params():
-    return pltpu.CompilerParams(vmem_limit_bytes=VMEM)
+def params(vmem=VMEM):
+    return pltpu.CompilerParams(vmem_limit_bytes=vmem)
 
 
 def cost(flops, moved):
     return pl.CostEstimate(flops=100000000000, bytes_accessed=370000000, transcendentals=0)
 
 
-def ordered_call(kernel, operands, in_specs, after=(), aliases=None, **kwargs):
+def ordered_call(kernel, operands, in_specs, after=(), aliases=None, vmem=VMEM, **kwargs):
     n = len(operands)
     after = [x for x in after if not any(x is y for y in operands)]
 
@@ -51,7 +52,7 @@
         body,
         in_specs=specs,
         input_output_aliases=aliases or {},
-        compiler_params=params(),
+        compiler_params=params(vmem),
         **kwargs,
     )(*operands, *after)
 
@@ -99,6 +100,7 @@
             pltpu.VMEM((blocks, rank, width), jnp.bfloat16),
             pltpu.SemaphoreType.DMA((STEPS, 2)),
         ],
+        vmem=WHOLE_VMEM,
         cost_estimate=cost(0, 0),
         name="one",
     )
@@ -146,18 +148,67 @@
 def level_two_chunk(weights, own, other, after):
     blocks, rank, size = own.shape
     half = blocks // 2
-    part = half // STEPS
+    part = half // 2
     pair = pl.BlockSpec((2, part, rank, size), lambda i: (0, i, 0, 0))
     return ordered_call(
         level_two_kernel,
         [weights, own.reshape(2, half, rank, size), other.reshape(2, half, rank, size)],
         [pl.BlockSpec((part, 2 * rank, 4 * rank), lambda i: (i, 0, 0)), pair, pair],
         after,
-        grid=(STEPS,),
+        grid=(2,),
         out_specs=pl.BlockSpec((part, 2, rank, size), lambda i: (i, 0, 0, 0)),
         out_shape=jax.ShapeDtypeStruct((half, 2, rank, size), jnp.bfloat16),
         cost_estimate=pl.CostEstimate(flops=100000000000, bytes_accessed=370000000, transcendentals=0),
         name="two",
+    )
+
+
+def level_two_apart_kernel(weights, own, other, kept, sent):
+    rank = own.shape[2]
+    for j in range(own.shape[1]):
+        rows = jnp.concatenate([own[0, j], own[1, j], other[0, j], other[1, j]], axis=0)
+        product = jnp.dot(weights[j], rows, preferred_element_type=jnp.float32)
+        product = product.astype(kept.dtype)
+        kept[j] = product[:rank]
+        sent[j] = product[rank:]
+
+
+def level_two_apart(weights, own, other, after):
+    blocks, rank, size = own.shape
+    half = blocks // 2
+    part = half // 2
+    pair = pl.BlockSpec((2, part, rank, size), lambda i: (0, i, 0, 0))
+    return ordered_call(
+        level_two_apart_kernel,
+        [weights, own.reshape(2, half, rank, size), other.reshape(2, half, rank, size)],
+        [pl.BlockSpec((part, 2 * rank, 4 * rank), lambda i: (i, 0, 0)), pair, pair],
+        after,
+        grid=(2,),
+        out_specs=[pl.BlockSpec((part, rank, size), lambda i: (i, 0, 0))] * 2,
+        out_shape=[jax.ShapeDtypeStruct((half, rank, size), jnp.bfloat16)] * 2,
+        cost_estimate=cost(0, 0),
+        name="apart",
+    )
+
+
+def pack_kernel(*refs):
+    for i, ref in enumerate(refs[:4]):
+        refs[4][:, i] = ref[...]
+
+
+def pack_chunk(pieces, after):
+    half, rank, size = pieces[0].shape
+    part = half // 2
+    return ordered_call(
+        pack_kernel,
+        pieces,
+        [pl.BlockSpec((part, rank, size), lambda i: (i, 0, 0))] * 4,
+        after,
+        grid=(2,),
+        out_specs=pl.BlockSpec((part, 4, rank, size), lambda i: (i, 0, 0, 0)),
+        out_shape=jax.ShapeDtypeStruct((half, 4, rank, size), jnp.bfloat16),
+        cost_estimate=cost(0, 0),
+        name="pack",
     )
 
 
@@ -220,11 +271,15 @@
     )
 
 
-def level_three_kernel(weights, *refs):
-    pieces, out = refs[:4], refs[-1]
+def level_three_kernel(count, weights, *refs):
+    pieces, out, token = refs[:count], refs[-2], refs[-1]
+    token[...] = jnp.zeros_like(token)
     rank = out.shape[2]
     for j in range(out.shape[1]):
-        rows = jnp.concatenate([piece[j] for piece in pieces], axis=0)
+        if len(pieces) == 1:
+            rows = pieces[0][j].reshape(4 * rank, -1)
+        else:
+            rows = jnp.concatenate([piece[j] for piece in pieces], axis=0)
         product = jnp.dot(weights[j], rows, preferred_element_type=jnp.float32)
         product = product.astype(out.dtype)
         out[0, j] = product[:rank]
@@ -232,25 +287,34 @@
 
 
 def level_three_chunk(weights, pieces, result, shape, start, after):
-    half, rank, size = pieces[0].shape
-    part = half // STEPS
+    half, rank, size = pieces[0].shape[0], *pieces[0].shape[-2:]
+    part = half // 2
     column = start // size
     in_specs = [pl.BlockSpec((part, 2 * rank, 4 * rank), lambda i: (i, 0, 0))]
-    in_specs += [pl.BlockSpec((part, rank, size), lambda i: (i, 0, 0))] * 4
+    if len(pieces) == 1:
+        in_specs.append(pl.BlockSpec((part, 4, rank, size), lambda i: (i, 0, 0, 0)))
+    else:
+        in_specs += [pl.BlockSpec((part, rank, size), lambda i: (i, 0, 0))] * 4
     operands, aliases = [weights, *pieces], {}
     if result is not None:
         in_specs.append(pl.BlockSpec(memory_space=pltpu.HBM))
         operands.append(result)
-        aliases = {5: 0}
-    return ordered_call(
-        level_three_kernel,
+        aliases = {len(operands) - 1: 0}
+    return ordered_call(
+        functools.partial(level_three_kernel, len(pieces)),
         operands,
         in_specs,
         after,
         aliases,
-        grid=(STEPS,),
-        out_specs=pl.BlockSpec((2, part, rank, size), lambda i: (0, i, 0, column)),
-        out_shape=jax.ShapeDtypeStruct((2, half, rank, shape[2]), jnp.bfloat16),
+        grid=(2,),
+        out_specs=[
+            pl.BlockSpec((2, part, rank, size), lambda i: (0, i, 0, column)),
+            pl.BlockSpec((8, 128), lambda i: (0, 0)),
+        ],
+        out_shape=[
+            jax.ShapeDtypeStruct((2, half, rank, shape[2]), jnp.bfloat16),
+            jax.ShapeDtypeStruct((8, 128), jnp.float32),
+        ],
         cost_estimate=cost(4 * half * rank * 4 * rank * size, 12 * half * rank * size),
         name="three",
     )
@@ -280,25 +344,40 @@
         last = (mixed,)
         both[c] = spread(mixed)
 
-    def split(c):
-        nonlocal last
-        kept, sent = split_chunk(both[c], last)
-        last = (sent,)
-        pieces[c] = (
+    def swapped(kept, sent):
+        return (
             kept,
             exchanged(kept, 0, 1),
             exchanged(sent, n_tr // 2, 0),
             exchanged(sent, n_tr // 2, 1),
         )
 
+    def apart(c):
+        nonlocal last
+        kept, sent = level_two_apart(weights_two, own[c], other[c], last)
+        last = (sent,)
+        pieces[c] = swapped(kept, sent)
+
+    def pack(c):
+        nonlocal last
+        packed = pack_chunk(pieces[c], last)
+        last = (packed,)
+        pieces[c] = (spread(packed),)
+
+    def split(c):
+        nonlocal last
+        kept, sent = split_chunk(both[c], last)
+        last = (sent,)
+        pieces[c] = swapped(kept, sent)
+
     def three(c):
         nonlocal result, last
         if c < 0:
             return
-        result = level_three_chunk(
+        result, token = level_three_chunk(
             weights_three, pieces[c], result, gathers.shape, CHUNKS[c][0], last
         )
-        last = (result,)
+        last = (token,)
 
     partner = exchanged(middle, 0, 1)
     one([0])
@@ -309,11 +388,19 @@
     weights_three = composed_three(flags, level_three, middle, partner, last)
     last = (weights_three,)
     two(1)
-    for c in range(count):
-        split(c)
-        three(c - 1)
-        two(c + 2)
-    three(count - 1)
+    split(0)
+    two(2)
+    split(1)
+    three(0)
+    two(3)
+    apart(4)
+    split(2)
+    three(1)
+    pack(4)
+    split(3)
+    three(2)
+    three(4)
+    three(3)
     return result.reshape(gathers.shape)
 
 

time: 199 us -> 184 us (0.925)
  Pallas kernels: 55.8 us -> 45.8 us
  local copies, waits for them, and re-layouts: 11 us -> 3.48 us
  waiting for transfers between devices: 69.6 us -> 74.1 us
    all_to_all x5, waiting for transfers between devices: 55.1 us -> 71.2 us  [spread(): lax.all_to_all(array, 'tr', split_axis=0, concat_axis=0, tiled=True, axis...]
    ppermute x21, waiting for transfers between devices: 14.5 us -> 2.9 us  [exchanged(): return lax.ppermute(array, AXES, pairs)]
    pallas_call x19, Pallas kernels: 55.8 us -> 45.8 us  [ordered_call(): pl.pallas_call(body, in_specs=specs, input_output_aliases=aliases or {},...]
    unnamed x22 -> x26, local copies, waits for them, and re-layouts: 11 us -> 3.48 us
  transfers between devices with their start and end apart: 26 -> 26, of which waited for: 9 -> 8; matrix products, arithmetic and copies ran while one was open for 0% -> 0% of each run, Pallas kernels for 26% -> 22%
where the time goes in v3:
time: 184 us; the launch traced here: 183 us
  waiting for transfers between devices  74.1 us (40%)
  starting transfers between devices  59.6 us (32%)
  Pallas kernels  45.8 us (25%)
  local copies, waits for them, and re-layouts  3.48 us (2%)
    all_to_all x5, waiting for transfers between devices, spread(): lax.all_to_all(array, 'tr', split_axis=0, concat_axis=0, tiled=True, axis...  71.2 us
    pallas_call x19, Pallas kernels, ordered_call(): pl.pallas_call(body, in_specs=specs, input_output_aliases=aliases or {},...  45.8 us
    ppermute x21, starting transfers between devices, exchanged(): return lax.ppermute(array, AXES, pairs)  31.2 us
    all_to_all x5, starting transfers between devices, spread(): lax.all_to_all(array, 'tr', split_axis=0, concat_axis=0, tiled=True, axis...  28.4 us
  transfers between devices with their start and end apart: 26, of which 8 were waited for; matrix products, arithmetic and copies ran while one was open for 0% of the time, Pallas kernels for 22%

profile of v3, /device:TPU:1, one launch (start us, length us, event | category | flops | bytes accessed | tf_op | source)
XLA Modules:
  0.0 183.2 jit_solution(10614621573230312161)
XLA Ops:
  0.0 2.8 %one.2.refs_2_ = bf16[32,64,128]{2,1,0:T(8,128)(2,1)} custom-call(bf16[8,256,256]{2,1,0:T(8,128)(2,1)} %refs_0_.3, bf16[32,64,1024]{2,1,0:T(8,128)(2,1)} %refs_1_.5), custom_call_target="tpu_custom_call" | custom-call | flops 99999997952 | bytes 370000000 | tf_op jit(solution)/shard_map/one/pallas_call | solution.py:51
  2.8 3.7 %collective-permute-start.1 = (bf16[32,64,128]{2,1,0:T(8,128)(2,1)}, bf16[32,64,128]{2,1,0:T(8,128)(2,1)}, u32[]{:S(2)}, u32[]{:S(2)}) collective-permute-start(bf16[32,64,128]{2,1,0:T(8,128)(2,1)} %one.2.refs_2_), channel_id=1, source_target_pairs={{0,4},{1,5},{2,6},{3,7},{4,0},{5,1},{6,2},{7,3},{8,12},{9,13},{10,... | collective-permute-start | bytes 1572872 | tf_op jit(solution)/shard_map/ppermute | solution.py:24
  7.7 4.9 %one.3 = (bf16[32,64,256]{2,1,0:T(8,128)(2,1)}, bf16[32,64,256]{2,1,0:T(8,128)(2,1)}, bf16[32,64,256]{2,1,0:T(8,128)(2,1)}, bf16[32,64,128]{2,1,0:T(8,128)(2,1)}) custom-call(bf16[8,256,256]{2,1,0:T(8,128)(2,1)} %refs_0_.3, bf16[32,64,1024]{2,1,0:T(8,128)(2,1)} %refs_1_.5, bf16[32,64,128]{2,1,0:T(8,128)(2,1)} %one.2.refs_2_), custom_call_target="tpu_custom_call" | custom-call | flops 99999997952 | bytes 370000000 | tf_op jit(solution)/shard_map/one/pallas_call | solution.py:51
  12.9 2.7 %collective-permute-start.7 = (bf16[32,64,256]{2,1,0:T(8,128)(2,1)}, bf16[32,64,256]{2,1,0:T(8,128)(2,1)}, u32[]{:S(2)}, u32[]{:S(2)}) collective-permute-start(bf16[32,64,256]{2,1,0:T(8,128)(2,1)} %get-tuple-element.32), channel_id=1, source_target_pairs={{0,4},{1,5},{2,6},{3,7},{4,0},{5,1},{6,2},{7,3},{8,12},{9,13},{10,... | collective-permute-start | bytes 3145736 | tf_op jit(solution)/shard_map/ppermute | solution.py:24
  17.9 3.1 %collective-permute-start.8 = (bf16[32,64,128]{2,1,0:T(8,128)(2,1)}, bf16[32,64,128]{2,1,0:T(8,128)(2,1)}, u32[]{:S(2)}, u32[]{:S(2)}) collective-permute-start(bf16[32,64,128]{2,1,0:T(8,128)(2,1)} %get-tuple-element.35), channel_id=1, source_target_pairs={{0,4},{1,5},{2,6},{3,7},{4,0},{5,1},{6,2},{7,3},{8,12},{9,13},{10,... | collective-permute-start | bytes 1572872 | tf_op jit(solution)/shard_map/ppermute | solution.py:24
  21.1 2.4 %two.4.refs_4_ = bf16[16,2,64,128]{3,2,1,0:T(8,128)(2,1)} custom-call(bf16[16,128,256]{2,1,0:T(8,128)(2,1)S(1)} %order.1.refs_0_, bf16[2,16,64,128]{3,2,1,0:T(8,128)(2,1)S(1)} %bitcast.17, bf16[2,16,64,128]{3,2,1,0:T(8,128)(2,1)} %bitcast.4.refs_2_), custom_call_target="tpu_custom_call" | custom-call | flops 99999997952 | bytes 370000000 | tf_op jit(solution)/shard_map/two/pallas_call | solution.py:51
  23.5 11.4 %all-to-all-start = ((bf16[16,2,64,128]{3,2,1,0:T(8,128)(2,1)}), bf16[16,2,64,128]{3,2,1,0:T(8,128)(2,1)}, u32[]{:S(2)}, u32[]{:S(2)}) async-start(bf16[16,2,64,128]{3,2,1,0:T(8,128)(2,1)} %two.4.refs_4_), calls=%async_computation | async-start | bytes 1048576 | tf_op jit(solution)/shard_map/all_to_all | solution.py:30
  34.9 2.3 %compose.1.refs_3_.refs_0_ = bf16[16,128,256]{2,1,0:T(8,128)(2,1)S(1)} custom-call(s32[3]{0:T(128)S(1)} %pad_add_fusion.refs_0_, bf16[32,64,256]{2,1,0:T(8,128)(2,1)S(1)} %copy-done.1, bf16[32,64,64]{2,1,0:T(8,128)(2,1)} %refs_2_.1, bf16[32,64,64]{2,1,0:T(8,128)(2,1)} %collective-permute-done.refs_3_, bf16[16,2,64,128]{3,2,1,0:T(8,128)(2,1)} %two.4.refs_4_), custom_call_target="tpu_custom_call" | custom-call | flops 99999997952 | bytes 370000000 | tf_op jit(solution)/shard_map/compose/pallas_call | solution.py:51
  37.3 2.6 %collective-permute-done.3 = bf16[32,64,256]{2,1,0:T(8,128)(2,1)} collective-permute-done((bf16[32,64,256]{2,1,0:T(8,128)(2,1)}, bf16[32,64,256]{2,1,0:T(8,128)(2,1)}, u32[]{:S(2)}, u32[]{:S(2)}) %collective-permute-start.3) | collective-permute-done | bytes 1048608 | tf_op jit(solution)/shard_map/ppermute | solution.py:24
  39.8 2.5 %two.5.refs_1_ = bf16[16,2,64,256]{3,2,1,0:T(8,128)(2,1)} custom-call(bf16[16,128,256]{2,1,0:T(8,128)(2,1)S(1)} %order.1.refs_0_, bf16[2,16,64,256]{3,2,1,0:T(8,128)(2,1)S(1)} %bitcast.16, bf16[2,16,64,256]{3,2,1,0:T(8,128)(2,1)} %bitcast.8.refs_2_, bf16[16,128,256]{2,1,0:T(8,128)(2,1)S(1)} %compose.1.refs_3_.refs_0_), custom_call_target="tpu_custom_call" | custom-call | flops 99999997952 | bytes 370000000 | tf_op jit(solution)/shard_map/two/pallas_call | solution.py:51
  43.4 9.0 %all-to-all-done.refs_0_ = bf16[16,2,64,128]{3,2,1,0:T(8,128)(2,1)} async-done(((bf16[16,2,64,128]{3,2,1,0:T(8,128)(2,1)}), bf16[16,2,64,128]{3,2,1,0:T(8,128)(2,1)}, u32[]{:S(2)}, u32[]{:S(2)}) %all-to-all-start) | async-done | bytes 524320 | tf_op jit(solution)/shard_map/all_to_all | solution.py:30
  52.3 4.3 %all-to-all-start.1 = ((bf16[16,2,64,256]{3,2,1,0:T(8,128)(2,1)}), bf16[16,2,64,256]{3,2,1,0:T(8,128)(2,1)}, u32[]{:S(2)}, u32[]{:S(2)}) async-start(bf16[16,2,64,256]{3,2,1,0:T(8,128)(2,1)} %two.5.refs_1_), calls=%async_computation.1 | async-start | bytes 2097152 | tf_op jit(solution)/shard_map/all_to_all | solution.py:30
  58.5 2.9 %collective-permute-start.5 = (bf16[16,64,128]{2,1,0:T(8,128)(2,1)}, bf16[16,64,128]{2,1,0:T(8,128)(2,1)}, u32[]{:S(2)}, u32[]{:S(2)}) collective-permute-start(bf16[16,64,128]{2,1,0:T(8,128)(2,1)} %get-tuple-element.31.refs_3_), channel_id=1, source_target_pairs={{0,128},{1,129},{2,130},{3,131},{4,132},{5,133},{6,134},{7,135},{8... | collective-permute-start | bytes 786440 | tf_op jit(solution)/shard_map/ppermute | solution.py:24
  62.3 2.2 %collective-permute-start.4 = (bf16[16,64,128]{2,1,0:T(8,128)(2,1)}, bf16[16,64,128]{2,1,0:T(8,128)(2,1)}, u32[]{:S(2)}, u32[]{:S(2)}) collective-permute-start(bf16[16,64,128]{2,1,0:T(8,128)(2,1)} %get-tuple-element.30.refs_1_), channel_id=1, source_target_pairs={{0,1},{1,0},{2,3},{3,2},{4,5},{5,4},{6,7},{7,6},{8,9},{9,8},{10,11... | collective-permute-start | bytes 786440 | tf_op jit(solution)/shard_map/ppermute | solution.py:24
  64.5 2.5 %two.6.refs_1_ = bf16[16,2,64,256]{3,2,1,0:T(8,128)(2,1)} custom-call(bf16[16,128,256]{2,1,0:T(8,128)(2,1)S(1)} %order.1.refs_0_, bf16[2,16,64,256]{3,2,1,0:T(8,128)(2,1)S(1)} %bitcast.15, bf16[2,16,64,256]{3,2,1,0:T(8,128)(2,1)} %bitcast.10.refs_2_, bf16[16,64,128]{2,1,0:T(8,128)(2,1)} %get-tuple-element.31.refs_3_), custom_call_target="tpu_custom_call" | custom-call | flops 99999997952 | bytes 370000000 | tf_op jit(solution)/shard_map/two/pallas_call | solution.py:51
  67.1 16.5 %all-to-all-done.1.refs_0_ = bf16[16,2,64,256]{3,2,1,0:T(8,128)(2,1)} async-done(((bf16[16,2,64,256]{3,2,1,0:T(8,128)(2,1)}), bf16[16,2,64,256]{3,2,1,0:T(8,128)(2,1)}, u32[]{:S(2)}, u32[]{:S(2)}) %all-to-all-start.1) | async-done | bytes 1048608 | tf_op jit(solution)/shard_map/all_to_all | solution.py:30
  83.5 4.2 %all-to-all-start.3 = ((bf16[16,2,64,256]{3,2,1,0:T(8,128)(2,1)}), bf16[16,2,64,256]{3,2,1,0:T(8,128)(2,1)}, u32[]{:S(2)}, u32[]{:S(2)}) async-start(bf16[16,2,64,256]{3,2,1,0:T(8,128)(2,1)} %two.6.refs_1_), calls=%async_computation.3 | async-start | bytes 2097152 | tf_op jit(solution)/shard_map/all_to_all | solution.py:30
  89.8 2.9 %collective-permute-start.13 = (bf16[16,64,256]{2,1,0:T(8,128)(2,1)}, bf16[16,64,256]{2,1,0:T(8,128)(2,1)}, u32[]{:S(2)}, u32[]{:S(2)}) collective-permute-start(bf16[16,64,256]{2,1,0:T(8,128)(2,1)} %get-tuple-element.33.refs_5_), channel_id=1, source_target_pairs={{0,128},{1,129},{2,130},{3,131},{4,132},{5,133},{6,134},{7,135},{8... | collective-permute-start | bytes 1572872 | tf_op jit(solution)/shard_map/ppermute | solution.py:24
  93.5 2.4 %three.5 = (bf16[2,16,64,1024]{3,2,1,0:T(8,128)(2,1)}, f32[8,128]{1,0:T(8,128)S(1)}) custom-call(bf16[16,128,256]{2,1,0:T(8,128)(2,1)S(1)} %copy-done.8, bf16[16,64,128]{2,1,0:T(8,128)(2,1)} %get-tuple-element.30.refs_1_, bf16[16,64,128]{2,1,0:T(8,128)(2,1)} %collective-permute-done.4.refs_2_, bf16[16,64,128]{2,1,0:T(8,128)(2,1)} %collective-permute-done.5.refs_3_, ...), custom_call_target="tpu_custom_call" | custom-call | flops 99999997952 | bytes 370000000 | tf_op jit(solution)/shard_map/three/pallas_call | solution.py:51
  96.0 2.5 %two.7.refs_3_ = bf16[16,2,64,256]{3,2,1,0:T(8,128)(2,1)} custom-call(bf16[16,128,256]{2,1,0:T(8,128)(2,1)S(1)} %order.1.refs_0_, bf16[2,16,64,256]{3,2,1,0:T(8,128)(2,1)S(1)} %bitcast.14, bf16[2,16,64,256]{3,2,1,0:T(8,128)(2,1)} %bitcast.6.refs_2_, f32[8,128]{1,0:T(8,128)S(1)} %get-tuple-element.34.refs_3_), custom_call_target="tpu_custom_call" | custom-call | flops 99999997952 | bytes 370000000 | tf_op jit(solution)/shard_map/two/pallas_call | solution.py:51
  99.8 2.3 %apart.1 = (bf16[16,64,128]{2,1,0:T(8,128)(2,1)S(1)}, bf16[16,64,128]{2,1,0:T(8,128)(2,1)}) custom-call(bf16[16,128,256]{2,1,0:T(8,128)(2,1)S(1)} %copy-done.12, bf16[2,16,64,128]{3,2,1,0:T(8,128)(2,1)} %bitcast.11.refs_1_, bf16[2,16,64,128]{3,2,1,0:T(8,128)(2,1)} %bitcast.12.refs_2_, bf16[16,2,64,256]{3,2,1,0:T(8,128)(2,1)} %two.7.refs_3_), custom_call_target="tpu_custom_call" | custom-call | flops 99999997952 | bytes 370000000 | tf_op jit(solution)/shard_map/apart/pallas_call | solution.py:51
  104.7 10.4 %all-to-all-done.3.refs_0_ = bf16[16,2,64,256]{3,2,1,0:T(8,128)(2,1)} async-done(((bf16[16,2,64,256]{3,2,1,0:T(8,128)(2,1)}), bf16[16,2,64,256]{3,2,1,0:T(8,128)(2,1)}, u32[]{:S(2)}, u32[]{:S(2)}) %all-to-all-start.3) | async-done | bytes 1048608 | tf_op jit(solution)/shard_map/all_to_all | solution.py:30
  115.1 4.2 %all-to-all-start.2 = ((bf16[16,2,64,256]{3,2,1,0:T(8,128)(2,1)}), bf16[16,2,64,256]{3,2,1,0:T(8,128)(2,1)}, u32[]{:S(2)}, u32[]{:S(2)}) async-start(bf16[16,2,64,256]{3,2,1,0:T(8,128)(2,1)} %two.7.refs_3_), calls=%async_computation.2 | async-start | bytes 2097152 | tf_op jit(solution)/shard_map/all_to_all | solution.py:30
  122.8 2.6 %collective-permute-start.19 = (bf16[16,64,256]{2,1,0:T(8,128)(2,1)}, bf16[16,64,256]{2,1,0:T(8,128)(2,1)}, u32[]{:S(2)}, u32[]{:S(2)}) collective-permute-start(bf16[16,64,256]{2,1,0:T(8,128)(2,1)} %get-tuple-element.40.refs_6_), channel_id=1, source_target_pairs={{0,128},{1,129},{2,130},{3,131},{4,132},{5,133},{6,134},{7,135},{8... | collective-permute-start | bytes 1572872 | tf_op jit(solution)/shard_map/ppermute | solution.py:24
  125.5 2.5 %three.6 = (bf16[2,16,64,1024]{3,2,1,0:T(8,128)(2,1)}, f32[8,128]{1,0:T(8,128)S(1)}) custom-call(bf16[16,128,256]{2,1,0:T(8,128)(2,1)S(1)} %copy-done.9, bf16[16,64,256]{2,1,0:T(8,128)(2,1)S(1)} %get-tuple-element.38.refs_1_, bf16[16,64,256]{2,1,0:T(8,128)(2,1)S(1)} %collective-permute-done.12.refs_2_, ...), custom_call_target="tpu_custom_call", output_to_operand_aliasing={{0}: (5, {})} | custom-call | flops 99999997952 | bytes 370000000 | tf_op jit(solution)/shard_map/three/pallas_call | solution.py:51
  130.0 16.6 %all-to-all-done.2.refs_0_ = bf16[16,2,64,256]{3,2,1,0:T(8,128)(2,1)} async-done(((bf16[16,2,64,256]{3,2,1,0:T(8,128)(2,1)}), bf16[16,2,64,256]{3,2,1,0:T(8,128)(2,1)}, u32[]{:S(2)}, u32[]{:S(2)}) %all-to-all-start.2) | async-done | bytes 1048608 | tf_op jit(solution)/shard_map/all_to_all | solution.py:30
  146.7 4.2 %all-to-all-start.4 = ((bf16[16,4,64,128]{3,2,1,0:T(8,128)(2,1)}), bf16[16,4,64,128]{3,2,1,0:T(8,128)(2,1)}, u32[]{:S(2)}, u32[]{:S(2)}) async-start(bf16[16,4,64,128]{3,2,1,0:T(8,128)(2,1)} %pack.1.refs_1_), calls=%async_computation.4 | async-start | bytes 2097152 | tf_op jit(solution)/shard_map/all_to_all | solution.py:30
  153.1 2.9 %collective-permute-start.16 = (bf16[16,64,256]{2,1,0:T(8,128)(2,1)}, bf16[16,64,256]{2,1,0:T(8,128)(2,1)}, u32[]{:S(2)}, u32[]{:S(2)}) collective-permute-start(bf16[16,64,256]{2,1,0:T(8,128)(2,1)} %get-tuple-element.43.refs_6_), channel_id=1, source_target_pairs={{0,128},{1,129},{2,130},{3,131},{4,132},{5,133},{6,134},{7,135},{8... | collective-permute-start | bytes 1572872 | tf_op jit(solution)/shard_map/ppermute | solution.py:24
  156.8 2.7 %three.7 = (bf16[2,16,64,1024]{3,2,1,0:T(8,128)(2,1)}, f32[8,128]{1,0:T(8,128)S(1)}) custom-call(bf16[16,128,256]{2,1,0:T(8,128)(2,1)S(1)} %copy-done.10, bf16[16,64,256]{2,1,0:T(8,128)(2,1)} %get-tuple-element.44.refs_1_, bf16[16,64,256]{2,1,0:T(8,128)(2,1)} %collective-permute-done.18.refs_2_, ...), custom_call_target="tpu_custom_call", output_to_operand_aliasing={{0}: (5, {})} | custom-call | flops 99999997952 | bytes 370000000 | tf_op jit(solution)/shard_map/three/pallas_call | solution.py:51
  159.5 18.7 %all-to-all-done.4.refs_1_ = bf16[16,4,64,128]{3,2,1,0:T(8,128)(2,1)} async-done(((bf16[16,4,64,128]{3,2,1,0:T(8,128)(2,1)}), bf16[16,4,64,128]{3,2,1,0:T(8,128)(2,1)}, u32[]{:S(2)}, u32[]{:S(2)}) %all-to-all-start.4) | async-done | bytes 1048608 | tf_op jit(solution)/shard_map/all_to_all | solution.py:30
  178.2 2.3 %three.8 = (bf16[2,16,64,1024]{3,2,1,0:T(8,128)(2,1)}, f32[8,128]{1,0:T(8,128)S(1)}) custom-call(bf16[16,128,256]{2,1,0:T(8,128)(2,1)S(1)} %copy-done.10, bf16[16,4,64,128]{3,2,1,0:T(8,128)(2,1)} %all-to-all-done.4.refs_1_, bf16[2,16,64,1024]{3,2,1,0:T(8,128)(2,1)} %get-tuple-element.46.refs_2_, ...), custom_call_target="tpu_custom_call", output_to_operand_aliasing={{0}: (2, {})} | custom-call | flops 99999997952 | bytes 370000000 | tf_op jit(solution)/shard_map/three/pallas_call | solution.py:51
  180.6 2.7 %three.9 = (bf16[2,16,64,1024]{3,2,1,0:T(8,128)(2,1)}, f32[8,128]{1,0:T(8,128)}) custom-call(bf16[16,128,256]{2,1,0:T(8,128)(2,1)S(1)} %copy-done.10, bf16[16,64,256]{2,1,0:T(8,128)(2,1)} %get-tuple-element.42.refs_1_, bf16[16,64,256]{2,1,0:T(8,128)(2,1)} %collective-permute-done.15.refs_2_, ...), custom_call_target="tpu_custom_call", output_to_operand_aliasing={{0}: (5, {})} | custom-call | flops 99999997952 | bytes 370000000 | tf_op jit(solution)/shard_map/three/pallas_call | solution.py:51
  (66 shorter events, 22.8 us)
Async XLA Ops:
  2.8 13.2 %copy-start = (bf16[32,64,256]{2,1,0:T(8,128)(2,1)S(1)}, bf16[32,64,256]{2,1,0:T(8,128)(2,1)}, u32[]{:S(2)}) copy-start(bf16[32,64,256]{2,1,0:T(8,128)(2,1)} %refs_1_.6) | copy-start | bytes 3145732
  2.8 15.1 %collective-permute-start.1 = (bf16[32,64,128]{2,1,0:T(8,128)(2,1)}, bf16[32,64,128]{2,1,0:T(8,128)(2,1)}, u32[]{:S(2)}, u32[]{:S(2)}) collective-permute-start(bf16[32,64,128]{2,1,0:T(8,128)(2,1)} %one.2.refs_2_), channel_id=1, source_target_pairs={{0,4},{1,5},{2,6},{3,7},{4,0},{5,1},{6,2},{7,3},{8,12},{9,13},{10,... | collective-permute-start | bytes 1572872 | tf_op jit(solution)/shard_map/ppermute | solution.py:24
  6.4 28.5 %collective-permute-start = (bf16[32,64,64]{2,1,0:T(8,128)(2,1)}, bf16[32,64,64]{2,1,0:T(8,128)(2,1)}, u32[]{:S(2)}, u32[]{:S(2)}) collective-permute-start(bf16[32,64,64]{2,1,0:T(8,128)(2,1)} %refs_2_.1), channel_id=1, source_target_pairs={{0,1},{1,0},{2,3},{3,2},{4,5},{5,4},{6,7},{7,6},{8,9},{9,8},{10,11... | collective-permute-start | bytes 786440 | tf_op jit(solution)/shard_map/ppermute | solution.py:24
  12.6 27.2 %collective-permute-start.3 = (bf16[32,64,256]{2,1,0:T(8,128)(2,1)}, bf16[32,64,256]{2,1,0:T(8,128)(2,1)}, u32[]{:S(2)}, u32[]{:S(2)}) collective-permute-start(bf16[32,64,256]{2,1,0:T(8,128)(2,1)} %get-tuple-element.28.refs_2_), channel_id=1, source_target_pairs={{0,4},{1,5},{2,6},{3,7},{4,0},{5,1},{6,2},{7,3},{8,12},{9,13},{10,... | collective-permute-start | bytes 3145736 | tf_op jit(solution)/shard_map/ppermute | solution.py:24
  12.9 49.4 %collective-permute-start.7 = (bf16[32,64,256]{2,1,0:T(8,128)(2,1)}, bf16[32,64,256]{2,1,0:T(8,128)(2,1)}, u32[]{:S(2)}, u32[]{:S(2)}) collective-permute-start(bf16[32,64,256]{2,1,0:T(8,128)(2,1)} %get-tuple-element.32), channel_id=1, source_target_pairs={{0,4},{1,5},{2,6},{3,7},{4,0},{5,1},{6,2},{7,3},{8,12},{9,13},{10,... | collective-permute-start | bytes 3145736 | tf_op jit(solution)/shard_map/ppermute | solution.py:24
  15.7 80.3 %collective-permute-start.2 = (bf16[32,64,256]{2,1,0:T(8,128)(2,1)}, bf16[32,64,256]{2,1,0:T(8,128)(2,1)}, u32[]{:S(2)}, u32[]{:S(2)}) collective-permute-start(bf16[32,64,256]{2,1,0:T(8,128)(2,1)} %get-tuple-element.29), channel_id=1, source_target_pairs={{0,4},{1,5},{2,6},{3,7},{4,0},{5,1},{6,2},{7,3},{8,12},{9,13},{10,... | collective-permute-start | bytes 3145736 | tf_op jit(solution)/shard_map/ppermute | solution.py:24
  17.9 78.1 %copy-start.11 = (bf16[16,128,256]{2,1,0:T(8,128)(2,1)}, bf16[16,128,256]{2,1,0:T(8,128)(2,1)S(1)}, u32[]{:S(2)}) copy-start(bf16[16,128,256]{2,1,0:T(8,128)(2,1)S(1)} %order.1.refs_0_) | copy-start | bytes 3145732
  17.9 80.6 %collective-permute-start.8 = (bf16[32,64,128]{2,1,0:T(8,128)(2,1)}, bf16[32,64,128]{2,1,0:T(8,128)(2,1)}, u32[]{:S(2)}, u32[]{:S(2)}) collective-permute-start(bf16[32,64,128]{2,1,0:T(8,128)(2,1)} %get-tuple-element.35), channel_id=1, source_target_pairs={{0,4},{1,5},{2,6},{3,7},{4,0},{5,1},{6,2},{7,3},{8,12},{9,13},{10,... | collective-permute-start | bytes 1572872 | tf_op jit(solution)/shard_map/ppermute | solution.py:24
  21.1 13.9 %copy-start.1 = (bf16[32,64,256]{2,1,0:T(8,128)(2,1)S(1)}, bf16[32,64,256]{2,1,0:T(8,128)(2,1)}, u32[]{:S(2)}) copy-start(bf16[32,64,256]{2,1,0:T(8,128)(2,1)} %refs_1_.7) | copy-start | bytes 3145732
  23.5 28.9 %all-to-all-start = ((bf16[16,2,64,128]{3,2,1,0:T(8,128)(2,1)}), bf16[16,2,64,128]{3,2,1,0:T(8,128)(2,1)}, u32[]{:S(2)}, u32[]{:S(2)}) async-start(bf16[16,2,64,128]{3,2,1,0:T(8,128)(2,1)} %two.4.refs_4_), calls=%async_computation | async-start | bytes 1048576 | tf_op jit(solution)/shard_map/all_to_all | solution.py:30
  52.3 31.2 %all-to-all-start.1 = ((bf16[16,2,64,256]{3,2,1,0:T(8,128)(2,1)}), bf16[16,2,64,256]{3,2,1,0:T(8,128)(2,1)}, u32[]{:S(2)}, u32[]{:S(2)}) async-start(bf16[16,2,64,256]{3,2,1,0:T(8,128)(2,1)} %two.5.refs_1_), calls=%async_computation.1 | async-start | bytes 2097152 | tf_op jit(solution)/shard_map/all_to_all | solution.py:30
  56.6 7.9 %copy-start.3 = (bf16[32,64,256]{2,1,0:T(8,128)(2,1)S(1)}, bf16[32,64,256]{2,1,0:T(8,128)(2,1)}, u32[]{:S(2)}) copy-start(bf16[32,64,256]{2,1,0:T(8,128)(2,1)} %get-tuple-element.32) | copy-start | bytes 3145732
  58.5 31.3 %collective-permute-start.5 = (bf16[16,64,128]{2,1,0:T(8,128)(2,1)}, bf16[16,64,128]{2,1,0:T(8,128)(2,1)}, u32[]{:S(2)}, u32[]{:S(2)}) collective-permute-start(bf16[16,64,128]{2,1,0:T(8,128)(2,1)} %get-tuple-element.31.refs_3_), channel_id=1, source_target_pairs={{0,128},{1,129},{2,130},{3,131},{4,132},{5,133},{6,134},{7,135},{8... | collective-permute-start | bytes 786440 | tf_op jit(solution)/shard_map/ppermute | solution.py:24
  61.4 31.3 %collective-permute-start.6 = (bf16[16,64,128]{2,1,0:T(8,128)(2,1)}, bf16[16,64,128]{2,1,0:T(8,128)(2,1)}, u32[]{:S(2)}, u32[]{:S(2)}) collective-permute-start(bf16[16,64,128]{2,1,0:T(8,128)(2,1)} %get-tuple-element.31.refs_3_), channel_id=1, source_target_pairs={{0,129},{1,128},{2,131},{3,130},{4,133},{5,132},{6,135},{7,134},{8... | collective-permute-start | bytes 786440 | tf_op jit(solution)/shard_map/ppermute | solution.py:24
  62.3 31.2 %collective-permute-start.4 = (bf16[16,64,128]{2,1,0:T(8,128)(2,1)}, bf16[16,64,128]{2,1,0:T(8,128)(2,1)}, u32[]{:S(2)}, u32[]{:S(2)}) collective-permute-start(bf16[16,64,128]{2,1,0:T(8,128)(2,1)} %get-tuple-element.30.refs_1_), channel_id=1, source_target_pairs={{0,1},{1,0},{2,3},{3,2},{4,5},{5,4},{6,7},{7,6},{8,9},{9,8},{10,11... | collective-permute-start | bytes 786440 | tf_op jit(solution)/shard_map/ppermute | solution.py:24
  83.5 31.6 %all-to-all-start.3 = ((bf16[16,2,64,256]{3,2,1,0:T(8,128)(2,1)}), bf16[16,2,64,256]{3,2,1,0:T(8,128)(2,1)}, u32[]{:S(2)}, u32[]{:S(2)}) async-start(bf16[16,2,64,256]{3,2,1,0:T(8,128)(2,1)} %two.6.refs_1_), calls=%async_computation.3 | async-start | bytes 2097152 | tf_op jit(solution)/shard_map/all_to_all | solution.py:30
  89.8 6.1 %copy-start.2 = (bf16[32,64,256]{2,1,0:T(8,128)(2,1)S(1)}, bf16[32,64,256]{2,1,0:T(8,128)(2,1)}, u32[]{:S(2)}) copy-start(bf16[32,64,256]{2,1,0:T(8,128)(2,1)} %get-tuple-element.29) | copy-start | bytes 3145732
  89.8 33.0 %collective-permute-start.13 = (bf16[16,64,256]{2,1,0:T(8,128)(2,1)}, bf16[16,64,256]{2,1,0:T(8,128)(2,1)}, u32[]{:S(2)}, u32[]{:S(2)}) collective-permute-start(bf16[16,64,256]{2,1,0:T(8,128)(2,1)} %get-tuple-element.33.refs_5_), channel_id=1, source_target_pairs={{0,128},{1,129},{2,130},{3,131},{4,132},{5,133},{6,134},{7,135},{8... | collective-permute-start | bytes 1572872 | tf_op jit(solution)/shard_map/ppermute | solution.py:24
  92.7 32.7 %collective-permute-start.14 = (bf16[16,64,256]{2,1,0:T(8,128)(2,1)}, bf16[16,64,256]{2,1,0:T(8,128)(2,1)}, u32[]{:S(2)}, u32[]{:S(2)}) collective-permute-start(bf16[16,64,256]{2,1,0:T(8,128)(2,1)} %get-tuple-element.33.refs_5_), channel_id=1, source_target_pairs={{0,129},{1,128},{2,131},{3,130},{4,133},{5,132},{6,135},{7,134},{8... | collective-permute-start | bytes 1572872 | tf_op jit(solution)/shard_map/ppermute | solution.py:24
  102.0 26.0 %collective-permute-start.10 = (bf16[16,64,128]{2,1,0:T(8,128)(2,1)}, bf16[16,64,128]{2,1,0:T(8,128)(2,1)}, u32[]{:S(2)}, u32[]{:S(2)}) collective-permute-start(bf16[16,64,128]{2,1,0:T(8,128)(2,1)} %get-tuple-element.37.refs_1_), channel_id=1, source_target_pairs={{0,128},{1,129},{2,130},{3,131},{4,132},{5,133},{6,134},{7,135},{8... | collective-permute-start | bytes 786440 | tf_op jit(solution)/shard_map/ppermute | solution.py:24
  103.5 24.6 %collective-permute-start.11 = (bf16[16,64,128]{2,1,0:T(8,128)(2,1)}, bf16[16,64,128]{2,1,0:T(8,128)(2,1)}, u32[]{:S(2)}, u32[]{:S(2)}) collective-permute-start(bf16[16,64,128]{2,1,0:T(8,128)(2,1)} %get-tuple-element.37.refs_1_), channel_id=1, source_target_pairs={{0,129},{1,128},{2,131},{3,130},{4,133},{5,132},{6,135},{7,134},{8... | collective-permute-start | bytes 786440 | tf_op jit(solution)/shard_map/ppermute | solution.py:24
  104.2 17.5 %collective-permute-start.12 = (bf16[16,64,256]{2,1,0:T(8,128)(2,1)S(1)}, bf16[16,64,256]{2,1,0:T(8,128)(2,1)S(1)}, u32[]{:S(2)}, u32[]{:S(2)}) collective-permute-start(bf16[16,64,256]{2,1,0:T(8,128)(2,1)S(1)} %get-tuple-element.38.refs_1_), channel_id=1, source_target_pairs={{0,1},{1,0},{2,3},{3,2},{4,5},{5,4},{6,7},{7,6},{8,9},{9,8},{10,11... | collective-permute-start | bytes 1572872 | tf_op jit(solution)/shard_map/ppermute | solution.py:24
  115.1 31.6 %all-to-all-start.2 = ((bf16[16,2,64,256]{3,2,1,0:T(8,128)(2,1)}), bf16[16,2,64,256]{3,2,1,0:T(8,128)(2,1)}, u32[]{:S(2)}, u32[]{:S(2)}) async-start(bf16[16,2,64,256]{3,2,1,0:T(8,128)(2,1)} %two.7.refs_3_), calls=%async_computation.2 | async-start | bytes 2097152 | tf_op jit(solution)/shard_map/all_to_all | solution.py:30
  119.3 6.2 %copy-start.9 = (bf16[16,128,256]{2,1,0:T(8,128)(2,1)S(1)}, bf16[16,128,256]{2,1,0:T(8,128)(2,1)}, u32[]{:S(2)}) copy-start(bf16[16,128,256]{2,1,0:T(8,128)(2,1)} %copy-done.7) | copy-start | bytes 3145732
  121.6 6.4 %collective-permute-start.9 = (bf16[16,64,128]{2,1,0:T(8,128)(2,1)S(1)}, bf16[16,64,128]{2,1,0:T(8,128)(2,1)S(1)}, u32[]{:S(2)}, u32[]{:S(2)}) collective-permute-start(bf16[16,64,128]{2,1,0:T(8,128)(2,1)S(1)} %get-tuple-element.36.refs_0_), channel_id=1, source_target_pairs={{0,1},{1,0},{2,3},{3,2},{4,5},{5,4},{6,7},{7,6},{8,9},{9,8},{10,11... | collective-permute-start | bytes 786440 | tf_op jit(solution)/shard_map/ppermute | solution.py:24
  122.8 34.0 %collective-permute-start.19 = (bf16[16,64,256]{2,1,0:T(8,128)(2,1)}, bf16[16,64,256]{2,1,0:T(8,128)(2,1)}, u32[]{:S(2)}, u32[]{:S(2)}) collective-permute-start(bf16[16,64,256]{2,1,0:T(8,128)(2,1)} %get-tuple-element.40.refs_6_), channel_id=1, source_target_pairs={{0,128},{1,129},{2,130},{3,131},{4,132},{5,133},{6,134},{7,135},{8... | collective-permute-start | bytes 1572872 | tf_op jit(solution)/shard_map/ppermute | solution.py:24
  125.4 31.4 %collective-permute-start.20 = (bf16[16,64,256]{2,1,0:T(8,128)(2,1)}, bf16[16,64,256]{2,1,0:T(8,128)(2,1)}, u32[]{:S(2)}, u32[]{:S(2)}) collective-permute-start(bf16[16,64,256]{2,1,0:T(8,128)(2,1)} %get-tuple-element.40.refs_6_), channel_id=1, source_target_pairs={{0,129},{1,128},{2,131},{3,130},{4,133},{5,132},{6,135},{7,134},{8... | collective-permute-start | bytes 1572872 | tf_op jit(solution)/shard_map/ppermute | solution.py:24
  128.0 28.8 %collective-permute-start.18 = (bf16[16,64,256]{2,1,0:T(8,128)(2,1)}, bf16[16,64,256]{2,1,0:T(8,128)(2,1)}, u32[]{:S(2)}, u32[]{:S(2)}) collective-permute-start(bf16[16,64,256]{2,1,0:T(8,128)(2,1)} %get-tuple-element.44.refs_1_), channel_id=1, source_target_pairs={{0,1},{1,0},{2,3},{3,2},{4,5},{5,4},{6,7},{7,6},{8,9},{9,8},{10,11... | collective-permute-start | bytes 1572872 | tf_op jit(solution)/shard_map/ppermute | solution.py:24
  146.7 31.6 %all-to-all-start.4 = ((bf16[16,4,64,128]{3,2,1,0:T(8,128)(2,1)}), bf16[16,4,64,128]{3,2,1,0:T(8,128)(2,1)}, u32[]{:S(2)}, u32[]{:S(2)}) async-start(bf16[16,4,64,128]{3,2,1,0:T(8,128)(2,1)} %pack.1.refs_1_), calls=%async_computation.4 | async-start | bytes 2097152 | tf_op jit(solution)/shard_map/all_to_all | solution.py:30
  153.1 27.5 %collective-permute-start.16 = (bf16[16,64,256]{2,1,0:T(8,128)(2,1)}, bf16[16,64,256]{2,1,0:T(8,128)(2,1)}, u32[]{:S(2)}, u32[]{:S(2)}) collective-permute-start(bf16[16,64,256]{2,1,0:T(8,128)(2,1)} %get-tuple-element.43.refs_6_), channel_id=1, source_target_pairs={{0,128},{1,129},{2,130},{3,131},{4,132},{5,133},{6,134},{7,135},{8... | collective-permute-start | bytes 1572872 | tf_op jit(solution)/shard_map/ppermute | solution.py:24
  156.0 24.6 %collective-permute-start.17 = (bf16[16,64,256]{2,1,0:T(8,128)(2,1)}, bf16[16,64,256]{2,1,0:T(8,128)(2,1)}, u32[]{:S(2)}, u32[]{:S(2)}) collective-permute-start(bf16[16,64,256]{2,1,0:T(8,128)(2,1)} %get-tuple-element.43.refs_6_), channel_id=1, source_target_pairs={{0,129},{1,128},{2,131},{3,130},{4,133},{5,132},{6,135},{7,134},{8... | collective-permute-start | bytes 1572872 | tf_op jit(solution)/shard_map/ppermute | solution.py:24
  156.8 23.8 %collective-permute-start.15 = (bf16[16,64,256]{2,1,0:T(8,128)(2,1)}, bf16[16,64,256]{2,1,0:T(8,128)(2,1)}, u32[]{:S(2)}, u32[]{:S(2)}) collective-permute-start(bf16[16,64,256]{2,1,0:T(8,128)(2,1)} %get-tuple-element.42.refs_1_), channel_id=1, source_target_pairs={{0,1},{1,0},{2,3},{3,2},{4,5},{5,4},{6,7},{7,6},{8,9},{9,8},{10,11... | collective-permute-start | bytes 1572872 | tf_op jit(solution)/shard_map/ppermute | solution.py:24
  (7 other events, 23.9 us)

commit v4 on v3

--- a/solution.py
+++ b/solution.py
@@ -158,6 +158,7 @@
         grid=(2,),
         out_specs=pl.BlockSpec((part, 2, rank, size), lambda i: (i, 0, 0, 0)),
         out_shape=jax.ShapeDtypeStruct((half, 2, rank, size), jnp.bfloat16),
+        vmem=WHOLE_VMEM,
         cost_estimate=pl.CostEstimate(flops=100000000000, bytes_accessed=370000000, transcendentals=0),
         name="two",
     )
@@ -381,7 +382,7 @@
 
     partner = exchanged(middle, 0, 1)
     one([0])
-    one(range(1, count))
+    one([1, 2, 3])
     weights_two = ordered_two(flags, level_two, last)
     last = (weights_two,)
     two(0)
@@ -390,6 +391,7 @@
     two(1)
     split(0)
     two(2)
+    one([4])
     split(1)
     three(0)
     two(3)

time: 184 us -> 184 us (level)
  waiting for transfers between devices: 74.1 us -> 65.7 us
  local copies, waits for them, and re-layouts: 3.48 us -> 7.17 us
  Pallas kernels: 45.8 us -> 48.9 us
    all_to_all x5, waiting for transfers between devices: 71.2 us -> 59 us  [spread(): lax.all_to_all(array, 'tr', split_axis=0, concat_axis=0, tiled=True, axis...]
    ppermute x21, waiting for transfers between devices: 2.9 us -> 6.7 us  [exchanged(): return lax.ppermute(array, AXES, pairs)]
    unnamed x26 -> x28, local copies, waits for them, and re-layouts: 3.48 us -> 7.17 us
    pallas_call x19 -> x20, Pallas kernels: 45.8 us -> 48.9 us  [ordered_call(): pl.pallas_call(body, in_specs=specs, input_output_aliases=aliases or {},...]
  transfers between devices with their start and end apart: 26 -> 26, of which waited for: 8 -> 9; matrix products, arithmetic and copies ran while one was open for 0% -> 0% of each run, Pallas kernels for 22% -> 24%
where the time goes in v4:
time: 184 us; the launch traced here: 183 us
  waiting for transfers between devices  65.7 us (36%)
  starting transfers between devices  60.5 us (33%)
  Pallas kernels  48.9 us (27%)
  local copies, waits for them, and re-layouts  7.17 us (4%)
    all_to_all x5, waiting for transfers between devices, spread(): lax.all_to_all(array, 'tr', split_axis=0, concat_axis=0, tiled=True, axis...  59 us
    pallas_call x20, Pallas kernels, ordered_call(): pl.pallas_call(body, in_specs=specs, input_output_aliases=aliases or {},...  48.9 us
    ppermute x21, starting transfers between devices, exchanged(): return lax.ppermute(array, AXES, pairs)  31.3 us
    all_to_all x5, starting transfers between devices, spread(): lax.all_to_all(array, 'tr', split_axis=0, concat_axis=0, tiled=True, axis...  29.2 us
    unnamed x28, local copies, waits for them, and re-layouts  7.17 us
    ppermute x21, waiting for transfers between devices, exchanged(): return lax.ppermute(array, AXES, pairs)  6.7 us
  transfers between devices with their start and end apart: 26, of which 9 were waited for; matrix products, arithmetic and copies ran while one was open for 0% of the time, Pallas kernels for 24%

profile of v4, /device:TPU:1, one launch (start us, length us, event | category | flops | bytes accessed | tf_op | source)
XLA Modules:
  0.0 182.6 jit_solution(7204931728191728486)
XLA Ops:
  0.0 2.7 %one.3.refs_2_ = bf16[32,64,128]{2,1,0:T(8,128)(2,1)} custom-call(bf16[8,256,256]{2,1,0:T(8,128)(2,1)} %refs_0_.5, bf16[32,64,1024]{2,1,0:T(8,128)(2,1)} %refs_1_.9), custom_call_target="tpu_custom_call" | custom-call | flops 99999997952 | bytes 370000000 | tf_op jit(solution)/shard_map/one/pallas_call | solution.py:51
  2.7 3.7 %collective-permute-start.1 = (bf16[32,64,128]{2,1,0:T(8,128)(2,1)}, bf16[32,64,128]{2,1,0:T(8,128)(2,1)}, u32[]{:S(2)}, u32[]{:S(2)}) collective-permute-start(bf16[32,64,128]{2,1,0:T(8,128)(2,1)} %one.3.refs_2_), channel_id=1, source_target_pairs={{0,4},{1,5},{2,6},{3,7},{4,0},{5,1},{6,2},{7,3},{8,12},{9,13},{10,... | collective-permute-start | bytes 1572872 | tf_op jit(solution)/shard_map/ppermute | solution.py:24
  7.7 4.4 %one.4 = (bf16[32,64,256]{2,1,0:T(8,128)(2,1)}, bf16[32,64,256]{2,1,0:T(8,128)(2,1)}, bf16[32,64,256]{2,1,0:T(8,128)(2,1)}) custom-call(bf16[8,256,256]{2,1,0:T(8,128)(2,1)} %refs_0_.5, bf16[32,64,1024]{2,1,0:T(8,128)(2,1)} %refs_1_.9, bf16[32,64,128]{2,1,0:T(8,128)(2,1)} %one.3.refs_2_), custom_call_target="tpu_custom_call" | custom-call | flops 99999997952 | bytes 370000000 | tf_op jit(solution)/shard_map/one/pallas_call | solution.py:51
  12.4 2.7 %collective-permute-start.7 = (bf16[32,64,256]{2,1,0:T(8,128)(2,1)}, bf16[32,64,256]{2,1,0:T(8,128)(2,1)}, u32[]{:S(2)}, u32[]{:S(2)}) collective-permute-start(bf16[32,64,256]{2,1,0:T(8,128)(2,1)} %get-tuple-element.31), channel_id=1, source_target_pairs={{0,4},{1,5},{2,6},{3,7},{4,0},{5,1},{6,2},{7,3},{8,12},{9,13},{10,... | collective-permute-start | bytes 3145736 | tf_op jit(solution)/shard_map/ppermute | solution.py:24
  18.4 2.6 %two.4.refs_4_ = bf16[16,2,64,128]{3,2,1,0:T(8,128)(2,1)} custom-call(bf16[16,128,256]{2,1,0:T(8,128)(2,1)} %copy-done.11, bf16[2,16,64,128]{3,2,1,0:T(8,128)(2,1)} %bitcast.18, bf16[2,16,64,128]{3,2,1,0:T(8,128)(2,1)} %bitcast.4.refs_2_), custom_call_target="tpu_custom_call" | custom-call | flops 99999997952 | bytes 370000000 | tf_op jit(solution)/shard_map/two/pallas_call | solution.py:51
  21.0 11.1 %all-to-all-start = ((bf16[16,2,64,128]{3,2,1,0:T(8,128)(2,1)}), bf16[16,2,64,128]{3,2,1,0:T(8,128)(2,1)}, u32[]{:S(2)}, u32[]{:S(2)}) async-start(bf16[16,2,64,128]{3,2,1,0:T(8,128)(2,1)} %two.4.refs_4_), calls=%async_computation | async-start | bytes 1048576 | tf_op jit(solution)/shard_map/all_to_all | solution.py:30
  33.1 2.2 %compose.1.refs_3_.refs_0_ = bf16[16,128,256]{2,1,0:T(8,128)(2,1)S(1)} custom-call(s32[3]{0:T(128)S(1)} %pad_add_fusion.refs_0_, bf16[32,64,256]{2,1,0:T(8,128)(2,1)S(1)} %copy-done.3, bf16[32,64,64]{2,1,0:T(8,128)(2,1)} %refs_2_.1, bf16[32,64,64]{2,1,0:T(8,128)(2,1)} %collective-permute-done.refs_3_, bf16[16,2,64,128]{3,2,1,0:T(8,128)(2,1)S(1)} %copy-done.1), custom_call_target="tpu_custom_call" | custom-call | flops 99999997952 | bytes 370000000 | tf_op jit(solution)/shard_map/compose/pallas_call | solution.py:51
  36.4 3.4 %collective-permute-done.3 = bf16[32,64,256]{2,1,0:T(8,128)(2,1)} collective-permute-done((bf16[32,64,256]{2,1,0:T(8,128)(2,1)}, bf16[32,64,256]{2,1,0:T(8,128)(2,1)}, u32[]{:S(2)}, u32[]{:S(2)}) %collective-permute-start.3) | collective-permute-done | bytes 1048608 | tf_op jit(solution)/shard_map/ppermute | solution.py:24
  39.8 2.9 %two.5.refs_1_ = bf16[16,2,64,256]{3,2,1,0:T(8,128)(2,1)} custom-call(bf16[16,128,256]{2,1,0:T(8,128)(2,1)} %copy-done.11, bf16[2,16,64,256]{3,2,1,0:T(8,128)(2,1)} %bitcast.14, bf16[2,16,64,256]{3,2,1,0:T(8,128)(2,1)} %bitcast.8.refs_2_, bf16[16,128,256]{2,1,0:T(8,128)(2,1)} %copy-done.7), custom_call_target="tpu_custom_call" | custom-call | flops 99999997952 | bytes 370000000 | tf_op jit(solution)/shard_map/two/pallas_call | solution.py:51
  42.7 6.7 %all-to-all-done.refs_0_ = bf16[16,2,64,128]{3,2,1,0:T(8,128)(2,1)} async-done(((bf16[16,2,64,128]{3,2,1,0:T(8,128)(2,1)}), bf16[16,2,64,128]{3,2,1,0:T(8,128)(2,1)}, u32[]{:S(2)}, u32[]{:S(2)}) %all-to-all-start) | async-done | bytes 524320 | tf_op jit(solution)/shard_map/all_to_all | solution.py:30
  49.5 5.4 %all-to-all-start.1 = ((bf16[16,2,64,256]{3,2,1,0:T(8,128)(2,1)}), bf16[16,2,64,256]{3,2,1,0:T(8,128)(2,1)}, u32[]{:S(2)}, u32[]{:S(2)}) async-start(bf16[16,2,64,256]{3,2,1,0:T(8,128)(2,1)} %two.5.refs_1_), calls=%async_computation.1 | async-start | bytes 2097152 | tf_op jit(solution)/shard_map/all_to_all | solution.py:30
  57.8 2.9 %collective-permute-start.5 = (bf16[16,64,128]{2,1,0:T(8,128)(2,1)}, bf16[16,64,128]{2,1,0:T(8,128)(2,1)}, u32[]{:S(2)}, u32[]{:S(2)}) collective-permute-start(bf16[16,64,128]{2,1,0:T(8,128)(2,1)} %get-tuple-element.30.refs_3_), channel_id=1, source_target_pairs={{0,128},{1,129},{2,130},{3,131},{4,132},{5,133},{6,134},{7,135},{8... | collective-permute-start | bytes 786440 | tf_op jit(solution)/shard_map/ppermute | solution.py:24
  62.3 2.9 %two.6.refs_2_ = bf16[16,2,64,256]{3,2,1,0:T(8,128)(2,1)} custom-call(bf16[16,128,256]{2,1,0:T(8,128)(2,1)} %copy-done.11, bf16[2,16,64,256]{3,2,1,0:T(8,128)(2,1)} %bitcast.17, bf16[2,16,64,256]{3,2,1,0:T(8,128)(2,1)} %bitcast.10.refs_2_, bf16[16,64,128]{2,1,0:T(8,128)(2,1)} %get-tuple-element.30.refs_3_), custom_call_target="tpu_custom_call" | custom-call | flops 99999997952 | bytes 370000000 | tf_op jit(solution)/shard_map/two/pallas_call | solution.py:51
  65.2 2.7 %one.5.refs_1_ = bf16[32,64,128]{2,1,0:T(8,128)(2,1)} custom-call(bf16[8,256,256]{2,1,0:T(8,128)(2,1)} %refs_0_.5, bf16[32,64,1024]{2,1,0:T(8,128)(2,1)} %refs_1_.9, bf16[16,2,64,256]{3,2,1,0:T(8,128)(2,1)} %two.6.refs_2_), custom_call_target="tpu_custom_call" | custom-call | flops 99999997952 | bytes 370000000 | tf_op jit(solution)/shard_map/one/pallas_call | solution.py:51
  67.9 2.5 %collective-permute-start.4 = (bf16[16,64,128]{2,1,0:T(8,128)(2,1)S(1)}, bf16[16,64,128]{2,1,0:T(8,128)(2,1)S(1)}, u32[]{:S(2)}, u32[]{:S(2)}) collective-permute-start(bf16[16,64,128]{2,1,0:T(8,128)(2,1)S(1)} %get-tuple-element.29.refs_1_), channel_id=1, source_target_pairs={{0,1},{1,0},{2,3},{3,2},{4,5},{5,4},{6,7},{7,6},{8,9},{9,8},{10,11... | collective-permute-start | bytes 786440 | tf_op jit(solution)/shard_map/ppermute | solution.py:24
  70.4 2.8 %collective-permute-start.8 = (bf16[32,64,128]{2,1,0:T(8,128)(2,1)}, bf16[32,64,128]{2,1,0:T(8,128)(2,1)}, u32[]{:S(2)}, u32[]{:S(2)}) collective-permute-start(bf16[32,64,128]{2,1,0:T(8,128)(2,1)} %one.5.refs_1_), channel_id=1, source_target_pairs={{0,4},{1,5},{2,6},{3,7},{4,0},{5,1},{6,2},{7,3},{8,12},{9,13},{10,... | collective-permute-start | bytes 1572872 | tf_op jit(solution)/shard_map/ppermute | solution.py:24
  73.2 9.7 %all-to-all-done.1.refs_0_ = bf16[16,2,64,256]{3,2,1,0:T(8,128)(2,1)} async-done(((bf16[16,2,64,256]{3,2,1,0:T(8,128)(2,1)}), bf16[16,2,64,256]{3,2,1,0:T(8,128)(2,1)}, u32[]{:S(2)}, u32[]{:S(2)}) %all-to-all-start.1) | async-done | bytes 1048608 | tf_op jit(solution)/shard_map/all_to_all | solution.py:30
  82.9 4.2 %all-to-all-start.3 = ((bf16[16,2,64,256]{3,2,1,0:T(8,128)(2,1)}), bf16[16,2,64,256]{3,2,1,0:T(8,128)(2,1)}, u32[]{:S(2)}, u32[]{:S(2)}) async-start(bf16[16,2,64,256]{3,2,1,0:T(8,128)(2,1)} %two.6.refs_2_), calls=%async_computation.3 | async-start | bytes 2097152 | tf_op jit(solution)/shard_map/all_to_all | solution.py:30
  90.2 2.9 %collective-permute-start.13 = (bf16[16,64,256]{2,1,0:T(8,128)(2,1)}, bf16[16,64,256]{2,1,0:T(8,128)(2,1)}, u32[]{:S(2)}, u32[]{:S(2)}) collective-permute-start(bf16[16,64,256]{2,1,0:T(8,128)(2,1)} %get-tuple-element.32.refs_5_), channel_id=1, source_target_pairs={{0,128},{1,129},{2,130},{3,131},{4,132},{5,133},{6,134},{7,135},{8... | collective-permute-start | bytes 1572872 | tf_op jit(solution)/shard_map/ppermute | solution.py:24
  93.9 2.3 %three.5 = (bf16[2,16,64,1024]{3,2,1,0:T(8,128)(2,1)}, f32[8,128]{1,0:T(8,128)S(1)}) custom-call(bf16[16,128,256]{2,1,0:T(8,128)(2,1)S(1)} %copy-done.8, bf16[16,64,128]{2,1,0:T(8,128)(2,1)S(1)} %get-tuple-element.29.refs_1_, bf16[16,64,128]{2,1,0:T(8,128)(2,1)S(1)} %collective-permute-done.4.refs_2_, bf16[16,64,128]{2,1,0:T(8,128)(2,1)} %collective-permute-done.5.refs_3_, ...), custom_call_target="tpu_custom_call" | custom-call | flops 99999997952 | bytes 370000000 | tf_op jit(solution)/shard_map/three/pallas_call | solution.py:51
  96.8 3.1 %two.7.refs_3_ = bf16[16,2,64,256]{3,2,1,0:T(8,128)(2,1)} custom-call(bf16[16,128,256]{2,1,0:T(8,128)(2,1)} %copy-done.11, bf16[2,16,64,256]{3,2,1,0:T(8,128)(2,1)} %bitcast.16, bf16[2,16,64,256]{3,2,1,0:T(8,128)(2,1)} %bitcast.6.refs_2_, f32[8,128]{1,0:T(8,128)} %copy-done.13), custom_call_target="tpu_custom_call" | custom-call | flops 99999997952 | bytes 370000000 | tf_op jit(solution)/shard_map/two/pallas_call | solution.py:51
  99.9 2.2 %apart.1 = (bf16[16,64,128]{2,1,0:T(8,128)(2,1)S(1)}, bf16[16,64,128]{2,1,0:T(8,128)(2,1)}) custom-call(bf16[16,128,256]{2,1,0:T(8,128)(2,1)S(1)} %copy-done.12, bf16[2,16,64,128]{3,2,1,0:T(8,128)(2,1)S(1)} %bitcast.15, bf16[2,16,64,128]{3,2,1,0:T(8,128)(2,1)} %bitcast.12.refs_2_, bf16[16,2,64,256]{3,2,1,0:T(8,128)(2,1)} %two.7.refs_3_), custom_call_target="tpu_custom_call" | custom-call | flops 99999997952 | bytes 370000000 | tf_op jit(solution)/shard_map/apart/pallas_call | solution.py:51
  104.7 9.7 %all-to-all-done.3.refs_0_ = bf16[16,2,64,256]{3,2,1,0:T(8,128)(2,1)} async-done(((bf16[16,2,64,256]{3,2,1,0:T(8,128)(2,1)}), bf16[16,2,64,256]{3,2,1,0:T(8,128)(2,1)}, u32[]{:S(2)}, u32[]{:S(2)}) %all-to-all-start.3) | async-done | bytes 1048608 | tf_op jit(solution)/shard_map/all_to_all | solution.py:30
  114.5 4.2 %all-to-all-start.2 = ((bf16[16,2,64,256]{3,2,1,0:T(8,128)(2,1)}), bf16[16,2,64,256]{3,2,1,0:T(8,128)(2,1)}, u32[]{:S(2)}, u32[]{:S(2)}) async-start(bf16[16,2,64,256]{3,2,1,0:T(8,128)(2,1)} %two.7.refs_3_), calls=%async_computation.2 | async-start | bytes 2097152 | tf_op jit(solution)/shard_map/all_to_all | solution.py:30
  126.6 2.5 %three.6 = (bf16[2,16,64,1024]{3,2,1,0:T(8,128)(2,1)}, f32[8,128]{1,0:T(8,128)S(1)}) custom-call(bf16[16,128,256]{2,1,0:T(8,128)(2,1)S(1)} %copy-done.9, bf16[16,64,256]{2,1,0:T(8,128)(2,1)S(1)} %get-tuple-element.36.refs_1_, bf16[16,64,256]{2,1,0:T(8,128)(2,1)S(1)} %collective-permute-done.12.refs_2_, ...), custom_call_target="tpu_custom_call", output_to_operand_aliasing={{0}: (5, {})} | custom-call | flops 99999997952 | bytes 370000000 | tf_op jit(solution)/shard_map/three/pallas_call | solution.py:51
  132.0 14.1 %all-to-all-done.2.refs_0_ = bf16[16,2,64,256]{3,2,1,0:T(8,128)(2,1)} async-done(((bf16[16,2,64,256]{3,2,1,0:T(8,128)(2,1)}), bf16[16,2,64,256]{3,2,1,0:T(8,128)(2,1)}, u32[]{:S(2)}, u32[]{:S(2)}) %all-to-all-start.2) | async-done | bytes 1048608 | tf_op jit(solution)/shard_map/all_to_all | solution.py:30
  146.0 4.2 %all-to-all-start.4 = ((bf16[16,4,64,128]{3,2,1,0:T(8,128)(2,1)}), bf16[16,4,64,128]{3,2,1,0:T(8,128)(2,1)}, u32[]{:S(2)}, u32[]{:S(2)}) async-start(bf16[16,4,64,128]{3,2,1,0:T(8,128)(2,1)} %pack.1.refs_1_), calls=%async_computation.4 | async-start | bytes 2097152 | tf_op jit(solution)/shard_map/all_to_all | solution.py:30
  152.4 2.9 %collective-permute-start.16 = (bf16[16,64,256]{2,1,0:T(8,128)(2,1)}, bf16[16,64,256]{2,1,0:T(8,128)(2,1)}, u32[]{:S(2)}, u32[]{:S(2)}) collective-permute-start(bf16[16,64,256]{2,1,0:T(8,128)(2,1)} %get-tuple-element.41.refs_6_), channel_id=1, source_target_pairs={{0,128},{1,129},{2,130},{3,131},{4,132},{5,133},{6,134},{7,135},{8... | collective-permute-start | bytes 1572872 | tf_op jit(solution)/shard_map/ppermute | solution.py:24
  156.2 2.7 %three.7 = (bf16[2,16,64,1024]{3,2,1,0:T(8,128)(2,1)}, f32[8,128]{1,0:T(8,128)S(1)}) custom-call(bf16[16,128,256]{2,1,0:T(8,128)(2,1)S(1)} %copy-done.10, bf16[16,64,256]{2,1,0:T(8,128)(2,1)} %get-tuple-element.42.refs_1_, bf16[16,64,256]{2,1,0:T(8,128)(2,1)} %collective-permute-done.18.refs_2_, ...), custom_call_target="tpu_custom_call", output_to_operand_aliasing={{0}: (5, {})} | custom-call | flops 99999997952 | bytes 370000000 | tf_op jit(solution)/shard_map/three/pallas_call | solution.py:51
  158.8 18.8 %all-to-all-done.4.refs_1_ = bf16[16,4,64,128]{3,2,1,0:T(8,128)(2,1)} async-done(((bf16[16,4,64,128]{3,2,1,0:T(8,128)(2,1)}), bf16[16,4,64,128]{3,2,1,0:T(8,128)(2,1)}, u32[]{:S(2)}, u32[]{:S(2)}) %all-to-all-start.4) | async-done | bytes 1048608 | tf_op jit(solution)/shard_map/all_to_all | solution.py:30
  177.6 2.3 %three.8 = (bf16[2,16,64,1024]{3,2,1,0:T(8,128)(2,1)}, f32[8,128]{1,0:T(8,128)S(1)}) custom-call(bf16[16,128,256]{2,1,0:T(8,128)(2,1)S(1)} %copy-done.10, bf16[16,4,64,128]{3,2,1,0:T(8,128)(2,1)} %all-to-all-done.4.refs_1_, bf16[2,16,64,1024]{3,2,1,0:T(8,128)(2,1)} %get-tuple-element.44.refs_2_, ...), custom_call_target="tpu_custom_call", output_to_operand_aliasing={{0}: (2, {})} | custom-call | flops 99999997952 | bytes 370000000 | tf_op jit(solution)/shard_map/three/pallas_call | solution.py:51
  179.9 2.7 %three.9 = (bf16[2,16,64,1024]{3,2,1,0:T(8,128)(2,1)}, f32[8,128]{1,0:T(8,128)}) custom-call(bf16[16,128,256]{2,1,0:T(8,128)(2,1)S(1)} %copy-done.10, bf16[16,64,256]{2,1,0:T(8,128)(2,1)} %get-tuple-element.40.refs_1_, bf16[16,64,256]{2,1,0:T(8,128)(2,1)} %collective-permute-done.15.refs_2_, ...), custom_call_target="tpu_custom_call", output_to_operand_aliasing={{0}: (5, {})} | custom-call | flops 99999997952 | bytes 370000000 | tf_op jit(solution)/shard_map/three/pallas_call | solution.py:51
  (69 shorter events, 32.1 us)
Async XLA Ops:
  2.7 12.7 %copy-start.2 = (bf16[32,64,256]{2,1,0:T(8,128)(2,1)S(1)}, bf16[32,64,256]{2,1,0:T(8,128)(2,1)}, u32[]{:S(2)}) copy-start(bf16[32,64,256]{2,1,0:T(8,128)(2,1)} %refs_1_.7) | copy-start | bytes 3145732
  2.7 15.6 %collective-permute-start.1 = (bf16[32,64,128]{2,1,0:T(8,128)(2,1)}, bf16[32,64,128]{2,1,0:T(8,128)(2,1)}, u32[]{:S(2)}, u32[]{:S(2)}) collective-permute-start(bf16[32,64,128]{2,1,0:T(8,128)(2,1)} %one.3.refs_2_), channel_id=1, source_target_pairs={{0,4},{1,5},{2,6},{3,7},{4,0},{5,1},{6,2},{7,3},{8,12},{9,13},{10,... | collective-permute-start | bytes 1572872 | tf_op jit(solution)/shard_map/ppermute | solution.py:24
  6.4 25.6 %collective-permute-start = (bf16[32,64,64]{2,1,0:T(8,128)(2,1)}, bf16[32,64,64]{2,1,0:T(8,128)(2,1)}, u32[]{:S(2)}, u32[]{:S(2)}) collective-permute-start(bf16[32,64,64]{2,1,0:T(8,128)(2,1)} %refs_2_.1), channel_id=1, source_target_pairs={{0,1},{1,0},{2,3},{3,2},{4,5},{5,4},{6,7},{7,6},{8,9},{9,8},{10,11... | collective-permute-start | bytes 786440 | tf_op jit(solution)/shard_map/ppermute | solution.py:24
  12.1 27.7 %collective-permute-start.3 = (bf16[32,64,256]{2,1,0:T(8,128)(2,1)}, bf16[32,64,256]{2,1,0:T(8,128)(2,1)}, u32[]{:S(2)}, u32[]{:S(2)}) collective-permute-start(bf16[32,64,256]{2,1,0:T(8,128)(2,1)} %get-tuple-element.27.refs_2_), channel_id=1, source_target_pairs={{0,4},{1,5},{2,6},{3,7},{4,0},{5,1},{6,2},{7,3},{8,12},{9,13},{10,... | collective-permute-start | bytes 3145736 | tf_op jit(solution)/shard_map/ppermute | solution.py:24
  12.4 49.9 %collective-permute-start.7 = (bf16[32,64,256]{2,1,0:T(8,128)(2,1)}, bf16[32,64,256]{2,1,0:T(8,128)(2,1)}, u32[]{:S(2)}, u32[]{:S(2)}) collective-permute-start(bf16[32,64,256]{2,1,0:T(8,128)(2,1)} %get-tuple-element.31), channel_id=1, source_target_pairs={{0,4},{1,5},{2,6},{3,7},{4,0},{5,1},{6,2},{7,3},{8,12},{9,13},{10,... | collective-permute-start | bytes 3145736 | tf_op jit(solution)/shard_map/ppermute | solution.py:24
  15.1 81.6 %collective-permute-start.2 = (bf16[32,64,256]{2,1,0:T(8,128)(2,1)}, bf16[32,64,256]{2,1,0:T(8,128)(2,1)}, u32[]{:S(2)}, u32[]{:S(2)}) collective-permute-start(bf16[32,64,256]{2,1,0:T(8,128)(2,1)} %get-tuple-element.28), channel_id=1, source_target_pairs={{0,4},{1,5},{2,6},{3,7},{4,0},{5,1},{6,2},{7,3},{8,12},{9,13},{10,... | collective-permute-start | bytes 3145736 | tf_op jit(solution)/shard_map/ppermute | solution.py:24
  18.3 13.7 %copy-start.3 = (bf16[32,64,256]{2,1,0:T(8,128)(2,1)S(1)}, bf16[32,64,256]{2,1,0:T(8,128)(2,1)}, u32[]{:S(2)}) copy-start(bf16[32,64,256]{2,1,0:T(8,128)(2,1)} %refs_1_.8) | copy-start | bytes 3145732
  21.0 28.5 %all-to-all-start = ((bf16[16,2,64,128]{3,2,1,0:T(8,128)(2,1)}), bf16[16,2,64,128]{3,2,1,0:T(8,128)(2,1)}, u32[]{:S(2)}, u32[]{:S(2)}) async-start(bf16[16,2,64,128]{3,2,1,0:T(8,128)(2,1)} %two.4.refs_4_), calls=%async_computation | async-start | bytes 1048576 | tf_op jit(solution)/shard_map/all_to_all | solution.py:30
  49.5 33.4 %all-to-all-start.1 = ((bf16[16,2,64,256]{3,2,1,0:T(8,128)(2,1)}), bf16[16,2,64,256]{3,2,1,0:T(8,128)(2,1)}, u32[]{:S(2)}, u32[]{:S(2)}) async-start(bf16[16,2,64,256]{3,2,1,0:T(8,128)(2,1)} %two.5.refs_1_), calls=%async_computation.1 | async-start | bytes 2097152 | tf_op jit(solution)/shard_map/all_to_all | solution.py:30
  57.8 32.4 %collective-permute-start.5 = (bf16[16,64,128]{2,1,0:T(8,128)(2,1)}, bf16[16,64,128]{2,1,0:T(8,128)(2,1)}, u32[]{:S(2)}, u32[]{:S(2)}) collective-permute-start(bf16[16,64,128]{2,1,0:T(8,128)(2,1)} %get-tuple-element.30.refs_3_), channel_id=1, source_target_pairs={{0,128},{1,129},{2,130},{3,131},{4,132},{5,133},{6,134},{7,135},{8... | collective-permute-start | bytes 786440 | tf_op jit(solution)/shard_map/ppermute | solution.py:24
  60.7 32.4 %collective-permute-start.6 = (bf16[16,64,128]{2,1,0:T(8,128)(2,1)}, bf16[16,64,128]{2,1,0:T(8,128)(2,1)}, u32[]{:S(2)}, u32[]{:S(2)}) collective-permute-start(bf16[16,64,128]{2,1,0:T(8,128)(2,1)} %get-tuple-element.30.refs_3_), channel_id=1, source_target_pairs={{0,129},{1,128},{2,131},{3,130},{4,133},{5,132},{6,135},{7,134},{8... | collective-permute-start | bytes 786440 | tf_op jit(solution)/shard_map/ppermute | solution.py:24
  67.9 26.0 %collective-permute-start.4 = (bf16[16,64,128]{2,1,0:T(8,128)(2,1)S(1)}, bf16[16,64,128]{2,1,0:T(8,128)(2,1)S(1)}, u32[]{:S(2)}, u32[]{:S(2)}) collective-permute-start(bf16[16,64,128]{2,1,0:T(8,128)(2,1)S(1)} %get-tuple-element.29.refs_1_), channel_id=1, source_target_pairs={{0,1},{1,0},{2,3},{3,2},{4,5},{5,4},{6,7},{7,6},{8,9},{9,8},{10,11... | collective-permute-start | bytes 786440 | tf_op jit(solution)/shard_map/ppermute | solution.py:24
  70.4 29.4 %collective-permute-start.8 = (bf16[32,64,128]{2,1,0:T(8,128)(2,1)}, bf16[32,64,128]{2,1,0:T(8,128)(2,1)}, u32[]{:S(2)}, u32[]{:S(2)}) collective-permute-start(bf16[32,64,128]{2,1,0:T(8,128)(2,1)} %one.5.refs_1_), channel_id=1, source_target_pairs={{0,4},{1,5},{2,6},{3,7},{4,0},{5,1},{6,2},{7,3},{8,12},{9,13},{10,... | collective-permute-start | bytes 1572872 | tf_op jit(solution)/shard_map/ppermute | solution.py:24
  82.9 31.6 %all-to-all-start.3 = ((bf16[16,2,64,256]{3,2,1,0:T(8,128)(2,1)}), bf16[16,2,64,256]{3,2,1,0:T(8,128)(2,1)}, u32[]{:S(2)}, u32[]{:S(2)}) async-start(bf16[16,2,64,256]{3,2,1,0:T(8,128)(2,1)} %two.6.refs_2_), calls=%async_computation.3 | async-start | bytes 2097152 | tf_op jit(solution)/shard_map/all_to_all | solution.py:30
  88.2 5.7 %copy-start.8 = (bf16[16,128,256]{2,1,0:T(8,128)(2,1)S(1)}, bf16[16,128,256]{2,1,0:T(8,128)(2,1)}, u32[]{:S(2)}) copy-start(bf16[16,128,256]{2,1,0:T(8,128)(2,1)} %copy-done.7) | copy-start | bytes 3145732
  90.2 34.0 %collective-permute-start.13 = (bf16[16,64,256]{2,1,0:T(8,128)(2,1)}, bf16[16,64,256]{2,1,0:T(8,128)(2,1)}, u32[]{:S(2)}, u32[]{:S(2)}) collective-permute-start(bf16[16,64,256]{2,1,0:T(8,128)(2,1)} %get-tuple-element.32.refs_5_), channel_id=1, source_target_pairs={{0,128},{1,129},{2,130},{3,131},{4,132},{5,133},{6,134},{7,135},{8... | collective-permute-start | bytes 1572872 | tf_op jit(solution)/shard_map/ppermute | solution.py:24
  93.1 31.7 %collective-permute-start.14 = (bf16[16,64,256]{2,1,0:T(8,128)(2,1)}, bf16[16,64,256]{2,1,0:T(8,128)(2,1)}, u32[]{:S(2)}, u32[]{:S(2)}) collective-permute-start(bf16[16,64,256]{2,1,0:T(8,128)(2,1)} %get-tuple-element.32.refs_5_), channel_id=1, source_target_pairs={{0,129},{1,128},{2,131},{3,130},{4,133},{5,132},{6,135},{7,134},{8... | collective-permute-start | bytes 1572872 | tf_op jit(solution)/shard_map/ppermute | solution.py:24
  96.8 3.1 %copy-start.12 = (bf16[16,128,256]{2,1,0:T(8,128)(2,1)S(1)}, bf16[16,128,256]{2,1,0:T(8,128)(2,1)}, u32[]{:S(2)}) copy-start(bf16[16,128,256]{2,1,0:T(8,128)(2,1)} %copy-done.11) | copy-start | bytes 3145732
  102.1 27.0 %collective-permute-start.10 = (bf16[16,64,128]{2,1,0:T(8,128)(2,1)}, bf16[16,64,128]{2,1,0:T(8,128)(2,1)}, u32[]{:S(2)}, u32[]{:S(2)}) collective-permute-start(bf16[16,64,128]{2,1,0:T(8,128)(2,1)} %get-tuple-element.35.refs_1_), channel_id=1, source_target_pairs={{0,128},{1,129},{2,130},{3,131},{4,132},{5,133},{6,134},{7,135},{8... | collective-permute-start | bytes 786440 | tf_op jit(solution)/shard_map/ppermute | solution.py:24
  103.5 25.8 %collective-permute-start.11 = (bf16[16,64,128]{2,1,0:T(8,128)(2,1)}, bf16[16,64,128]{2,1,0:T(8,128)(2,1)}, u32[]{:S(2)}, u32[]{:S(2)}) collective-permute-start(bf16[16,64,128]{2,1,0:T(8,128)(2,1)} %get-tuple-element.35.refs_1_), channel_id=1, source_target_pairs={{0,129},{1,128},{2,131},{3,130},{4,133},{5,132},{6,135},{7,134},{8... | collective-permute-start | bytes 786440 | tf_op jit(solution)/shard_map/ppermute | solution.py:24
  104.1 18.6 %collective-permute-start.12 = (bf16[16,64,256]{2,1,0:T(8,128)(2,1)S(1)}, bf16[16,64,256]{2,1,0:T(8,128)(2,1)S(1)}, u32[]{:S(2)}, u32[]{:S(2)}) collective-permute-start(bf16[16,64,256]{2,1,0:T(8,128)(2,1)S(1)} %get-tuple-element.36.refs_1_), channel_id=1, source_target_pairs={{0,1},{1,0},{2,3},{3,2},{4,5},{5,4},{6,7},{7,6},{8,9},{9,8},{10,11... | collective-permute-start | bytes 1572872 | tf_op jit(solution)/shard_map/ppermute | solution.py:24
  114.5 31.6 %all-to-all-start.2 = ((bf16[16,2,64,256]{3,2,1,0:T(8,128)(2,1)}), bf16[16,2,64,256]{3,2,1,0:T(8,128)(2,1)}, u32[]{:S(2)}, u32[]{:S(2)}) async-start(bf16[16,2,64,256]{3,2,1,0:T(8,128)(2,1)} %two.7.refs_3_), calls=%async_computation.2 | async-start | bytes 2097152 | tf_op jit(solution)/shard_map/all_to_all | solution.py:30
  118.7 7.9 %copy-start.9 = (bf16[16,128,256]{2,1,0:T(8,128)(2,1)S(1)}, bf16[16,128,256]{2,1,0:T(8,128)(2,1)}, u32[]{:S(2)}) copy-start(bf16[16,128,256]{2,1,0:T(8,128)(2,1)} %copy-done.7) | copy-start | bytes 3145732
  122.7 7.3 %collective-permute-start.9 = (bf16[16,64,128]{2,1,0:T(8,128)(2,1)S(1)}, bf16[16,64,128]{2,1,0:T(8,128)(2,1)S(1)}, u32[]{:S(2)}, u32[]{:S(2)}) collective-permute-start(bf16[16,64,128]{2,1,0:T(8,128)(2,1)S(1)} %get-tuple-element.34.refs_0_), channel_id=1, source_target_pairs={{0,1},{1,0},{2,3},{3,2},{4,5},{5,4},{6,7},{7,6},{8,9},{9,8},{10,11... | collective-permute-start | bytes 786440 | tf_op jit(solution)/shard_map/ppermute | solution.py:24
  124.2 32.0 %collective-permute-start.19 = (bf16[16,64,256]{2,1,0:T(8,128)(2,1)}, bf16[16,64,256]{2,1,0:T(8,128)(2,1)}, u32[]{:S(2)}, u32[]{:S(2)}) collective-permute-start(bf16[16,64,256]{2,1,0:T(8,128)(2,1)} %get-tuple-element.38.refs_6_), channel_id=1, source_target_pairs={{0,128},{1,129},{2,130},{3,131},{4,132},{5,133},{6,134},{7,135},{8... | collective-permute-start | bytes 1572872 | tf_op jit(solution)/shard_map/ppermute | solution.py:24
  124.8 31.4 %collective-permute-start.20 = (bf16[16,64,256]{2,1,0:T(8,128)(2,1)}, bf16[16,64,256]{2,1,0:T(8,128)(2,1)}, u32[]{:S(2)}, u32[]{:S(2)}) collective-permute-start(bf16[16,64,256]{2,1,0:T(8,128)(2,1)} %get-tuple-element.38.refs_6_), channel_id=1, source_target_pairs={{0,129},{1,128},{2,131},{3,130},{4,133},{5,132},{6,135},{7,134},{8... | collective-permute-start | bytes 1572872 | tf_op jit(solution)/shard_map/ppermute | solution.py:24
  129.1 27.1 %collective-permute-start.18 = (bf16[16,64,256]{2,1,0:T(8,128)(2,1)}, bf16[16,64,256]{2,1,0:T(8,128)(2,1)}, u32[]{:S(2)}, u32[]{:S(2)}) collective-permute-start(bf16[16,64,256]{2,1,0:T(8,128)(2,1)} %get-tuple-element.42.refs_1_), channel_id=1, source_target_pairs={{0,1},{1,0},{2,3},{3,2},{4,5},{5,4},{6,7},{7,6},{8,9},{9,8},{10,11... | collective-permute-start | bytes 1572872 | tf_op jit(solution)/shard_map/ppermute | solution.py:24
  146.0 31.6 %all-to-all-start.4 = ((bf16[16,4,64,128]{3,2,1,0:T(8,128)(2,1)}), bf16[16,4,64,128]{3,2,1,0:T(8,128)(2,1)}, u32[]{:S(2)}, u32[]{:S(2)}) async-start(bf16[16,4,64,128]{3,2,1,0:T(8,128)(2,1)} %pack.1.refs_1_), calls=%async_computation.4 | async-start | bytes 2097152 | tf_op jit(solution)/shard_map/all_to_all | solution.py:30
  150.3 5.9 %copy-start.10 = (bf16[16,128,256]{2,1,0:T(8,128)(2,1)S(1)}, bf16[16,128,256]{2,1,0:T(8,128)(2,1)}, u32[]{:S(2)}) copy-start(bf16[16,128,256]{2,1,0:T(8,128)(2,1)} %copy-done.7) | copy-start | bytes 3145732
  152.4 27.5 %collective-permute-start.16 = (bf16[16,64,256]{2,1,0:T(8,128)(2,1)}, bf16[16,64,256]{2,1,0:T(8,128)(2,1)}, u32[]{:S(2)}, u32[]{:S(2)}) collective-permute-start(bf16[16,64,256]{2,1,0:T(8,128)(2,1)} %get-tuple-element.41.refs_6_), channel_id=1, source_target_pairs={{0,128},{1,129},{2,130},{3,131},{4,132},{5,133},{6,134},{7,135},{8... | collective-permute-start | bytes 1572872 | tf_op jit(solution)/shard_map/ppermute | solution.py:24
  155.4 24.6 %collective-permute-start.17 = (bf16[16,64,256]{2,1,0:T(8,128)(2,1)}, bf16[16,64,256]{2,1,0:T(8,128)(2,1)}, u32[]{:S(2)}, u32[]{:S(2)}) collective-permute-start(bf16[16,64,256]{2,1,0:T(8,128)(2,1)} %get-tuple-element.41.refs_6_), channel_id=1, source_target_pairs={{0,129},{1,128},{2,131},{3,130},{4,133},{5,132},{6,135},{7,134},{8... | collective-permute-start | bytes 1572872 | tf_op jit(solution)/shard_map/ppermute | solution.py:24
  156.1 23.8 %collective-permute-start.15 = (bf16[16,64,256]{2,1,0:T(8,128)(2,1)}, bf16[16,64,256]{2,1,0:T(8,128)(2,1)}, u32[]{:S(2)}, u32[]{:S(2)}) collective-permute-start(bf16[16,64,256]{2,1,0:T(8,128)(2,1)} %get-tuple-element.40.refs_1_), channel_id=1, source_target_pairs={{0,1},{1,0},{2,3},{3,2},{4,5},{5,4},{6,7},{7,6},{8,9},{9,8},{10,11... | collective-permute-start | bytes 1572872 | tf_op jit(solution)/shard_map/ppermute | solution.py:24
  (8 other events, 10.2 us)

commit v5 on v4

--- a/solution.py
+++ b/solution.py
@@ -393,8 +393,8 @@
     two(2)
     one([4])
     split(1)
+    two(3)
     three(0)
-    two(3)
     apart(4)
     split(2)
     three(1)

time: 184 us -> 184 us (level)
    unnamed x28 -> x26, local copies, waits for them, and re-layouts: 7.17 us -> 6.54 us
where the time goes in v5:
time: 184 us; the launch traced here: 183 us
  waiting for transfers between devices  66.3 us (36%)
  starting transfers between devices  60.4 us (33%)
  Pallas kernels  49.1 us (27%)
  local copies, waits for them, and re-layouts  6.54 us (4%)
    all_to_all x5, waiting for transfers between devices, spread(): lax.all_to_all(array, 'tr', split_axis=0, concat_axis=0, tiled=True, axis...  58.8 us
    pallas_call x20, Pallas kernels, ordered_call(): pl.pallas_call(body, in_specs=specs, input_output_aliases=aliases or {},...  49.1 us
    ppermute x21, starting transfers between devices, exchanged(): return lax.ppermute(array, AXES, pairs)  31.2 us
    all_to_all x5, starting transfers between devices, spread(): lax.all_to_all(array, 'tr', split_axis=0, concat_axis=0, tiled=True, axis...  29.2 us
    ppermute x21, waiting for transfers between devices, exchanged(): return lax.ppermute(array, AXES, pairs)  7.54 us
    unnamed x26, local copies, waits for them, and re-layouts  6.54 us
  transfers between devices with their start and end apart: 26, of which 9 were waited for; matrix products, arithmetic and copies ran while one was open for 0% of the time, Pallas kernels for 24%

profile of v5, /device:TPU:1, one launch (start us, length us, event | category | flops | bytes accessed | tf_op | source)
XLA Modules:
  0.0 182.6 jit_solution(13402479835460731956)
XLA Ops:
  0.0 2.7 %one.3.refs_2_ = bf16[32,64,128]{2,1,0:T(8,128)(2,1)} custom-call(bf16[8,256,256]{2,1,0:T(8,128)(2,1)} %refs_0_.5, bf16[32,64,1024]{2,1,0:T(8,128)(2,1)} %refs_1_.9), custom_call_target="tpu_custom_call" | custom-call | flops 99999997952 | bytes 370000000 | tf_op jit(solution)/shard_map/one/pallas_call | solution.py:51
  2.7 3.7 %collective-permute-start.1 = (bf16[32,64,128]{2,1,0:T(8,128)(2,1)}, bf16[32,64,128]{2,1,0:T(8,128)(2,1)}, u32[]{:S(2)}, u32[]{:S(2)}) collective-permute-start(bf16[32,64,128]{2,1,0:T(8,128)(2,1)} %one.3.refs_2_), channel_id=1, source_target_pairs={{0,4},{1,5},{2,6},{3,7},{4,0},{5,1},{6,2},{7,3},{8,12},{9,13},{10,... | collective-permute-start | bytes 1572872 | tf_op jit(solution)/shard_map/ppermute | solution.py:24
  7.7 4.4 %one.4 = (bf16[32,64,256]{2,1,0:T(8,128)(2,1)}, bf16[32,64,256]{2,1,0:T(8,128)(2,1)}, bf16[32,64,256]{2,1,0:T(8,128)(2,1)}) custom-call(bf16[8,256,256]{2,1,0:T(8,128)(2,1)} %refs_0_.5, bf16[32,64,1024]{2,1,0:T(8,128)(2,1)} %refs_1_.9, bf16[32,64,128]{2,1,0:T(8,128)(2,1)} %one.3.refs_2_), custom_call_target="tpu_custom_call" | custom-call | flops 99999997952 | bytes 370000000 | tf_op jit(solution)/shard_map/one/pallas_call | solution.py:51
  12.4 2.7 %collective-permute-start.4 = (bf16[32,64,256]{2,1,0:T(8,128)(2,1)}, bf16[32,64,256]{2,1,0:T(8,128)(2,1)}, u32[]{:S(2)}, u32[]{:S(2)}) collective-permute-start(bf16[32,64,256]{2,1,0:T(8,128)(2,1)} %get-tuple-element.29), channel_id=1, source_target_pairs={{0,4},{1,5},{2,6},{3,7},{4,0},{5,1},{6,2},{7,3},{8,12},{9,13},{10,... | collective-permute-start | bytes 3145736 | tf_op jit(solution)/shard_map/ppermute | solution.py:24
  18.3 2.6 %two.4.refs_4_ = bf16[16,2,64,128]{3,2,1,0:T(8,128)(2,1)} custom-call(bf16[16,128,256]{2,1,0:T(8,128)(2,1)} %copy-done.11, bf16[2,16,64,128]{3,2,1,0:T(8,128)(2,1)} %bitcast.18, bf16[2,16,64,128]{3,2,1,0:T(8,128)(2,1)} %bitcast.4.refs_2_), custom_call_target="tpu_custom_call" | custom-call | flops 99999997952 | bytes 370000000 | tf_op jit(solution)/shard_map/two/pallas_call | solution.py:51
  20.9 11.1 %all-to-all-start.1 = ((bf16[16,2,64,128]{3,2,1,0:T(8,128)(2,1)}), bf16[16,2,64,128]{3,2,1,0:T(8,128)(2,1)}, u32[]{:S(2)}, u32[]{:S(2)}) async-start(bf16[16,2,64,128]{3,2,1,0:T(8,128)(2,1)} %two.4.refs_4_), calls=%async_computation.1 | async-start | bytes 1048576 | tf_op jit(solution)/shard_map/all_to_all | solution.py:30
  33.1 2.2 %compose.1.refs_3_.refs_0_ = bf16[16,128,256]{2,1,0:T(8,128)(2,1)S(1)} custom-call(s32[3]{0:T(128)S(1)} %pad_add_fusion.refs_0_, bf16[32,64,256]{2,1,0:T(8,128)(2,1)S(1)} %copy-done.3, bf16[32,64,64]{2,1,0:T(8,128)(2,1)} %refs_2_.1, bf16[32,64,64]{2,1,0:T(8,128)(2,1)} %collective-permute-done.refs_3_, bf16[16,2,64,128]{3,2,1,0:T(8,128)(2,1)S(1)} %copy-done.1), custom_call_target="tpu_custom_call" | custom-call | flops 99999997952 | bytes 370000000 | tf_op jit(solution)/shard_map/compose/pallas_call | solution.py:51
  36.4 3.4 %collective-permute-done.3 = bf16[32,64,256]{2,1,0:T(8,128)(2,1)} collective-permute-done((bf16[32,64,256]{2,1,0:T(8,128)(2,1)}, bf16[32,64,256]{2,1,0:T(8,128)(2,1)}, u32[]{:S(2)}, u32[]{:S(2)}) %collective-permute-start.3) | collective-permute-done | bytes 1048608 | tf_op jit(solution)/shard_map/ppermute | solution.py:24
  39.8 3.0 %two.5.refs_1_ = bf16[16,2,64,256]{3,2,1,0:T(8,128)(2,1)} custom-call(bf16[16,128,256]{2,1,0:T(8,128)(2,1)} %copy-done.11, bf16[2,16,64,256]{3,2,1,0:T(8,128)(2,1)} %bitcast.14, bf16[2,16,64,256]{3,2,1,0:T(8,128)(2,1)} %bitcast.8.refs_2_, bf16[16,128,256]{2,1,0:T(8,128)(2,1)} %copy-done.7), custom_call_target="tpu_custom_call" | custom-call | flops 99999997952 | bytes 370000000 | tf_op jit(solution)/shard_map/two/pallas_call | solution.py:51
  42.7 6.7 %all-to-all-done.1.refs_0_ = bf16[16,2,64,128]{3,2,1,0:T(8,128)(2,1)} async-done(((bf16[16,2,64,128]{3,2,1,0:T(8,128)(2,1)}), bf16[16,2,64,128]{3,2,1,0:T(8,128)(2,1)}, u32[]{:S(2)}, u32[]{:S(2)}) %all-to-all-start.1) | async-done | bytes 524320 | tf_op jit(solution)/shard_map/all_to_all | solution.py:30
  49.5 5.4 %all-to-all-start = ((bf16[16,2,64,256]{3,2,1,0:T(8,128)(2,1)}), bf16[16,2,64,256]{3,2,1,0:T(8,128)(2,1)}, u32[]{:S(2)}, u32[]{:S(2)}) async-start(bf16[16,2,64,256]{3,2,1,0:T(8,128)(2,1)} %two.5.refs_1_), calls=%async_computation | async-start | bytes 2097152 | tf_op jit(solution)/shard_map/all_to_all | solution.py:30
  57.9 2.9 %collective-permute-start.7 = (bf16[16,64,128]{2,1,0:T(8,128)(2,1)}, bf16[16,64,128]{2,1,0:T(8,128)(2,1)}, u32[]{:S(2)}, u32[]{:S(2)}) collective-permute-start(bf16[16,64,128]{2,1,0:T(8,128)(2,1)} %get-tuple-element.30.refs_3_), channel_id=1, source_target_pairs={{0,128},{1,129},{2,130},{3,131},{4,132},{5,133},{6,134},{7,135},{8... | collective-permute-start | bytes 786440 | tf_op jit(solution)/shard_map/ppermute | solution.py:24
  62.3 2.9 %two.6.refs_2_ = bf16[16,2,64,256]{3,2,1,0:T(8,128)(2,1)} custom-call(bf16[16,128,256]{2,1,0:T(8,128)(2,1)} %copy-done.11, bf16[2,16,64,256]{3,2,1,0:T(8,128)(2,1)} %bitcast.17, bf16[2,16,64,256]{3,2,1,0:T(8,128)(2,1)} %bitcast.10.refs_2_, bf16[16,64,128]{2,1,0:T(8,128)(2,1)} %get-tuple-element.30.refs_3_), custom_call_target="tpu_custom_call" | custom-call | flops 99999997952 | bytes 370000000 | tf_op jit(solution)/shard_map/two/pallas_call | solution.py:51
  65.2 2.7 %one.5.refs_1_ = bf16[32,64,128]{2,1,0:T(8,128)(2,1)} custom-call(bf16[8,256,256]{2,1,0:T(8,128)(2,1)} %refs_0_.5, bf16[32,64,1024]{2,1,0:T(8,128)(2,1)} %refs_1_.9, bf16[16,2,64,256]{3,2,1,0:T(8,128)(2,1)} %two.6.refs_2_), custom_call_target="tpu_custom_call" | custom-call | flops 99999997952 | bytes 370000000 | tf_op jit(solution)/shard_map/one/pallas_call | solution.py:51
  67.9 2.5 %collective-permute-start.6 = (bf16[16,64,128]{2,1,0:T(8,128)(2,1)}, bf16[16,64,128]{2,1,0:T(8,128)(2,1)}, u32[]{:S(2)}, u32[]{:S(2)}) collective-permute-start(bf16[16,64,128]{2,1,0:T(8,128)(2,1)} %get-tuple-element.32.refs_1_), channel_id=1, source_target_pairs={{0,1},{1,0},{2,3},{3,2},{4,5},{5,4},{6,7},{7,6},{8,9},{9,8},{10,11... | collective-permute-start | bytes 786440 | tf_op jit(solution)/shard_map/ppermute | solution.py:24
  70.4 2.8 %collective-permute-start.5 = (bf16[32,64,128]{2,1,0:T(8,128)(2,1)}, bf16[32,64,128]{2,1,0:T(8,128)(2,1)}, u32[]{:S(2)}, u32[]{:S(2)}) collective-permute-start(bf16[32,64,128]{2,1,0:T(8,128)(2,1)} %one.5.refs_1_), channel_id=1, source_target_pairs={{0,4},{1,5},{2,6},{3,7},{4,0},{5,1},{6,2},{7,3},{8,12},{9,13},{10,... | collective-permute-start | bytes 1572872 | tf_op jit(solution)/shard_map/ppermute | solution.py:24
  73.2 9.7 %all-to-all-done.refs_0_ = bf16[16,2,64,256]{3,2,1,0:T(8,128)(2,1)} async-done(((bf16[16,2,64,256]{3,2,1,0:T(8,128)(2,1)}), bf16[16,2,64,256]{3,2,1,0:T(8,128)(2,1)}, u32[]{:S(2)}, u32[]{:S(2)}) %all-to-all-start) | async-done | bytes 1048608 | tf_op jit(solution)/shard_map/all_to_all | solution.py:30
  82.9 4.3 %all-to-all-start.3 = ((bf16[16,2,64,256]{3,2,1,0:T(8,128)(2,1)}), bf16[16,2,64,256]{3,2,1,0:T(8,128)(2,1)}, u32[]{:S(2)}, u32[]{:S(2)}) async-start(bf16[16,2,64,256]{3,2,1,0:T(8,128)(2,1)} %two.6.refs_2_), calls=%async_computation.3 | async-start | bytes 2097152 | tf_op jit(solution)/shard_map/all_to_all | solution.py:30
  90.1 2.9 %collective-permute-start.13 = (bf16[16,64,256]{2,1,0:T(8,128)(2,1)}, bf16[16,64,256]{2,1,0:T(8,128)(2,1)}, u32[]{:S(2)}, u32[]{:S(2)}) collective-permute-start(bf16[16,64,256]{2,1,0:T(8,128)(2,1)} %get-tuple-element.31.refs_3_), channel_id=1, source_target_pairs={{0,128},{1,129},{2,130},{3,131},{4,132},{5,133},{6,134},{7,135},{8... | collective-permute-start | bytes 1572872 | tf_op jit(solution)/shard_map/ppermute | solution.py:24
  93.1 3.0 %two.7.refs_5_ = bf16[16,2,64,256]{3,2,1,0:T(8,128)(2,1)} custom-call(bf16[16,128,256]{2,1,0:T(8,128)(2,1)} %copy-done.11, bf16[2,16,64,256]{3,2,1,0:T(8,128)(2,1)} %bitcast.16, bf16[2,16,64,256]{3,2,1,0:T(8,128)(2,1)} %bitcast.6.refs_2_, bf16[16,64,256]{2,1,0:T(8,128)(2,1)} %get-tuple-element.31.refs_3_), custom_call_target="tpu_custom_call" | custom-call | flops 99999997952 | bytes 370000000 | tf_op jit(solution)/shard_map/two/pallas_call | solution.py:51
  97.0 2.4 %three.5 = (bf16[2,16,64,1024]{3,2,1,0:T(8,128)(2,1)}, f32[8,128]{1,0:T(8,128)S(1)}) custom-call(bf16[16,128,256]{2,1,0:T(8,128)(2,1)S(1)} %copy-done.8, bf16[16,64,128]{2,1,0:T(8,128)(2,1)} %get-tuple-element.32.refs_1_, bf16[16,64,128]{2,1,0:T(8,128)(2,1)} %collective-permute-done.6.refs_2_, bf16[16,64,128]{2,1,0:T(8,128)(2,1)} %collective-permute-done.7.refs_3_, ...), custom_call_target="tpu_custom_call" | custom-call | flops 99999997952 | bytes 370000000 | tf_op jit(solution)/shard_map/three/pallas_call | solution.py:51
  99.4 2.2 %apart.1 = (bf16[16,64,128]{2,1,0:T(8,128)(2,1)S(1)}, bf16[16,64,128]{2,1,0:T(8,128)(2,1)}) custom-call(bf16[16,128,256]{2,1,0:T(8,128)(2,1)S(1)} %copy-done.12, bf16[2,16,64,128]{3,2,1,0:T(8,128)(2,1)S(1)} %bitcast.15, bf16[2,16,64,128]{3,2,1,0:T(8,128)(2,1)} %bitcast.12.refs_2_, f32[8,128]{1,0:T(8,128)S(1)} %get-tuple-element.33.refs_3_), custom_call_target="tpu_custom_call" | custom-call | flops 99999997952 | bytes 370000000 | tf_op jit(solution)/shard_map/apart/pallas_call | solution.py:51
  104.3 10.2 %all-to-all-done.3.refs_0_ = bf16[16,2,64,256]{3,2,1,0:T(8,128)(2,1)} async-done(((bf16[16,2,64,256]{3,2,1,0:T(8,128)(2,1)}), bf16[16,2,64,256]{3,2,1,0:T(8,128)(2,1)}, u32[]{:S(2)}, u32[]{:S(2)}) %all-to-all-start.3) | async-done | bytes 1048608 | tf_op jit(solution)/shard_map/all_to_all | solution.py:30
  114.5 4.2 %all-to-all-start.2 = ((bf16[16,2,64,256]{3,2,1,0:T(8,128)(2,1)}), bf16[16,2,64,256]{3,2,1,0:T(8,128)(2,1)}, u32[]{:S(2)}, u32[]{:S(2)}) async-start(bf16[16,2,64,256]{3,2,1,0:T(8,128)(2,1)} %two.7.refs_5_), calls=%async_computation.2 | async-start | bytes 2097152 | tf_op jit(solution)/shard_map/all_to_all | solution.py:30
  126.9 2.5 %three.6 = (bf16[2,16,64,1024]{3,2,1,0:T(8,128)(2,1)}, f32[8,128]{1,0:T(8,128)S(1)}) custom-call(bf16[16,128,256]{2,1,0:T(8,128)(2,1)S(1)} %copy-done.9, bf16[16,64,256]{2,1,0:T(8,128)(2,1)S(1)} %get-tuple-element.36.refs_1_, bf16[16,64,256]{2,1,0:T(8,128)(2,1)S(1)} %collective-permute-done.12.refs_2_, ...), custom_call_target="tpu_custom_call", output_to_operand_aliasing={{0}: (5, {})} | custom-call | flops 99999997952 | bytes 370000000 | tf_op jit(solution)/shard_map/three/pallas_call | solution.py:51
  132.6 13.4 %all-to-all-done.2.refs_0_ = bf16[16,2,64,256]{3,2,1,0:T(8,128)(2,1)} async-done(((bf16[16,2,64,256]{3,2,1,0:T(8,128)(2,1)}), bf16[16,2,64,256]{3,2,1,0:T(8,128)(2,1)}, u32[]{:S(2)}, u32[]{:S(2)}) %all-to-all-start.2) | async-done | bytes 1048608 | tf_op jit(solution)/shard_map/all_to_all | solution.py:30
  146.0 4.2 %all-to-all-start.4 = ((bf16[16,4,64,128]{3,2,1,0:T(8,128)(2,1)}), bf16[16,4,64,128]{3,2,1,0:T(8,128)(2,1)}, u32[]{:S(2)}, u32[]{:S(2)}) async-start(bf16[16,4,64,128]{3,2,1,0:T(8,128)(2,1)} %pack.1.refs_1_), calls=%async_computation.4 | async-start | bytes 2097152 | tf_op jit(solution)/shard_map/all_to_all | solution.py:30
  152.5 2.9 %collective-permute-start.16 = (bf16[16,64,256]{2,1,0:T(8,128)(2,1)}, bf16[16,64,256]{2,1,0:T(8,128)(2,1)}, u32[]{:S(2)}, u32[]{:S(2)}) collective-permute-start(bf16[16,64,256]{2,1,0:T(8,128)(2,1)} %get-tuple-element.41.refs_6_), channel_id=1, source_target_pairs={{0,128},{1,129},{2,130},{3,131},{4,132},{5,133},{6,134},{7,135},{8... | collective-permute-start | bytes 1572872 | tf_op jit(solution)/shard_map/ppermute | solution.py:24
  156.2 2.7 %three.7 = (bf16[2,16,64,1024]{3,2,1,0:T(8,128)(2,1)}, f32[8,128]{1,0:T(8,128)S(1)}) custom-call(bf16[16,128,256]{2,1,0:T(8,128)(2,1)S(1)} %copy-done.10, bf16[16,64,256]{2,1,0:T(8,128)(2,1)} %get-tuple-element.42.refs_1_, bf16[16,64,256]{2,1,0:T(8,128)(2,1)} %collective-permute-done.18.refs_2_, ...), custom_call_target="tpu_custom_call", output_to_operand_aliasing={{0}: (5, {})} | custom-call | flops 99999997952 | bytes 370000000 | tf_op jit(solution)/shard_map/three/pallas_call | solution.py:51
  158.9 18.7 %all-to-all-done.4.refs_1_ = bf16[16,4,64,128]{3,2,1,0:T(8,128)(2,1)} async-done(((bf16[16,4,64,128]{3,2,1,0:T(8,128)(2,1)}), bf16[16,4,64,128]{3,2,1,0:T(8,128)(2,1)}, u32[]{:S(2)}, u32[]{:S(2)}) %all-to-all-start.4) | async-done | bytes 1048608 | tf_op jit(solution)/shard_map/all_to_all | solution.py:30
  177.6 2.3 %three.8 = (bf16[2,16,64,1024]{3,2,1,0:T(8,128)(2,1)}, f32[8,128]{1,0:T(8,128)S(1)}) custom-call(bf16[16,128,256]{2,1,0:T(8,128)(2,1)S(1)} %copy-done.10, bf16[16,4,64,128]{3,2,1,0:T(8,128)(2,1)} %all-to-all-done.4.refs_1_, bf16[2,16,64,1024]{3,2,1,0:T(8,128)(2,1)} %get-tuple-element.44.refs_2_, ...), custom_call_target="tpu_custom_call", output_to_operand_aliasing={{0}: (2, {})} | custom-call | flops 99999997952 | bytes 370000000 | tf_op jit(solution)/shard_map/three/pallas_call | solution.py:51
  179.9 2.7 %three.9 = (bf16[2,16,64,1024]{3,2,1,0:T(8,128)(2,1)}, f32[8,128]{1,0:T(8,128)}) custom-call(bf16[16,128,256]{2,1,0:T(8,128)(2,1)S(1)} %copy-done.10, bf16[16,64,256]{2,1,0:T(8,128)(2,1)} %get-tuple-element.40.refs_1_, bf16[16,64,256]{2,1,0:T(8,128)(2,1)} %collective-permute-done.15.refs_2_, ...), custom_call_target="tpu_custom_call", output_to_operand_aliasing={{0}: (5, {})} | custom-call | flops 99999997952 | bytes 370000000 | tf_op jit(solution)/shard_map/three/pallas_call | solution.py:51
  (67 shorter events, 32.2 us)
Async XLA Ops:
  2.7 12.7 %copy-start.2 = (bf16[32,64,256]{2,1,0:T(8,128)(2,1)S(1)}, bf16[32,64,256]{2,1,0:T(8,128)(2,1)}, u32[]{:S(2)}) copy-start(bf16[32,64,256]{2,1,0:T(8,128)(2,1)} %refs_1_.7) | copy-start | bytes 3145732
  2.7 15.6 %collective-permute-start.1 = (bf16[32,64,128]{2,1,0:T(8,128)(2,1)}, bf16[32,64,128]{2,1,0:T(8,128)(2,1)}, u32[]{:S(2)}, u32[]{:S(2)}) collective-permute-start(bf16[32,64,128]{2,1,0:T(8,128)(2,1)} %one.3.refs_2_), channel_id=1, source_target_pairs={{0,4},{1,5},{2,6},{3,7},{4,0},{5,1},{6,2},{7,3},{8,12},{9,13},{10,... | collective-permute-start | bytes 1572872 | tf_op jit(solution)/shard_map/ppermute | solution.py:24
  6.4 25.7 %collective-permute-start = (bf16[32,64,64]{2,1,0:T(8,128)(2,1)}, bf16[32,64,64]{2,1,0:T(8,128)(2,1)}, u32[]{:S(2)}, u32[]{:S(2)}) collective-permute-start(bf16[32,64,64]{2,1,0:T(8,128)(2,1)} %refs_2_.1), channel_id=1, source_target_pairs={{0,1},{1,0},{2,3},{3,2},{4,5},{5,4},{6,7},{7,6},{8,9},{9,8},{10,11... | collective-permute-start | bytes 786440 | tf_op jit(solution)/shard_map/ppermute | solution.py:24
  12.1 27.7 %collective-permute-start.3 = (bf16[32,64,256]{2,1,0:T(8,128)(2,1)}, bf16[32,64,256]{2,1,0:T(8,128)(2,1)}, u32[]{:S(2)}, u32[]{:S(2)}) collective-permute-start(bf16[32,64,256]{2,1,0:T(8,128)(2,1)} %get-tuple-element.27.refs_2_), channel_id=1, source_target_pairs={{0,4},{1,5},{2,6},{3,7},{4,0},{5,1},{6,2},{7,3},{8,12},{9,13},{10,... | collective-permute-start | bytes 3145736 | tf_op jit(solution)/shard_map/ppermute | solution.py:24
  12.4 49.9 %collective-permute-start.4 = (bf16[32,64,256]{2,1,0:T(8,128)(2,1)}, bf16[32,64,256]{2,1,0:T(8,128)(2,1)}, u32[]{:S(2)}, u32[]{:S(2)}) collective-permute-start(bf16[32,64,256]{2,1,0:T(8,128)(2,1)} %get-tuple-element.29), channel_id=1, source_target_pairs={{0,4},{1,5},{2,6},{3,7},{4,0},{5,1},{6,2},{7,3},{8,12},{9,13},{10,... | collective-permute-start | bytes 3145736 | tf_op jit(solution)/shard_map/ppermute | solution.py:24
  15.1 75.0 %collective-permute-start.2 = (bf16[32,64,256]{2,1,0:T(8,128)(2,1)}, bf16[32,64,256]{2,1,0:T(8,128)(2,1)}, u32[]{:S(2)}, u32[]{:S(2)}) collective-permute-start(bf16[32,64,256]{2,1,0:T(8,128)(2,1)} %get-tuple-element.28), channel_id=1, source_target_pairs={{0,4},{1,5},{2,6},{3,7},{4,0},{5,1},{6,2},{7,3},{8,12},{9,13},{10,... | collective-permute-start | bytes 3145736 | tf_op jit(solution)/shard_map/ppermute | solution.py:24
  18.3 13.7 %copy-start.3 = (bf16[32,64,256]{2,1,0:T(8,128)(2,1)S(1)}, bf16[32,64,256]{2,1,0:T(8,128)(2,1)}, u32[]{:S(2)}) copy-start(bf16[32,64,256]{2,1,0:T(8,128)(2,1)} %refs_1_.8) | copy-start | bytes 3145732
  20.9 28.5 %all-to-all-start.1 = ((bf16[16,2,64,128]{3,2,1,0:T(8,128)(2,1)}), bf16[16,2,64,128]{3,2,1,0:T(8,128)(2,1)}, u32[]{:S(2)}, u32[]{:S(2)}) async-start(bf16[16,2,64,128]{3,2,1,0:T(8,128)(2,1)} %two.4.refs_4_), calls=%async_computation.1 | async-start | bytes 1048576 | tf_op jit(solution)/shard_map/all_to_all | solution.py:30
  49.5 33.4 %all-to-all-start = ((bf16[16,2,64,256]{3,2,1,0:T(8,128)(2,1)}), bf16[16,2,64,256]{3,2,1,0:T(8,128)(2,1)}, u32[]{:S(2)}, u32[]{:S(2)}) async-start(bf16[16,2,64,256]{3,2,1,0:T(8,128)(2,1)} %two.5.refs_1_), calls=%async_computation | async-start | bytes 2097152 | tf_op jit(solution)/shard_map/all_to_all | solution.py:30
  57.9 38.2 %collective-permute-start.7 = (bf16[16,64,128]{2,1,0:T(8,128)(2,1)}, bf16[16,64,128]{2,1,0:T(8,128)(2,1)}, u32[]{:S(2)}, u32[]{:S(2)}) collective-permute-start(bf16[16,64,128]{2,1,0:T(8,128)(2,1)} %get-tuple-element.30.refs_3_), channel_id=1, source_target_pairs={{0,128},{1,129},{2,130},{3,131},{4,132},{5,133},{6,134},{7,135},{8... | collective-permute-start | bytes 786440 | tf_op jit(solution)/shard_map/ppermute | solution.py:24
  60.8 36.2 %collective-permute-start.8 = (bf16[16,64,128]{2,1,0:T(8,128)(2,1)}, bf16[16,64,128]{2,1,0:T(8,128)(2,1)}, u32[]{:S(2)}, u32[]{:S(2)}) collective-permute-start(bf16[16,64,128]{2,1,0:T(8,128)(2,1)} %get-tuple-element.30.refs_3_), channel_id=1, source_target_pairs={{0,129},{1,128},{2,131},{3,130},{4,133},{5,132},{6,135},{7,134},{8... | collective-permute-start | bytes 786440 | tf_op jit(solution)/shard_map/ppermute | solution.py:24
  67.9 29.0 %collective-permute-start.6 = (bf16[16,64,128]{2,1,0:T(8,128)(2,1)}, bf16[16,64,128]{2,1,0:T(8,128)(2,1)}, u32[]{:S(2)}, u32[]{:S(2)}) collective-permute-start(bf16[16,64,128]{2,1,0:T(8,128)(2,1)} %get-tuple-element.32.refs_1_), channel_id=1, source_target_pairs={{0,1},{1,0},{2,3},{3,2},{4,5},{5,4},{6,7},{7,6},{8,9},{9,8},{10,11... | collective-permute-start | bytes 786440 | tf_op jit(solution)/shard_map/ppermute | solution.py:24
  70.4 29.0 %collective-permute-start.5 = (bf16[32,64,128]{2,1,0:T(8,128)(2,1)}, bf16[32,64,128]{2,1,0:T(8,128)(2,1)}, u32[]{:S(2)}, u32[]{:S(2)}) collective-permute-start(bf16[32,64,128]{2,1,0:T(8,128)(2,1)} %one.5.refs_1_), channel_id=1, source_target_pairs={{0,4},{1,5},{2,6},{3,7},{4,0},{5,1},{6,2},{7,3},{8,12},{9,13},{10,... | collective-permute-start | bytes 1572872 | tf_op jit(solution)/shard_map/ppermute | solution.py:24
  82.9 31.6 %all-to-all-start.3 = ((bf16[16,2,64,256]{3,2,1,0:T(8,128)(2,1)}), bf16[16,2,64,256]{3,2,1,0:T(8,128)(2,1)}, u32[]{:S(2)}, u32[]{:S(2)}) async-start(bf16[16,2,64,256]{3,2,1,0:T(8,128)(2,1)} %two.6.refs_2_), calls=%async_computation.3 | async-start | bytes 2097152 | tf_op jit(solution)/shard_map/all_to_all | solution.py:30
  90.1 34.0 %collective-permute-start.13 = (bf16[16,64,256]{2,1,0:T(8,128)(2,1)}, bf16[16,64,256]{2,1,0:T(8,128)(2,1)}, u32[]{:S(2)}, u32[]{:S(2)}) collective-permute-start(bf16[16,64,256]{2,1,0:T(8,128)(2,1)} %get-tuple-element.31.refs_3_), channel_id=1, source_target_pairs={{0,128},{1,129},{2,130},{3,131},{4,132},{5,133},{6,134},{7,135},{8... | collective-permute-start | bytes 1572872 | tf_op jit(solution)/shard_map/ppermute | solution.py:24
  93.1 3.9 %copy-start.8 = (bf16[16,128,256]{2,1,0:T(8,128)(2,1)S(1)}, bf16[16,128,256]{2,1,0:T(8,128)(2,1)}, u32[]{:S(2)}) copy-start(bf16[16,128,256]{2,1,0:T(8,128)(2,1)} %copy-done.7) | copy-start | bytes 3145732
  96.1 3.3 %copy-start.12 = (bf16[16,128,256]{2,1,0:T(8,128)(2,1)S(1)}, bf16[16,128,256]{2,1,0:T(8,128)(2,1)}, u32[]{:S(2)}) copy-start(bf16[16,128,256]{2,1,0:T(8,128)(2,1)} %copy-done.11) | copy-start | bytes 3145732
  96.1 28.8 %collective-permute-start.14 = (bf16[16,64,256]{2,1,0:T(8,128)(2,1)}, bf16[16,64,256]{2,1,0:T(8,128)(2,1)}, u32[]{:S(2)}, u32[]{:S(2)}) collective-permute-start(bf16[16,64,256]{2,1,0:T(8,128)(2,1)} %get-tuple-element.31.refs_3_), channel_id=1, source_target_pairs={{0,129},{1,128},{2,131},{3,130},{4,133},{5,132},{6,135},{7,134},{8... | collective-permute-start | bytes 1572872 | tf_op jit(solution)/shard_map/ppermute | solution.py:24
  101.6 27.7 %collective-permute-start.10 = (bf16[16,64,128]{2,1,0:T(8,128)(2,1)}, bf16[16,64,128]{2,1,0:T(8,128)(2,1)}, u32[]{:S(2)}, u32[]{:S(2)}) collective-permute-start(bf16[16,64,128]{2,1,0:T(8,128)(2,1)} %get-tuple-element.35.refs_1_), channel_id=1, source_target_pairs={{0,128},{1,129},{2,130},{3,131},{4,132},{5,133},{6,134},{7,135},{8... | collective-permute-start | bytes 786440 | tf_op jit(solution)/shard_map/ppermute | solution.py:24
  103.1 26.3 %collective-permute-start.11 = (bf16[16,64,128]{2,1,0:T(8,128)(2,1)}, bf16[16,64,128]{2,1,0:T(8,128)(2,1)}, u32[]{:S(2)}, u32[]{:S(2)}) collective-permute-start(bf16[16,64,128]{2,1,0:T(8,128)(2,1)} %get-tuple-element.35.refs_1_), channel_id=1, source_target_pairs={{0,129},{1,128},{2,131},{3,130},{4,133},{5,132},{6,135},{7,134},{8... | collective-permute-start | bytes 786440 | tf_op jit(solution)/shard_map/ppermute | solution.py:24
  103.8 19.2 %collective-permute-start.12 = (bf16[16,64,256]{2,1,0:T(8,128)(2,1)S(1)}, bf16[16,64,256]{2,1,0:T(8,128)(2,1)S(1)}, u32[]{:S(2)}, u32[]{:S(2)}) collective-permute-start(bf16[16,64,256]{2,1,0:T(8,128)(2,1)S(1)} %get-tuple-element.36.refs_1_), channel_id=1, source_target_pairs={{0,1},{1,0},{2,3},{3,2},{4,5},{5,4},{6,7},{7,6},{8,9},{9,8},{10,11... | collective-permute-start | bytes 1572872 | tf_op jit(solution)/shard_map/ppermute | solution.py:24
  114.5 31.6 %all-to-all-start.2 = ((bf16[16,2,64,256]{3,2,1,0:T(8,128)(2,1)}), bf16[16,2,64,256]{3,2,1,0:T(8,128)(2,1)}, u32[]{:S(2)}, u32[]{:S(2)}) async-start(bf16[16,2,64,256]{3,2,1,0:T(8,128)(2,1)} %two.7.refs_5_), calls=%async_computation.2 | async-start | bytes 2097152 | tf_op jit(solution)/shard_map/all_to_all | solution.py:30
  118.7 8.1 %copy-start.9 = (bf16[16,128,256]{2,1,0:T(8,128)(2,1)S(1)}, bf16[16,128,256]{2,1,0:T(8,128)(2,1)}, u32[]{:S(2)}) copy-start(bf16[16,128,256]{2,1,0:T(8,128)(2,1)} %copy-done.7) | copy-start | bytes 3145732
  123.0 7.7 %collective-permute-start.9 = (bf16[16,64,128]{2,1,0:T(8,128)(2,1)S(1)}, bf16[16,64,128]{2,1,0:T(8,128)(2,1)S(1)}, u32[]{:S(2)}, u32[]{:S(2)}) collective-permute-start(bf16[16,64,128]{2,1,0:T(8,128)(2,1)S(1)} %get-tuple-element.34.refs_0_), channel_id=1, source_target_pairs={{0,1},{1,0},{2,3},{3,2},{4,5},{5,4},{6,7},{7,6},{8,9},{9,8},{10,11... | collective-permute-start | bytes 786440 | tf_op jit(solution)/shard_map/ppermute | solution.py:24
  124.1 32.1 %collective-permute-start.19 = (bf16[16,64,256]{2,1,0:T(8,128)(2,1)}, bf16[16,64,256]{2,1,0:T(8,128)(2,1)}, u32[]{:S(2)}, u32[]{:S(2)}) collective-permute-start(bf16[16,64,256]{2,1,0:T(8,128)(2,1)} %get-tuple-element.38.refs_6_), channel_id=1, source_target_pairs={{0,128},{1,129},{2,130},{3,131},{4,132},{5,133},{6,134},{7,135},{8... | collective-permute-start | bytes 1572872 | tf_op jit(solution)/shard_map/ppermute | solution.py:24
  124.8 31.3 %collective-permute-start.20 = (bf16[16,64,256]{2,1,0:T(8,128)(2,1)}, bf16[16,64,256]{2,1,0:T(8,128)(2,1)}, u32[]{:S(2)}, u32[]{:S(2)}) collective-permute-start(bf16[16,64,256]{2,1,0:T(8,128)(2,1)} %get-tuple-element.38.refs_6_), channel_id=1, source_target_pairs={{0,129},{1,128},{2,131},{3,130},{4,133},{5,132},{6,135},{7,134},{8... | collective-permute-start | bytes 1572872 | tf_op jit(solution)/shard_map/ppermute | solution.py:24
  129.3 26.8 %collective-permute-start.18 = (bf16[16,64,256]{2,1,0:T(8,128)(2,1)}, bf16[16,64,256]{2,1,0:T(8,128)(2,1)}, u32[]{:S(2)}, u32[]{:S(2)}) collective-permute-start(bf16[16,64,256]{2,1,0:T(8,128)(2,1)} %get-tuple-element.42.refs_1_), channel_id=1, source_target_pairs={{0,1},{1,0},{2,3},{3,2},{4,5},{5,4},{6,7},{7,6},{8,9},{9,8},{10,11... | collective-permute-start | bytes 1572872 | tf_op jit(solution)/shard_map/ppermute | solution.py:24
  146.0 31.6 %all-to-all-start.4 = ((bf16[16,4,64,128]{3,2,1,0:T(8,128)(2,1)}), bf16[16,4,64,128]{3,2,1,0:T(8,128)(2,1)}, u32[]{:S(2)}, u32[]{:S(2)}) async-start(bf16[16,4,64,128]{3,2,1,0:T(8,128)(2,1)} %pack.1.refs_1_), calls=%async_computation.4 | async-start | bytes 2097152 | tf_op jit(solution)/shard_map/all_to_all | solution.py:30
  150.3 5.9 %copy-start.10 = (bf16[16,128,256]{2,1,0:T(8,128)(2,1)S(1)}, bf16[16,128,256]{2,1,0:T(8,128)(2,1)}, u32[]{:S(2)}) copy-start(bf16[16,128,256]{2,1,0:T(8,128)(2,1)} %copy-done.7) | copy-start | bytes 3145732
  152.5 27.5 %collective-permute-start.16 = (bf16[16,64,256]{2,1,0:T(8,128)(2,1)}, bf16[16,64,256]{2,1,0:T(8,128)(2,1)}, u32[]{:S(2)}, u32[]{:S(2)}) collective-permute-start(bf16[16,64,256]{2,1,0:T(8,128)(2,1)} %get-tuple-element.41.refs_6_), channel_id=1, source_target_pairs={{0,128},{1,129},{2,130},{3,131},{4,132},{5,133},{6,134},{7,135},{8... | collective-permute-start | bytes 1572872 | tf_op jit(solution)/shard_map/ppermute | solution.py:24
  155.4 24.6 %collective-permute-start.17 = (bf16[16,64,256]{2,1,0:T(8,128)(2,1)}, bf16[16,64,256]{2,1,0:T(8,128)(2,1)}, u32[]{:S(2)}, u32[]{:S(2)}) collective-permute-start(bf16[16,64,256]{2,1,0:T(8,128)(2,1)} %get-tuple-element.41.refs_6_), channel_id=1, source_target_pairs={{0,129},{1,128},{2,131},{3,130},{4,133},{5,132},{6,135},{7,134},{8... | collective-permute-start | bytes 1572872 | tf_op jit(solution)/shard_map/ppermute | solution.py:24
  156.2 23.8 %collective-permute-start.15 = (bf16[16,64,256]{2,1,0:T(8,128)(2,1)}, bf16[16,64,256]{2,1,0:T(8,128)(2,1)}, u32[]{:S(2)}, u32[]{:S(2)}) collective-permute-start(bf16[16,64,256]{2,1,0:T(8,128)(2,1)} %get-tuple-element.40.refs_1_), channel_id=1, source_target_pairs={{0,1},{1,0},{2,3},{3,2},{4,5},{5,4},{6,7},{7,6},{8,9},{9,8},{10,11... | collective-permute-start | bytes 1572872 | tf_op jit(solution)/shard_map/ppermute | solution.py:24
  (7 other events, 9.9 us)
